TPU v7x, 256 devices: a whole 4x4x8 slice. The times are simulated.
256 devices in a mesh: tile: 8 (over y, core), depth: 32 (over z, x).
Axes of the slice: x: 4, y: 4, z: 8, core: 2. Of those that a mesh axis runs over, the one named last changes fastest.
Arguments:
- volume: float32 [512, 1536, 512], P('depth', 'tile'), may hold values from 0.2 to 5
- flat_field: float32 [1536, 512], P('tile'), may hold values from 0.5 to 2
Outputs:
- corrected: float32 [512, 1536, 512], P('depth', 'tile')
All inputs are finite; a program needn't handle non-finite values.
Results may differ from a plain program's by a relative error of at most 0.0003.
Values sent between devices are 32-bit elements; how exact they have to be, the bound alone decides.
No kernel may reach another device: no remote copies, remote signals or barrier semaphores. Data moves between devices by JAX's collectives and lax.ppermute only.
A program may use at most 64 MiB of HBM per device.

v0:
```python
import jax
import jax.numpy as jnp
from jax import lax
from jax.sharding import PartitionSpec as P

RADIUS = 24


CLIP_LIMIT = 0.08


def padded(cells, sides, width):
    for axis, dim in sides:
        count = lax.axis_size(axis)
        ends = count - 1
        head = lax.slice_in_dim(cells, 0, width, axis=dim)
        tail = lax.slice_in_dim(cells, cells.shape[dim] - width, cells.shape[dim], axis=dim)
        cells = jnp.concatenate(
            [
                lax.ppermute(tail, axis, [(i, (i + 1) % count) for i in range(ends)]),
                cells,
                lax.ppermute(head, axis, [((i + 1) % count, i) for i in range(ends)]),
            ],
            axis=dim,
        )
    return cells


def from_behind(value, axis, steps):
    count = lax.axis_size(axis)
    first, last = (max(0, -steps), min(count, count - steps))
    return lax.ppermute(value, axis, [(source, source + steps) for source in range(first, last)])


def carried_in(value, axis, join, neutral):
    count, mine = (lax.axis_size(axis), lax.axis_index(axis))
    pieces = lax.all_gather(value, axis)
    subtotal = jnp.full_like(value, 0) + jnp.asarray(neutral, value.dtype)

    def turn(position, subtotal):
        longer = join(subtotal, pieces[position])
        return jnp.where(position < mine, longer, subtotal)

    return lax.fori_loop(0, count - 1, turn, subtotal)


def blur_weights(out_count, in_count, out_start, in_start, extent, radius):
    spread = radius / 3.0
    out_index = out_start + lax.iota(jnp.int32, out_count)[:, None]
    in_index = in_start + lax.iota(jnp.int32, in_count)[None, :]
    distance = (out_index - in_index).astype(jnp.float32)
    inside = (jnp.abs(out_index - in_index) <= radius) & (in_index >= 0) & (in_index < extent)
    kernel = jnp.where(inside, jnp.exp(-distance * distance / (2.0 * spread * spread)), 0.0)
    reach = lax.iota(jnp.int32, 2 * radius + 1)[None, :] - radius
    target = out_index + reach
    valid = (target >= 0) & (target < extent)
    reach_float = reach.astype(jnp.float32)
    weights = jnp.where(valid, jnp.exp(-reach_float * reach_float / (2.0 * spread * spread)), 0.0)
    normaliser = jnp.sum(weights, axis=1, keepdims=True)
    return kernel / normaliser


def clipped(values):
    return jnp.clip(values, -CLIP_LIMIT, CLIP_LIMIT)


def body(volume, flat_field):
    plane_count, row_count, col_count = volume.shape
    tile_index = lax.axis_index("tile")
    depth_index = lax.axis_index("depth")
    levelled = volume / flat_field[None]
    column_weights = blur_weights(col_count, col_count, 0, 0, col_count, RADIUS)
    across = jnp.einsum("prc,oc->pro", levelled, column_weights, precision=lax.Precision.HIGHEST)
    extended = padded(across, (("tile", 1),), RADIUS)
    row_start = tile_index * row_count
    row_weights = blur_weights(
        row_count,
        row_count + 2 * RADIUS,
        row_start,
        row_start - RADIUS,
        row_count * lax.axis_size("tile"),
        RADIUS,
    )
    blurred = jnp.einsum("ok,pkc->poc", row_weights, extended, precision=lax.Precision.HIGHEST)
    log_planes = jnp.log(blurred)
    inner_ratios = clipped(log_planes[:-1] - log_planes[1:])
    empty_plane = jnp.zeros((row_count, col_count), jnp.float32)
    prev_last = from_behind(log_planes[-1], "depth", 1)
    first_ratio = jnp.where(depth_index == 0, empty_plane, clipped(prev_last - log_planes[0]))
    local_sums = jnp.cumsum(jnp.concatenate([first_ratio[None], inner_ratios], axis=0), axis=0)

    def add_planes(earlier, later):
        return earlier + later

    offset = carried_in(local_sums[-1], "depth", add_planes, empty_plane)
    attenuation = local_sums + offset[None]
    return levelled * jnp.exp(attenuation)


def solution(mesh):
    return jax.shard_map(
        body,
        mesh=mesh,
        in_specs=(P("depth", "tile", None), P("tile", None)),
        out_specs=P("depth", "tile", None),
        check_vma=False,
    )
```

profile of v0, /device:TPU:8, one launch (start us, length us, event | category | flops | bytes accessed | tf_op | source)
XLA Modules:
  0.0 241.1 jit_solution(15827439268085056873)
XLA Ops:
  6.5 0.0 all-gather.2.cloned.1.call-start
  6.6 0.1 select_reduce_fusion
  6.7 13.3 %fusion.13 = f32[16,192,512]{2,1,0:T(8,128)S(1)} fusion(f32[16,192,512]{2,1,0:T(8,128)} %param.4, f32[192,512]{1,0:T(8,128)} %param.5, f32[512]{0:T(512)S(1)} %select_reduce_fusion, pred[512]{0:T(512)(128)(4,1)S(1)} %iota_compare_fusion), kind=kOutput, calls=%fused_computation.16 | convolution fusion | flops 9667870720 | bytes 12978688 | tf_op jit(solution)/shard_map/prc,oc->pro/dot_general | solution.py:73
  19.9 0.0 copy-start.1
  20.0 2.7 %copy-done.1 = f32[16,192,512]{2,1,0:T(8,128)} copy-done((f32[16,192,512]{2,1,0:T(8,128)}, f32[16,192,512]{2,1,0:T(8,128)S(1)}, u32[]{:S(2)}) %copy-start.1) | copy-done | bytes 6291480
  22.7 0.1 fusion.66
  22.8 1.9 collective-permute-start
  24.7 3.6 %collective-permute-start.1 = (f32[16,24,512]{2,1,0:T(8,128)S(1)}, f32[16,24,512]{2,1,0:T(8,128)S(1)}, u32[]{:S(2)}, u32[]{:S(2)}) collective-permute-start(f32[16,24,512]{2,1,0:T(8,128)S(1)} %get-tuple-element.109), channel_id=1, source_target_pairs={{32,0},{64,32},{96,64},{128,96},{160,128},{192,160},{224,192},{33,... | collective-permute-start | bytes 2359304 | tf_op jit(solution)/shard_map/ppermute | solution.py:22
  28.4 0.1 select_reduce_fusion.1
  28.5 7.6 %collective-permute-done = f32[16,24,512]{2,1,0:T(8,128)S(1)} collective-permute-done((f32[16,24,512]{2,1,0:T(8,128)S(1)}, f32[16,24,512]{2,1,0:T(8,128)S(1)}, u32[]{:S(2)}, u32[]{:S(2)}) %collective-permute-start) | collective-permute-done | bytes 786464 | tf_op jit(solution)/shard_map/ppermute | solution.py:20
  36.1 1.8 collective-permute-done.1
  37.8 9.7 %log_bitcast_fusion = f32[16,192,512]{2,1,0:T(8,128)S(1)} fusion(f32[16,24,512]{2,1,0:T(8,128)S(1)} %collective-permute-done.1, f32[16,192,512]{2,1,0:T(8,128)} %copy-done.1, f32[16,24,512]{2,1,0:T(8,128)S(1)} %collective-permute-done, f32[192]{0:T(256)S(1)} %select_reduce_fusion.1, s32[240]{0:T(256)S(1)} %iota_add_fusion.1, s32[192]{0:T(256)S(1)} %iota_add_fusion.2, ...), kind=kOutput, calls=%fused_computation.12 | convolution fusion | flops 4534287360 | bytes 14158752 | tf_op jit(solution)/shard_map/ok,pkc->poc/dot_general | solution.py:84
  47.5 3.6 %collective-permute-start.2 = (f32[192,512]{1,0:T(8,128)S(1)}, f32[192,512]{1,0:T(8,128)S(1)}, u32[]{:S(2)}, u32[]{:S(2)}) collective-permute-start(f32[192,512]{1,0:T(8,128)S(1)} %slice_bitcast_fusion.1), channel_id=1, source_target_pairs={{0,1},{1,2},{2,3},{3,4},{4,5},{5,6},{6,7},{7,8},{8,9},{9,10},{10,1... | collective-permute-start | bytes 1179656 | tf_op jit(solution)/shard_map/ppermute | solution.py:32
  51.1 0.8 fusion.10
  52.0 7.6 %collective-permute-done.2 = f32[192,512]{1,0:T(8,128)S(1)} collective-permute-done((f32[192,512]{1,0:T(8,128)S(1)}, f32[192,512]{1,0:T(8,128)S(1)}, u32[]{:S(2)}, u32[]{:S(2)}) %collective-permute-start.2) | collective-permute-done | bytes 393248 | tf_op jit(solution)/shard_map/ppermute | solution.py:32
  59.6 0.1 fusion.31
  59.7 1.1 fusion.6
  60.8 0.0 copy-start
  60.8 2.7 %copy-done = f32[16,192,512]{2,1,0:T(8,128)} copy-done((f32[16,192,512]{2,1,0:T(8,128)}, f32[16,192,512]{2,1,0:T(8,128)S(1)}, u32[]{:S(2)}) %copy-start) | copy-done | bytes 6291480
  63.5 0.0 copy-start.2
  63.5 0.8 slice.34
  64.3 0.0 all-gather.2.cloned.1.call-update
  64.3 124.9 %all-gather.2.cloned.1.call-done = f32[32,192,512]{2,1,0:T(8,128)} async-done(((f32[1,192,512]{2,1,0:T(8,128)}), f32[32,192,512]{2,1,0:T(8,128)}) %all-gather.2.cloned.1.call-update) | async-done | bytes 12582928 | tf_op jit(solution)/shard_map/all_gather | solution.py:37
  189.2 36.1 %while.14 = (s32[]{:T(128)}, f32[192,512]{1,0:T(8,128)S(1)}, s32[]{:T(128)}, f32[32,192,512]{2,1,0:T(8,128)}, s32[]{:T(128)}, /*index=5*/s32[]{:T(128)}) while((s32[]{:T(128)}, f32[192,512]{1,0:T(8,128)S(1)}, s32[]{:T(128)}, f32[32,192,512]{2,1,0:T(8,128)}, s32[]{:T(128)}, /*index=5*/s32[]{:T(128)}) %tuple.34), condition=%wide.region_4.5_spmd.clone, body=%wide.region_3.4_spmd.clone.sunk | while | flops 294916 | bytes 1179741 | solution.py:44
  189.2 1.1 add_select_fusion.2
  190.3 1.1 add_select_fusion.2
  191.5 1.1 add_select_fusion.2
  192.7 1.1 add_select_fusion.2
  193.8 1.1 add_select_fusion.2
  195.0 1.1 add_select_fusion.2
  196.2 1.1 add_select_fusion.2
  197.3 1.1 add_select_fusion.2
  198.5 1.1 add_select_fusion.2
  199.7 1.1 add_select_fusion.2
  200.8 1.1 add_select_fusion.2
  202.0 1.1 add_select_fusion.2
  203.1 1.1 add_select_fusion.2
  204.3 1.1 add_select_fusion.2
  205.5 1.1 add_select_fusion.2
  206.6 1.1 add_select_fusion.2
  207.8 1.1 add_select_fusion.2
  209.0 1.1 add_select_fusion.2
  210.1 1.1 add_select_fusion.2
  211.3 1.1 add_select_fusion.2
  212.5 1.1 add_select_fusion.2
  213.6 1.1 add_select_fusion.2
  214.8 1.1 add_select_fusion.2
  216.0 1.1 add_select_fusion.2
  217.1 1.1 add_select_fusion.2
  218.3 1.1 add_select_fusion.2
  219.5 1.1 add_select_fusion.2
  220.6 1.1 add_select_fusion.2
  221.8 1.1 add_select_fusion.2
  223.0 1.1 add_select_fusion.2
  224.1 1.1 add_select_fusion.2
  225.3 0.0 copy-done.2
  225.3 9.0 %exponential_multiply_fusion = f32[16,192,512]{2,1,0:T(8,128)} fusion(f32[16,192,512]{2,1,0:T(8,128)} %copy-done, f32[192,512]{1,0:T(8,128)S(1)} %get-tuple-element.84, f32[16,192,512]{2,1,0:T(8,128)} %param.4, f32[192,512]{1,0:T(8,128)S(1)} %copy-done.2), kind=kLoop, calls=%fused_computation.11 | loop fusion | flops 4718592 | bytes 19660800 | tf_op jit(solution)/shard_map/mul | solution.py:97
  (8 shorter events, 0.1 us)
Async XLA Ops:
  6.5 182.6 %all-gather.2.cloned.1.call-start = ((), (), s32[]{:S(2)}) async-start(), calls=%async_computation | async-start | bytes 12976128 | tf_op jit(solution)/shard_map/all_gather | solution.py:37
  19.9 2.7 %copy-start.1 = (f32[16,192,512]{2,1,0:T(8,128)}, f32[16,192,512]{2,1,0:T(8,128)S(1)}, u32[]{:S(2)}) copy-start(f32[16,192,512]{2,1,0:T(8,128)S(1)} %fusion.13) | copy-start | bytes 18874372
  22.8 13.3 %collective-permute-start = (f32[16,24,512]{2,1,0:T(8,128)S(1)}, f32[16,24,512]{2,1,0:T(8,128)S(1)}, u32[]{:S(2)}, u32[]{:S(2)}) collective-permute-start(f32[16,24,512]{2,1,0:T(8,128)S(1)} %get-tuple-element.108), channel_id=1, source_target_pairs={{0,32},{32,64},{64,96},{96,128},{128,160},{160,192},{192,224},{1,3... | collective-permute-start | bytes 2359304 | tf_op jit(solution)/shard_map/ppermute | solution.py:20
  24.7 13.1 %collective-permute-start.1 = (f32[16,24,512]{2,1,0:T(8,128)S(1)}, f32[16,24,512]{2,1,0:T(8,128)S(1)}, u32[]{:S(2)}, u32[]{:S(2)}) collective-permute-start(f32[16,24,512]{2,1,0:T(8,128)S(1)} %get-tuple-element.109), channel_id=1, source_target_pairs={{32,0},{64,32},{96,64},{128,96},{160,128},{192,160},{224,192},{33,... | collective-permute-start | bytes 2359304 | tf_op jit(solution)/shard_map/ppermute | solution.py:22
  47.5 12.0 %collective-permute-start.2 = (f32[192,512]{1,0:T(8,128)S(1)}, f32[192,512]{1,0:T(8,128)S(1)}, u32[]{:S(2)}, u32[]{:S(2)}) collective-permute-start(f32[192,512]{1,0:T(8,128)S(1)} %slice_bitcast_fusion.1), channel_id=1, source_target_pairs={{0,1},{1,2},{2,3},{3,4},{4,5},{5,6},{6,7},{7,8},{8,9},{9,10},{10,1... | collective-permute-start | bytes 1179656 | tf_op jit(solution)/shard_map/ppermute | solution.py:32
  60.8 2.7 %copy-start = (f32[16,192,512]{2,1,0:T(8,128)}, f32[16,192,512]{2,1,0:T(8,128)S(1)}, u32[]{:S(2)}) copy-start(f32[16,192,512]{2,1,0:T(8,128)S(1)} %fusion.6) | copy-start | bytes 18874372
  63.5 161.8 %copy-start.2 = (f32[192,512]{1,0:T(8,128)S(1)}, f32[192,512]{1,0:T(8,128)}, u32[]{:S(2)}) copy-start(f32[192,512]{1,0:T(8,128)} %param.5) | copy-start | bytes 1179652
Sparse Core Ops, SparseCore 0:
  64.4 124.6 all-gather.1
where the time goes:
time: 243 us; the launch traced here: 241 us
  waiting for transfers between devices  142 us (58%)
  other arithmetic  46.6 us (19%)
  matrix products  22.9 us (9%)
  between operations  13.5 us (6%)
  starting transfers between devices  9.16 us (4%)
  local copies, waits for them, and re-layouts  6.34 us (3%)
    all_gather x1, waiting for transfers between devices, carried_in(): pieces = lax.all_gather(value, axis)  125 us
    select_n x31, other arithmetic, turn(): return jnp.where(position < mine, longer, subtotal)  35.4 us
    dot_general x1, matrix products, body(): jnp.einsum('prc,oc->pro', levelled, column_weights, precision=lax.Precisi...  13.3 us
    dot_general x1, matrix products, body(): jnp.einsum('ok,pkc->poc', row_weights, extended, precision=lax.Precision....  9.65 us
    mul x1, other arithmetic, body(): return levelled * jnp.exp(attenuation)  9 us
    ppermute x1, waiting for transfers between devices, from_behind(): lax.ppermute(value, axis, [(source, source + steps) for source in range(f...  7.63 us
    ppermute x1, waiting for transfers between devices, padded(): lax.ppermute(tail, axis, [(i, (i + 1) % count) for i in range(ends)])  7.58 us
    unnamed x6, local copies, waits for them, and re-layouts  5.4 us
  transfers between devices with their start and end apart: 4, of which 4 were waited for; matrix products, arithmetic and copies ran while one was open for 0% of the time, Pallas kernels for 0%

commit v1 on v0

--- a/solution.py
+++ b/solution.py
@@ -32,16 +32,13 @@
     return lax.ppermute(value, axis, [(source, source + steps) for source in range(first, last)])
 
 
-def carried_in(value, axis, join, neutral):
-    count, mine = (lax.axis_size(axis), lax.axis_index(axis))
-    pieces = lax.all_gather(value, axis)
-    subtotal = jnp.full_like(value, 0) + jnp.asarray(neutral, value.dtype)
-
-    def turn(position, subtotal):
-        longer = join(subtotal, pieces[position])
-        return jnp.where(position < mine, longer, subtotal)
-
-    return lax.fori_loop(0, count - 1, turn, subtotal)
+def carried_in(total):
+    rows, cols = total.shape
+    pieces = total.reshape(8, rows // 8, 4, cols // 4).transpose(0, 2, 1, 3).reshape(32, rows // 8, cols // 4)
+    mine = lax.all_to_all(pieces, "depth", 0, 0, tiled=True)
+    earlier = jnp.cumsum(mine, axis=0) - mine
+    back = lax.all_to_all(earlier, "depth", 0, 0, tiled=True)
+    return back.reshape(8, 4, rows // 8, cols // 4).transpose(0, 2, 1, 3).reshape(rows, cols)
 
 
 def blur_weights(out_count, in_count, out_start, in_start, extent, radius):
@@ -89,10 +86,7 @@
     first_ratio = jnp.where(depth_index == 0, empty_plane, clipped(prev_last - log_planes[0]))
     local_sums = jnp.cumsum(jnp.concatenate([first_ratio[None], inner_ratios], axis=0), axis=0)
 
-    def add_planes(earlier, later):
-        return earlier + later
-
-    offset = carried_in(local_sums[-1], "depth", add_planes, empty_plane)
+    offset = carried_in(local_sums[-1])
     attenuation = local_sums + offset[None]
     return levelled * jnp.exp(attenuation)
 

time: 243 us -> 117 us (0.48)
  waiting for transfers between devices: 142 us -> 17.1 us
  blocking collectives: 0 us -> 48.2 us
  other arithmetic: 46.6 us -> 13.1 us
  between operations: 13.5 us -> 0.18 us
    all_gather x1 -> x0, waiting for transfers between devices: 125 us -> none  [carried_in(): pieces = lax.all_gather(value, axis)]
    all_to_all x0 -> x2, blocking collectives: none -> 48.2 us  [the longest x1 29.2 us: carried_in(): mine = lax.all_to_all(pieces, 'depth', 0, 0, tiled=True)]
    select_n x31 -> x0, other arithmetic: 35.4 us -> none  [turn(): return jnp.where(position < mine, longer, subtotal)]
    unnamed x6 -> x7, local copies, waits for them, and re-layouts: 5.4 us -> 5.43 us
  transfers between devices with their start and end apart: 4 -> 3, of which waited for: 4 -> 3; matrix products, arithmetic and copies ran while one was open for 0% -> 1% of each run, Pallas kernels for 0% -> 0%
where the time goes in v1:
time: 117 us; the launch traced here: 116 us
  blocking collectives  48.2 us (41%)
  matrix products  22.9 us (20%)
  waiting for transfers between devices  17.1 us (15%)
  other arithmetic  13.1 us (11%)
  starting transfers between devices  8.97 us (8%)
  local copies, waits for them, and re-layouts  5.87 us (5%)
    all_to_all x1, blocking collectives, carried_in(): mine = lax.all_to_all(pieces, 'depth', 0, 0, tiled=True)  29.2 us
    all_to_all x1, blocking collectives, carried_in(): back = lax.all_to_all(earlier, 'depth', 0, 0, tiled=True)  19.1 us
    dot_general x1, matrix products, body(): jnp.einsum('prc,oc->pro', levelled, column_weights, precision=lax.Precisi...  13.3 us
    dot_general x1, matrix products, body(): jnp.einsum('ok,pkc->poc', row_weights, extended, precision=lax.Precision....  9.65 us
    mul x1, other arithmetic, body(): return levelled * jnp.exp(attenuation)  9 us
    ppermute x1, waiting for transfers between devices, from_behind(): lax.ppermute(value, axis, [(source, source + steps) for source in range(f...  7.79 us
    ppermute x1, waiting for transfers between devices, padded(): lax.ppermute(tail, axis, [(i, (i + 1) % count) for i in range(ends)])  7.58 us
    unnamed x7, local copies, waits for them, and re-layouts  5.43 us
  transfers between devices with their start and end apart: 3, of which 3 were waited for; matrix products, arithmetic and copies ran while one was open for 1% of the time, Pallas kernels for 0%

profile of v1, /device:TPU:8, one launch (start us, length us, event | category | flops | bytes accessed | tf_op | source)
XLA Modules:
  0.0 116.4 jit_solution(6899539436796097964)
XLA Ops:
  0.0 0.1 select_reduce_fusion
  0.1 13.3 %fusion.13 = f32[16,192,512]{2,1,0:T(8,128)S(1)} fusion(f32[16,192,512]{2,1,0:T(8,128)} %param.2, f32[192,512]{1,0:T(8,128)} %param.3, f32[512]{0:T(512)S(1)} %select_reduce_fusion, pred[512]{0:T(512)(128)(4,1)S(1)} %iota_compare_fusion), kind=kOutput, calls=%fused_computation.15 | convolution fusion | flops 9667870720 | bytes 12978688 | tf_op jit(solution)/shard_map/prc,oc->pro/dot_general | solution.py:70
  13.4 0.0 copy-start.1
  13.4 2.7 %copy-done.1 = f32[16,192,512]{2,1,0:T(8,128)} copy-done((f32[16,192,512]{2,1,0:T(8,128)}, f32[16,192,512]{2,1,0:T(8,128)S(1)}, u32[]{:S(2)}) %copy-start.1) | copy-done | bytes 6291480
  16.1 0.1 fusion.66
  16.2 1.9 %collective-permute-start = (f32[16,24,512]{2,1,0:T(8,128)S(1)}, f32[16,24,512]{2,1,0:T(8,128)S(1)}, u32[]{:S(2)}, u32[]{:S(2)}) collective-permute-start(f32[16,24,512]{2,1,0:T(8,128)S(1)} %get-tuple-element.5), channel_id=1, source_target_pairs={{0,32},{32,64},{64,96},{96,128},{128,160},{160,192},{192,224},{1,3... | collective-permute-start | bytes 2359304 | tf_op jit(solution)/shard_map/ppermute | solution.py:20
  18.2 3.6 %collective-permute-start.1 = (f32[16,24,512]{2,1,0:T(8,128)S(1)}, f32[16,24,512]{2,1,0:T(8,128)S(1)}, u32[]{:S(2)}, u32[]{:S(2)}) collective-permute-start(f32[16,24,512]{2,1,0:T(8,128)S(1)} %get-tuple-element.6), channel_id=1, source_target_pairs={{32,0},{64,32},{96,64},{128,96},{160,128},{192,160},{224,192},{33,... | collective-permute-start | bytes 2359304 | tf_op jit(solution)/shard_map/ppermute | solution.py:22
  21.9 0.1 select_reduce_fusion.1
  22.0 7.6 %collective-permute-done = f32[16,24,512]{2,1,0:T(8,128)S(1)} collective-permute-done((f32[16,24,512]{2,1,0:T(8,128)S(1)}, f32[16,24,512]{2,1,0:T(8,128)S(1)}, u32[]{:S(2)}, u32[]{:S(2)}) %collective-permute-start) | collective-permute-done | bytes 786464 | tf_op jit(solution)/shard_map/ppermute | solution.py:20
  29.6 1.8 %collective-permute-done.1 = f32[16,24,512]{2,1,0:T(8,128)S(1)} collective-permute-done((f32[16,24,512]{2,1,0:T(8,128)S(1)}, f32[16,24,512]{2,1,0:T(8,128)S(1)}, u32[]{:S(2)}, u32[]{:S(2)}) %collective-permute-start.1) | collective-permute-done | bytes 786464 | tf_op jit(solution)/shard_map/ppermute | solution.py:22
  31.3 9.7 %log_bitcast_fusion = f32[16,192,512]{2,1,0:T(8,128)S(1)} fusion(f32[16,24,512]{2,1,0:T(8,128)S(1)} %collective-permute-done.1, f32[16,192,512]{2,1,0:T(8,128)} %copy-done.1, f32[16,24,512]{2,1,0:T(8,128)S(1)} %collective-permute-done, f32[192]{0:T(256)S(1)} %select_reduce_fusion.1, s32[240]{0:T(256)S(1)} %iota_add_fusion.1, s32[192]{0:T(256)S(1)} %iota_add_fusion.2, ...), kind=kOutput, calls=%fused_computation.11 | convolution fusion | flops 4534287360 | bytes 14158752 | tf_op jit(solution)/shard_map/ok,pkc->poc/dot_general | solution.py:81
  41.0 3.4 %collective-permute-start.2 = (f32[192,512]{1,0:T(8,128)S(1)}, f32[192,512]{1,0:T(8,128)S(1)}, u32[]{:S(2)}, u32[]{:S(2)}) collective-permute-start(f32[192,512]{1,0:T(8,128)S(1)} %slice_bitcast_fusion.1), channel_id=1, source_target_pairs={{0,1},{1,2},{2,3},{3,4},{4,5},{5,6},{6,7},{7,8},{8,9},{9,10},{10,1... | collective-permute-start | bytes 1179656 | tf_op jit(solution)/shard_map/ppermute | solution.py:32
  44.4 0.8 fusion.10
  45.2 7.8 %collective-permute-done.2 = f32[192,512]{1,0:T(8,128)S(1)} collective-permute-done((f32[192,512]{1,0:T(8,128)S(1)}, f32[192,512]{1,0:T(8,128)S(1)}, u32[]{:S(2)}, u32[]{:S(2)}) %collective-permute-start.2) | collective-permute-done | bytes 393248 | tf_op jit(solution)/shard_map/ppermute | solution.py:32
  53.0 0.1 fusion.31
  53.1 1.1 fusion.6
  54.2 0.0 copy-start
  54.2 2.7 %copy-done = f32[16,192,512]{2,1,0:T(8,128)} copy-done((f32[16,192,512]{2,1,0:T(8,128)}, f32[16,192,512]{2,1,0:T(8,128)S(1)}, u32[]{:S(2)}) %copy-start) | copy-done | bytes 6291480
  56.9 0.0 copy-start.2
  56.9 0.1 reshape_squeeze.3
  57.1 29.2 %all_to_all.10 = f32[32,24,128]{2,1,0:T(8,128)S(1)} all-to-all(f32[32,24,128]{2,1,0:T(8,128)S(1)} %bitcast.34), channel_id=1, replica_groups=mesh['tile'=8,'depth'=32] {'depth'}, dimensions={0} | all-to-all | bytes 786432 | tf_op jit(solution)/shard_map/all_to_all | solution.py:38
  86.3 1.9 %reduce-window_subtract_fusion = f32[32,24,128]{2,1,0:T(8,128)S(1)} fusion(f32[32,24,128]{2,1,0:T(8,128)S(1)} %all_to_all.10), kind=kOutput, calls=%fused_computation.17 | output fusion | flops 3145728 | bytes 786432 | tf_op jit(solution)/shard_map/jit(cumsum)/reduce_window_sum | solution.py:39
  88.2 19.1 %all_to_all.11 = f32[32,24,128]{2,1,0:T(8,128)S(1)} all-to-all(f32[32,24,128]{2,1,0:T(8,128)S(1)} %reduce-window_subtract_fusion), channel_id=1, replica_groups=mesh['tile'=8,'depth'=32] {'depth'}, dimensions={0} | all-to-all | bytes 786432 | tf_op jit(solution)/shard_map/all_to_all | solution.py:40
  107.3 0.1 copy.6
  107.4 0.0 copy-done.2
  107.4 9.0 %exponential_multiply_fusion = f32[16,192,512]{2,1,0:T(8,128)} fusion(f32[16,192,512]{2,1,0:T(8,128)} %copy-done, f32[192,512]{1,0:T(8,128)S(1)} %bitcast.37, f32[16,192,512]{2,1,0:T(8,128)} %param.2, f32[192,512]{1,0:T(8,128)S(1)} %copy-done.2), kind=kLoop, calls=%fused_computation.10 | loop fusion | flops 4718592 | bytes 19660800 | tf_op jit(solution)/shard_map/mul | solution.py:91
  (10 shorter events, 0.1 us)
Async XLA Ops:
  13.4 2.7 %copy-start.1 = (f32[16,192,512]{2,1,0:T(8,128)}, f32[16,192,512]{2,1,0:T(8,128)S(1)}, u32[]{:S(2)}) copy-start(f32[16,192,512]{2,1,0:T(8,128)S(1)} %fusion.13) | copy-start | bytes 18874372
  16.2 13.3 %collective-permute-start = (f32[16,24,512]{2,1,0:T(8,128)S(1)}, f32[16,24,512]{2,1,0:T(8,128)S(1)}, u32[]{:S(2)}, u32[]{:S(2)}) collective-permute-start(f32[16,24,512]{2,1,0:T(8,128)S(1)} %get-tuple-element.5), channel_id=1, source_target_pairs={{0,32},{32,64},{64,96},{96,128},{128,160},{160,192},{192,224},{1,3... | collective-permute-start | bytes 2359304 | tf_op jit(solution)/shard_map/ppermute | solution.py:20
  18.2 13.1 %collective-permute-start.1 = (f32[16,24,512]{2,1,0:T(8,128)S(1)}, f32[16,24,512]{2,1,0:T(8,128)S(1)}, u32[]{:S(2)}, u32[]{:S(2)}) collective-permute-start(f32[16,24,512]{2,1,0:T(8,128)S(1)} %get-tuple-element.6), channel_id=1, source_target_pairs={{32,0},{64,32},{96,64},{128,96},{160,128},{192,160},{224,192},{33,... | collective-permute-start | bytes 2359304 | tf_op jit(solution)/shard_map/ppermute | solution.py:22
  41.0 12.0 %collective-permute-start.2 = (f32[192,512]{1,0:T(8,128)S(1)}, f32[192,512]{1,0:T(8,128)S(1)}, u32[]{:S(2)}, u32[]{:S(2)}) collective-permute-start(f32[192,512]{1,0:T(8,128)S(1)} %slice_bitcast_fusion.1), channel_id=1, source_target_pairs={{0,1},{1,2},{2,3},{3,4},{4,5},{5,6},{6,7},{7,8},{8,9},{9,10},{10,1... | collective-permute-start | bytes 1179656 | tf_op jit(solution)/shard_map/ppermute | solution.py:32
  54.2 2.7 %copy-start = (f32[16,192,512]{2,1,0:T(8,128)}, f32[16,192,512]{2,1,0:T(8,128)S(1)}, u32[]{:S(2)}) copy-start(f32[16,192,512]{2,1,0:T(8,128)S(1)} %fusion.6) | copy-start | bytes 18874372
  56.9 50.5 %copy-start.2 = (f32[192,512]{1,0:T(8,128)S(1)}, f32[192,512]{1,0:T(8,128)}, u32[]{:S(2)}) copy-start(f32[192,512]{1,0:T(8,128)} %param.3) | copy-start | bytes 1179652

commit v2 on v1

v2 whole, which is shorter than its diff:
```python
import jax
import jax.numpy as jnp
from jax import lax
from jax.experimental import pallas as pl
from jax.experimental.pallas import tpu as pltpu
from jax.sharding import PartitionSpec as P
import math

RADIUS = 24
CLIP_LIMIT = 0.08
LOW = math.exp(-CLIP_LIMIT)
HIGH = math.exp(CLIP_LIMIT)
MIB = 1 << 20
STEP = 2


def blur_weights(out_index, in_index, extent, radius):
    spread = radius / 3.0
    out_index = out_index[:, None]
    in_index = in_index[None, :]
    distance = (out_index - in_index).astype(jnp.float32)
    inside = (jnp.abs(out_index - in_index) <= radius) & (in_index >= 0) & (in_index < extent)
    kernel = jnp.where(inside, jnp.exp(-distance * distance / (2.0 * spread * spread)), 0.0)
    reach = lax.iota(jnp.int32, 2 * radius + 1)[None, :] - radius
    target = out_index + reach
    valid = (target >= 0) & (target < extent)
    reach_float = reach.astype(jnp.float32)
    weights = jnp.where(valid, jnp.exp(-reach_float * reach_float / (2.0 * spread * spread)), 0.0)
    normaliser = jnp.sum(weights, axis=1, keepdims=True)
    return kernel / normaliser


def halves(value):
    high = value.astype(jnp.bfloat16)
    return high, (value - high.astype(jnp.float32)).astype(jnp.bfloat16)


def split_weights(weights):
    high = lax.reduce_precision(weights, 8, 7)
    return high.astype(jnp.bfloat16), (weights - high).astype(jnp.bfloat16)


def mul(left, right):
    return jnp.dot(left, right, preferred_element_type=jnp.float32)


def row_blur(high_low, low, weight):
    rows = weight.shape[0] // 2
    both = mul(weight[...], high_low)
    return both[:rows] + (both[rows:] + mul(weight[:rows], low))


def column_blur(value, weight_high, weight_low):
    high, low = halves(value)
    return mul(high, weight_high) + (mul(high, weight_low) + mul(low, weight_high))


def advance(blurred, levelled, start, first, last, product, out, put):
    rows = first.shape[0]
    before = last[...]
    running = product[...]
    for plane in range(STEP):
        now = blurred[plane * rows:(plane + 1) * rows]
        ratio = jnp.clip(before / now, LOW, HIGH)
        if plane == 0:
            ratio = jnp.where(start, 1.0, ratio)
            running = jnp.where(start, 1.0, running)

            @pl.when(start)
            def _():
                first[...] = now
        running = running * ratio
        put(out, plane, levelled[plane] * running)
        before = now
    last[...] = before
    product[...] = running


def middle_kernel(volume, flat, row_weight, col_high, col_low, out, first, last, product, inverse):
    start = pl.program_id(0) == 0

    @pl.when(start)
    def _():
        inverse[...] = 1.0 / flat[...]
        last[...] = jnp.ones_like(last)
        product[...] = jnp.ones_like(product)

    count = volume.shape[1]
    levelled, parts = [], []
    for plane in range(STEP):
        value = volume[plane] * inverse[...]
        high, low = halves(value)
        parts.append(row_blur(high, low, row_weight))
        levelled.append(value[RADIUS:count - RADIUS])
    blurred = column_blur(jnp.concatenate(parts, axis=0), col_high[...], col_low[...])

    def put(ref, plane, value):
        ref[plane] = value

    advance(blurred, levelled, start, first, last, product, out, put)


def edge_kernel(top, bottom, above, below, flat_top, flat_bottom, row_weight, col_high, col_low, out, first, last, product, inverse):
    start = pl.program_id(0) == 0
    near = 2 * RADIUS

    @pl.when(start)
    def _():
        inverse[:near] = 1.0 / flat_top[...]
        inverse[near:] = 1.0 / flat_bottom[...]
        last[...] = jnp.ones_like(last)
        product[...] = jnp.ones_like(product)

    levelled, parts = [], []
    for plane in range(STEP):
        upper = top[plane] * inverse[:near]
        lower = bottom[plane] * inverse[near:]
        value = jnp.concatenate([above[plane], upper, lower, below[plane]], axis=0)
        high, low = halves(value)
        parts.append(row_blur(high, low, row_weight))
        levelled.append(jnp.concatenate([upper[:RADIUS], lower[RADIUS:]], axis=0))
    blurred = column_blur(jnp.concatenate(parts, axis=0), col_high[...], col_low[...])

    def put(ref, plane, value):
        ref[plane] = value

    advance(blurred, levelled, start, first, last, product, out, put)


def join_kernel(at_start, before, first_mid, first_edge, product_mid, product_edge, step_out, pieces):
    rows, cols = before.shape
    groups = rows // RADIUS
    lead = at_start[0] == 1
    wide = cols // 4
    for group in range(groups):
        at = pl.ds(group * RADIUS, RADIUS)
        if group == 0:
            edge = pl.ds(0, RADIUS)
        elif group == groups - 1:
            edge = pl.ds(RADIUS, RADIUS)
        else:
            edge = None
        inner = pl.ds((group - 1) * RADIUS, RADIUS)
        first = first_mid[inner] if edge is None else first_edge[edge]
        product = product_mid[inner] if edge is None else product_edge[edge]
        ratio = jnp.where(lead, 1.0, jnp.clip(before[at] / first, LOW, HIGH))
        step_out[at] = ratio
        product = product * ratio
        for part in range(4):
            pieces[group * 4 + part] = product[:, part * wide:(part + 1) * wide]


def scan_kernel(pieces, out):
    running = jnp.ones(pieces.shape[1:], jnp.float32)
    for slab in range(pieces.shape[0]):
        out[slab] = running
        running = running * pieces[slab]


def final_kernel(middle, edge, step, pieces, out, factor):
    rows, cols = step.shape
    wide = cols // 4

    @pl.when(pl.program_id(0) == 0)
    def _():
        for group in range(rows // RADIUS):
            at = pl.ds(group * RADIUS, RADIUS)
            for part in range(4):
                over = pl.ds(part * wide, wide)
                factor[at, over] = step[at, over] * pieces[group * 4 + part]

    for plane in range(out.shape[0]):
        out[plane, :RADIUS] = edge[plane, :RADIUS] * factor[:RADIUS]
        out[plane, RADIUS:rows - RADIUS] = middle[plane] * factor[RADIUS:rows - RADIUS]
        out[plane, rows - RADIUS:] = edge[plane, RADIUS:] * factor[rows - RADIUS:]


def shape(*dims):
    return jax.ShapeDtypeStruct(dims, jnp.float32)


def whole(*dims):
    return pl.BlockSpec(dims, lambda i: (0,) * len(dims))


def params(mib=48):
    return pltpu.CompilerParams(vmem_limit_bytes=mib * MIB)


def middle_call(volume, flat, row_weight, col_high, col_low):
    planes, rows, cols = volume.shape
    inner = rows - 2 * RADIUS
    return pl.pallas_call(
        middle_kernel,
        grid=(planes // STEP,),
        in_specs=[
            pl.BlockSpec((STEP, rows, cols), lambda i: (i, 0, 0)),
            whole(rows, cols),
            whole(*row_weight.shape),
            whole(cols, cols),
            whole(cols, cols),
        ],
        out_specs=[pl.BlockSpec((STEP, inner, cols), lambda i: (i, 0, 0))] + [whole(inner, cols)] * 3,
        out_shape=[shape(planes, inner, cols)] + [shape(inner, cols)] * 3,
        scratch_shapes=[pltpu.VMEM((rows, cols), jnp.float32)],
        compiler_params=params(),
        cost_estimate=pl.CostEstimate(flops=12_000_000_000, bytes_accessed=12_000_000, transcendentals=1_000_000),
    )(volume, flat, row_weight, col_high, col_low)


def edge_call(volume, above, below, flat, row_weight, col_high, col_low):
    planes, rows, cols = volume.shape
    near = 2 * RADIUS
    ends = rows // near - 1
    halo = pl.BlockSpec((STEP, RADIUS, cols), lambda i: (i, 0, 0))
    return pl.pallas_call(
        edge_kernel,
        grid=(planes // STEP,),
        in_specs=[
            pl.BlockSpec((STEP, near, cols), lambda i: (i, 0, 0)),
            pl.BlockSpec((STEP, near, cols), lambda i: (i, ends, 0)),
            halo,
            halo,
            pl.BlockSpec((near, cols), lambda i: (0, 0)),
            pl.BlockSpec((near, cols), lambda i: (ends, 0)),
            whole(*row_weight.shape),
            whole(cols, cols),
            whole(cols, cols),
        ],
        out_specs=[pl.BlockSpec((STEP, near, cols), lambda i: (i, 0, 0))] + [whole(near, cols)] * 3,
        out_shape=[shape(planes, near, cols)] + [shape(near, cols)] * 3,
        scratch_shapes=[pltpu.VMEM((2 * near, cols), jnp.float32)],
        compiler_params=params(),
        cost_estimate=pl.CostEstimate(flops=4_000_000_000, bytes_accessed=8_000_000, transcendentals=400_000),
    )(volume, volume, above, below, flat, flat, row_weight, col_high, col_low)


def final_call(middle, edge, step, pieces):
    planes, inner, cols = middle.shape
    rows = inner + 2 * RADIUS
    group = 4
    return pl.pallas_call(
        final_kernel,
        grid=(planes // group,),
        in_specs=[
            pl.BlockSpec((group, inner, cols), lambda i: (i, 0, 0)),
            pl.BlockSpec((group, 2 * RADIUS, cols), lambda i: (i, 0, 0)),
            whole(rows, cols),
            whole(*pieces.shape),
        ],
        out_specs=pl.BlockSpec((group, rows, cols), lambda i: (i, 0, 0)),
        out_shape=shape(planes, rows, cols),
        scratch_shapes=[pltpu.VMEM((rows, cols), jnp.float32)],
        compiler_params=params(),
    )(middle, edge, step, pieces)


def make_weights(rows, cols, tile_index, extent):
    base = tile_index * rows
    column = blur_weights(lax.iota(jnp.int32, cols), lax.iota(jnp.int32, cols), cols, RADIUS).T
    col_high, col_low = split_weights(column)
    ext = base - RADIUS + lax.iota(jnp.int32, rows + 2 * RADIUS)
    every = blur_weights(base + lax.iota(jnp.int32, rows), ext, extent, RADIUS)
    mid_high, mid_low = split_weights(every[RADIUS:rows - RADIUS, RADIUS:rows + RADIUS])
    near = 3 * RADIUS
    gap = jnp.zeros((RADIUS, near), jnp.float32)
    edge = jnp.concatenate(
        [
            jnp.concatenate([every[:RADIUS, :near], gap], axis=1),
            jnp.concatenate([gap, every[rows - RADIUS:, rows + 2 * RADIUS - near:]], axis=1),
        ],
        axis=0,
    )
    edge_high, edge_low = split_weights(edge)
    return (
        jnp.concatenate([mid_high, mid_low], axis=0),
        jnp.concatenate([edge_high, edge_low], axis=0),
        col_high,
        col_low,
    )


def body(volume, flat_field):
    planes, rows, cols = volume.shape
    tile_index = lax.axis_index("tile")
    depth_index = lax.axis_index("depth")
    tiles, slabs = lax.axis_size("tile"), lax.axis_size("depth")
    top = volume[:, :RADIUS] / flat_field[:RADIUS]
    bottom = volume[:, rows - RADIUS:] / flat_field[rows - RADIUS:]
    above = lax.ppermute(bottom, "tile", [(i, i + 1) for i in range(tiles - 1)])
    below = lax.ppermute(top, "tile", [(i + 1, i) for i in range(tiles - 1)])
    mid_weight, edge_weight, col_high, col_low = make_weights(rows, cols, tile_index, rows * tiles)
    middle, first_mid, last_mid, product_mid = middle_call(volume, flat_field, mid_weight, col_high, col_low)
    edge, first_edge, last_edge, product_edge = edge_call(volume, above, below, flat_field, edge_weight, col_high, col_low)
    deepest = jnp.concatenate([last_edge[:RADIUS], last_mid, last_edge[RADIUS:]], axis=0)
    before = lax.ppermute(deepest, "depth", [(i, i + 1) for i in range(slabs - 1)])
    at_start = (depth_index == 0).astype(jnp.int32).reshape(1)
    vmem = pl.BlockSpec(memory_space=pltpu.VMEM)
    step, pieces = pl.pallas_call(
        join_kernel,
        in_specs=[pl.BlockSpec(memory_space=pltpu.SMEM)] + [vmem] * 5,
        out_specs=[vmem] * 2,
        out_shape=[shape(rows, cols), shape(slabs, RADIUS, cols // 4)],
        compiler_params=params(16),
    )(at_start, before, first_mid, first_edge, product_mid, product_edge)
    mine = lax.all_to_all(pieces, "depth", 0, 0, tiled=True)
    earlier = pl.pallas_call(
        scan_kernel, in_specs=[vmem], out_specs=vmem, out_shape=shape(slabs, RADIUS, cols // 4), compiler_params=params(16)
    )(mine)
    back = lax.all_to_all(earlier, "depth", 0, 0, tiled=True)
    return final_call(middle, edge, step, back)


def solution(mesh):
    return jax.shard_map(
        body,
        mesh=mesh,
        in_specs=(P("depth", "tile", None), P("tile", None)),
        out_specs=P("depth", "tile", None),
        check_vma=False,
    )
```

time: 117 us -> 97.3 us (0.83)
  Pallas kernels: 0 us -> 25 us
  matrix products: 22.9 us -> 0 us
  other arithmetic: 13.1 us -> 2.53 us
  waiting for transfers between devices: 17.1 us -> 9.24 us
  local copies, waits for them, and re-layouts: 5.87 us -> 4.33 us
  starting transfers between devices: 8.97 us -> 7.74 us
    pallas_call x0 -> x5, Pallas kernels: none -> 25 us  [the longest x1 11.7 us: middle_call(): pl.pallas_call(middle_kernel, grid=(planes // STEP,), in_specs=[pl.BlockS...]
    dot_general x2 -> x0, matrix products: 22.9 us -> none  [the longest x1 13.3 us: body(): jnp.einsum('prc,oc->pro', levelled, column_weights, precision=lax.Precisi...]
    mul x1 -> x0, other arithmetic: 9 us -> none  [body(): return levelled * jnp.exp(attenuation)]
    ppermute x3, waiting for transfers between devices: 17.1 us -> 9.24 us  [the longest x1 9.23 us: body(): lax.ppermute(deepest, 'depth', [(i, i + 1) for i in range(slabs - 1)])]
    another operation x2 -> x0, other arithmetic: 2.99 us -> none  [the longest x1 1.87 us: carried_in(): earlier = jnp.cumsum(mine, axis=0) - mine]
    unnamed x7 -> x10, local copies, waits for them, and re-layouts: 5.43 us -> 3.42 us
    div x0 -> x2, other arithmetic: none -> 1.8 us  [the longest x1 1.62 us: body(): top = volume[:, :RADIUS] / flat_field[:RADIUS]]
    ppermute x3, starting transfers between devices: 8.97 us -> 7.74 us  [the longest x1 3.41 us: body(): lax.ppermute(deepest, 'depth', [(i, i + 1) for i in range(slabs - 1)])]
  transfers between devices with their start and end apart: 3 -> 3, of which waited for: 3 -> 1; matrix products, arithmetic and copies ran while one was open for 1% -> 1% of each run, Pallas kernels for 0% -> 12%
where the time goes in v2:
time: 97.3 us; the launch traced here: 96.3 us
  blocking collectives  47.2 us (49%)
  Pallas kernels  25 us (26%)
  waiting for transfers between devices  9.24 us (9%)
  starting transfers between devices  7.74 us (8%)
  local copies, waits for them, and re-layouts  4.33 us (4%)
  other arithmetic  2.53 us (3%)
    all_to_all x1, blocking collectives, body(): mine = lax.all_to_all(pieces, 'depth', 0, 0, tiled=True)  28.5 us
    all_to_all x1, blocking collectives, body(): back = lax.all_to_all(earlier, 'depth', 0, 0, tiled=True)  18.7 us
    pallas_call x1, Pallas kernels, middle_call(): pl.pallas_call(middle_kernel, grid=(planes // STEP,), in_specs=[pl.BlockS...  11.7 us
    ppermute x1, waiting for transfers between devices, body(): lax.ppermute(deepest, 'depth', [(i, i + 1) for i in range(slabs - 1)])  9.23 us
    pallas_call x1, Pallas kernels, edge_call(): pl.pallas_call(edge_kernel, grid=(planes // STEP,), in_specs=[pl.BlockSpe...  7.63 us
    pallas_call x1, Pallas kernels, final_call(): pl.pallas_call(final_kernel, grid=(planes // group,), in_specs=[pl.BlockS...  5.56 us
    unnamed x10, local copies, waits for them, and re-layouts  3.42 us
    ppermute x1, starting transfers between devices, body(): lax.ppermute(deepest, 'depth', [(i, i + 1) for i in range(slabs - 1)])  3.41 us
  transfers between devices with their start and end apart: 3, of which 1 were waited for; matrix products, arithmetic and copies ran while one was open for 1% of the time, Pallas kernels for 12%

profile of v2, /device:TPU:8, one launch (start us, length us, event | category | flops | bytes accessed | tf_op | source)
XLA Modules:
  0.0 96.3 jit_solution(10487645363440247361)
XLA Ops:
  0.0 0.8 fusion.23
  0.8 1.6 %slice_divide_fusion = (f32[16,24,512]{2,1,0:T(8,128)S(1)}, f32[16,24,512]{2,1,0:T(8,128)S(1)}) fusion(f32[16,192,512]{2,1,0:T(8,128)} %bottom.1, f32[24,512]{1,0:T(8,128)S(1)} %get-tuple-element.27, f32[24,512]{1,0:T(8,128)S(1)} %get-tuple-element.28), kind=kLoop, calls=%fused_computation.11 | loop fusion | flops 393216 | bytes 3244032 | tf_op jit(solution)/shard_map/div | solution.py:288
  2.5 1.9 %collective-permute-start.1 = (f32[16,24,512]{2,1,0:T(8,128)S(1)}, f32[16,24,512]{2,1,0:T(8,128)S(1)}, u32[]{:S(2)}, u32[]{:S(2)}) collective-permute-start(f32[16,24,512]{2,1,0:T(8,128)S(1)} %get-tuple-element.25), channel_id=1, source_target_pairs={{32,0},{64,32},{96,64},{128,96},{160,128},{192,160},{224,192},{33,... | collective-permute-start | bytes 2359304 | tf_op jit(solution)/shard_map/ppermute | solution.py:291
  4.4 2.4 %collective-permute-start = (f32[16,24,512]{2,1,0:T(8,128)S(1)}, f32[16,24,512]{2,1,0:T(8,128)S(1)}, u32[]{:S(2)}, u32[]{:S(2)}) collective-permute-start(f32[16,24,512]{2,1,0:T(8,128)S(1)} %get-tuple-element.26), channel_id=1, source_target_pairs={{0,32},{32,64},{64,96},{96,128},{128,160},{160,192},{192,224},{1,3... | collective-permute-start | bytes 2359304 | tf_op jit(solution)/shard_map/ppermute | solution.py:290
  6.9 0.1 select_reduce_fusion
  7.0 0.1 select_reduce_fusion.1
  7.1 0.2 fusion.10
  7.3 0.1 fusion.24
  7.4 0.1 reduce-precision_convert_fusion.1
  7.5 0.1 reduce-precision_convert_fusion.2
  7.6 0.2 fusion
  7.8 0.0 copy-start
  7.9 1.0 %copy-done = f32[192,512]{1,0:T(8,128)S(1)} copy-done((f32[192,512]{1,0:T(8,128)S(1)}, f32[192,512]{1,0:T(8,128)}, u32[]{:S(2)}) %copy-start) | copy-done | bytes 393240
  8.8 11.7 %shard_map.28 = (f32[16,144,512]{2,1,0:T(8,128)}, f32[144,512]{1,0:T(8,128)S(1)}, f32[144,512]{1,0:T(8,128)S(1)}, f32[144,512]{1,0:T(8,128)S(1)}) custom-call(f32[16,192,512]{2,1,0:T(8,128)} %bottom.1, f32[192,512]{1,0:T(8,128)S(1)} %copy-done, bf16[288,192]{1,0:T(8,128)(2,1)S(1)} %pad_maximum_fusion.1.row_weight, ...), custom_call_target="tpu_custom_call" | custom-call | flops 12000000000 | bytes 12000000 | tf_op jit(solution)/shard_map/pallas_call | solution.py:193
  20.6 0.0 copy-start.1
  20.6 0.0 collective-permute-done.1.below
  20.6 0.0 collective-permute-done.above
  20.6 7.6 %shard_map.29 = (f32[16,48,512]{2,1,0:T(8,128)S(1)}, f32[48,512]{1,0:T(8,128)S(1)}, f32[48,512]{1,0:T(8,128)S(1)}, f32[48,512]{1,0:T(8,128)S(1)}) custom-call(f32[16,192,512]{2,1,0:T(8,128)} %bottom.1, f32[16,192,512]{2,1,0:T(8,128)} %bottom.1, f32[16,24,512]{2,1,0:T(8,128)S(1)} %collective-permute-done.above, ...), custom_call_target="tpu_custom_call" | custom-call | flops 4000000000 | bytes 8000000 | tf_op jit(solution)/shard_map/pallas_call | solution.py:216
  28.2 0.0 copy-done.1
  28.2 0.0 copy-start.3
  28.3 0.6 copy-done.3
  28.9 3.4 %collective-permute-start.2 = (f32[192,512]{1,0:T(8,128)S(1)}, f32[192,512]{1,0:T(8,128)S(1)}, u32[]{:S(2)}, u32[]{:S(2)}) collective-permute-start(f32[192,512]{1,0:T(8,128)S(1)} %pad_maximum_fusion), channel_id=1, source_target_pairs={{0,1},{1,2},{2,3},{3,4},{4,5},{5,6},{6,7},{7,8},{8,9},{9,10},{10,1... | collective-permute-start | bytes 1179656 | tf_op jit(solution)/shard_map/ppermute | solution.py:296
  32.3 9.2 %collective-permute-done.2.before = f32[192,512]{1,0:T(8,128)S(1)} collective-permute-done((f32[192,512]{1,0:T(8,128)S(1)}, f32[192,512]{1,0:T(8,128)S(1)}, u32[]{:S(2)}, u32[]{:S(2)}) %collective-permute-start.2) | collective-permute-done | bytes 393248 | tf_op jit(solution)/shard_map/ppermute | solution.py:296
  41.5 0.0 copy-start.2
  41.5 1.0 copy-done.2
  42.5 0.0 copy-start.4
  42.5 0.9 copy-done.4
  43.4 0.1 shard_map.30
  43.5 28.5 %all_to_all.10.pieces = f32[32,24,128]{2,1,0:T(8,128)S(1)} all-to-all(f32[32,24,128]{2,1,0:T(8,128)S(1)} %get-tuple-element.24), channel_id=1, replica_groups=mesh['tile'=8,'depth'=32] {'depth'}, dimensions={0} | all-to-all | bytes 786432 | tf_op jit(solution)/shard_map/all_to_all | solution.py:306
  72.0 18.7 %all_to_all.11.pieces = f32[32,24,128]{2,1,0:T(8,128)S(1)} all-to-all(f32[32,24,128]{2,1,0:T(8,128)S(1)} %shard_map.31), channel_id=1, replica_groups=mesh['tile'=8,'depth'=32] {'depth'}, dimensions={0} | all-to-all | bytes 786432 | tf_op jit(solution)/shard_map/all_to_all | solution.py:310
  90.7 5.6 %shard_map.32 = f32[16,192,512]{2,1,0:T(8,128)} custom-call(f32[16,144,512]{2,1,0:T(8,128)} %get-tuple-element.15.middle, f32[16,48,512]{2,1,0:T(8,128)S(1)} %get-tuple-element.16.edge, f32[192,512]{1,0:T(8,128)S(1)} %get-tuple-element.23.step, f32[32,24,128]{2,1,0:T(8,128)S(1)} %all_to_all.11.pieces), custom_call_target="tpu_custom_call" | custom-call | tf_op jit(solution)/shard_map/pallas_call | solution.py:242
  (11 shorter events, 0.1 us)
Async XLA Ops:
  2.5 18.1 %collective-permute-start.1 = (f32[16,24,512]{2,1,0:T(8,128)S(1)}, f32[16,24,512]{2,1,0:T(8,128)S(1)}, u32[]{:S(2)}, u32[]{:S(2)}) collective-permute-start(f32[16,24,512]{2,1,0:T(8,128)S(1)} %get-tuple-element.25), channel_id=1, source_target_pairs={{32,0},{64,32},{96,64},{128,96},{160,128},{192,160},{224,192},{33,... | collective-permute-start | bytes 2359304 | tf_op jit(solution)/shard_map/ppermute | solution.py:291
  4.4 16.2 %collective-permute-start = (f32[16,24,512]{2,1,0:T(8,128)S(1)}, f32[16,24,512]{2,1,0:T(8,128)S(1)}, u32[]{:S(2)}, u32[]{:S(2)}) collective-permute-start(f32[16,24,512]{2,1,0:T(8,128)S(1)} %get-tuple-element.26), channel_id=1, source_target_pairs={{0,32},{32,64},{64,96},{96,128},{128,160},{160,192},{192,224},{1,3... | collective-permute-start | bytes 2359304 | tf_op jit(solution)/shard_map/ppermute | solution.py:290
  7.8 1.0 %copy-start = (f32[192,512]{1,0:T(8,128)S(1)}, f32[192,512]{1,0:T(8,128)}, u32[]{:S(2)}) copy-start(f32[192,512]{1,0:T(8,128)} %flat_bottom.1) | copy-start | bytes 1179652
  20.6 7.7 %copy-start.1 = (f32[144,512]{1,0:T(8,128)}, f32[144,512]{1,0:T(8,128)S(1)}, u32[]{:S(2)}) copy-start(f32[144,512]{1,0:T(8,128)S(1)} %get-tuple-element.21.product_mid) | copy-start | bytes 884740
  28.2 0.6 copy-start.3
  28.9 12.7 %collective-permute-start.2 = (f32[192,512]{1,0:T(8,128)S(1)}, f32[192,512]{1,0:T(8,128)S(1)}, u32[]{:S(2)}, u32[]{:S(2)}) collective-permute-start(f32[192,512]{1,0:T(8,128)S(1)} %pad_maximum_fusion), channel_id=1, source_target_pairs={{0,1},{1,2},{2,3},{3,4},{4,5},{5,6},{6,7},{7,8},{8,9},{9,10},{10,1... | collective-permute-start | bytes 1179656 | tf_op jit(solution)/shard_map/ppermute | solution.py:296
  41.5 1.0 copy-start.2
  42.5 0.9 copy-start.4

commit v3 on v2

v3 whole, which is shorter than its diff:
```python
import jax
import jax.numpy as jnp
from jax import lax
from jax.experimental import pallas as pl
from jax.experimental.pallas import tpu as pltpu
from jax.sharding import PartitionSpec as P
import math

RADIUS = 24
CLIP_LIMIT = 0.08
LOW = math.exp(-CLIP_LIMIT)
HIGH = math.exp(CLIP_LIMIT)
MIB = 1 << 20
STEP = 4
EDGE_STEP = 8
GRANT = 20
TOGETHER = True


def blur_weights(out_index, in_index, extent, radius):
    spread = radius / 3.0
    out_index = out_index[:, None]
    in_index = in_index[None, :]
    distance = (out_index - in_index).astype(jnp.float32)
    inside = (jnp.abs(out_index - in_index) <= radius) & (in_index >= 0) & (in_index < extent)
    kernel = jnp.where(inside, jnp.exp(-distance * distance / (2.0 * spread * spread)), 0.0)
    reach = lax.iota(jnp.int32, 2 * radius + 1)[None, :] - radius
    target = out_index + reach
    valid = (target >= 0) & (target < extent)
    reach_float = reach.astype(jnp.float32)
    weights = jnp.where(valid, jnp.exp(-reach_float * reach_float / (2.0 * spread * spread)), 0.0)
    normaliser = jnp.sum(weights, axis=1, keepdims=True)
    return kernel / normaliser


def halves(value):
    high = value.astype(jnp.bfloat16)
    return high, (value - high.astype(jnp.float32)).astype(jnp.bfloat16)


def split_weights(weights):
    high = lax.reduce_precision(weights, 8, 7)
    return high.astype(jnp.bfloat16), (weights - high).astype(jnp.bfloat16)


def mul(left, right):
    return jnp.dot(left, right, preferred_element_type=jnp.float32)


def row_blur(high, low, weight):
    rows = weight.shape[0] // 2
    both = mul(weight[...], high)
    return both[:rows] + (both[rows:] + mul(weight[:rows], low))


def column_blur(value, weight_high, weight_low):
    high, low = halves(value)
    return mul(high, weight_high) + (mul(high, weight_low) + mul(low, weight_high))


def retreat(blurred, levelled, fresh, later, factor, deepest, out):
    after, running = later[...], factor[...]
    for plane in reversed(range(len(blurred))):
        now = blurred[plane]
        inverse = jnp.clip(after / now, LOW, HIGH)
        if plane == len(blurred) - 1 and fresh is not None:
            inverse = jnp.where(fresh, 1.0, inverse)

            @pl.when(fresh)
            def _():
                deepest[...] = now

        running = running * inverse
        out[plane] = levelled[plane] * running
        after = now
    later[...] = after
    factor[...] = running


def blur_planes(parts, col_high, col_low, together):
    rows = parts[0].shape[0]
    if together:
        blurred = column_blur(jnp.concatenate(parts, axis=0), col_high[...], col_low[...])
        return [blurred[plane * rows:(plane + 1) * rows] for plane in range(len(parts))]
    return [column_blur(part, col_high[...], col_low[...]) for part in parts]


def middle_planes(volume, inverse, row_weight):
    count = volume.shape[1]
    levelled, parts = [], []
    for plane in range(volume.shape[0]):
        value = volume[plane] * inverse[...]
        high, low = halves(value)
        parts.append(row_blur(high, low, row_weight))
        levelled.append(value[RADIUS:count - RADIUS])
    return levelled, parts


def deep_kernel(volume, flat, row_weight, col_high, col_low, out, deepest, later, factor, inverse):
    start = pl.program_id(0) == 0

    @pl.when(start)
    def _():
        inverse[...] = 1.0 / flat[...]
        later[...] = jnp.ones_like(later)
        factor[...] = jnp.ones_like(factor)

    levelled, parts = middle_planes(volume, inverse, row_weight)
    retreat(blur_planes(parts, col_high, col_low, TOGETHER), levelled, start, later, factor, deepest, out)


def shallow_kernel(volume, flat, row_weight, col_high, col_low, later_in, factor_in, out, later, factor, inverse):
    @pl.when(pl.program_id(0) == 0)
    def _():
        inverse[...] = 1.0 / flat[...]
        later[...] = later_in[...]
        factor[...] = factor_in[...]

    levelled, parts = middle_planes(volume, inverse, row_weight)
    retreat(blur_planes(parts, col_high, col_low, TOGETHER), levelled, None, later, factor, None, out)


def edge_kernel(top, bottom, above, below, flat_top, flat_bottom, row_weight, col_high, col_low, out, deepest, later, factor, inverse):
    start = pl.program_id(0) == 0
    near = 2 * RADIUS

    @pl.when(start)
    def _():
        inverse[:near] = 1.0 / flat_top[...]
        inverse[near:] = 1.0 / flat_bottom[...]
        later[...] = jnp.ones_like(later)
        factor[...] = jnp.ones_like(factor)

    levelled, parts = [], []
    for plane in range(top.shape[0]):
        upper = top[plane] * inverse[:near]
        lower = bottom[plane] * inverse[near:]
        value = jnp.concatenate([above[plane], upper, lower, below[plane]], axis=0)
        high, low = halves(value)
        parts.append(row_blur(high, low, row_weight))
        levelled.append(jnp.concatenate([upper[:RADIUS], lower[RADIUS:]], axis=0))
    retreat(blur_planes(parts, col_high, col_low, True), levelled, start, later, factor, deepest, out)


def join_kernel(at_start, before, first_mid, first_edge, factor_mid, factor_edge, pieces):
    rows, cols = before.shape
    groups = rows // RADIUS
    lead = at_start[0] == 1
    wide = cols // 4
    for group in range(groups):
        at = pl.ds(group * RADIUS, RADIUS)
        if group in (0, groups - 1):
            edge = pl.ds(0 if group == 0 else RADIUS, RADIUS)
            first, factor = first_edge[edge], factor_edge[edge]
        else:
            inner = pl.ds((group - 1) * RADIUS, RADIUS)
            first, factor = first_mid[inner], factor_mid[inner]
        total = jnp.where(lead, 1.0, jnp.clip(before[at] / first, LOW, HIGH)) / factor
        for part in range(4):
            pieces[group * 4 + part] = total[:, part * wide:(part + 1) * wide]


def scan_kernel(pieces, out):
    running = jnp.ones(pieces.shape[1:], jnp.float32)
    for slab in range(pieces.shape[0]):
        running = running * pieces[slab]
        out[slab] = running


def final_kernel(shallow, deep, edge, pieces, out, factor):
    step, rows, cols = out.shape
    wide = cols // 4
    at_deep = pl.program_id(0) >= pl.num_programs(0) // 2

    @pl.when(pl.program_id(0) == 0)
    def _():
        for group in range(rows // RADIUS):
            for part in range(4):
                factor[pl.ds(group * RADIUS, RADIUS), pl.ds(part * wide, wide)] = pieces[group * 4 + part]

    inner = pl.ds(RADIUS, rows - 2 * RADIUS)
    for plane in range(step):
        out[plane, :RADIUS] = edge[plane, :RADIUS] * factor[:RADIUS]
        out[plane, rows - RADIUS:] = edge[plane, RADIUS:] * factor[rows - RADIUS:]

    @pl.when(at_deep)
    def _():
        for plane in range(step):
            out[plane, inner] = deep[plane] * factor[inner]

    @pl.when(jnp.logical_not(at_deep))
    def _():
        for plane in range(step):
            out[plane, inner] = shallow[plane] * factor[inner]


def shape(*dims):
    return jax.ShapeDtypeStruct(dims, jnp.float32)


def whole(*dims):
    return pl.BlockSpec(dims, lambda i: (0,) * len(dims))


def params(mib):
    return pltpu.CompilerParams(vmem_limit_bytes=mib * MIB)


def cost(flops, moved):
    return pl.CostEstimate(flops=int(flops), bytes_accessed=int(moved), transcendentals=0)


def deep_call(volume, flat, row_weight, col_high, col_low):
    planes, rows, cols = volume.shape
    inner, half = rows - 2 * RADIUS, planes // 2
    steps = half // STEP
    return pl.pallas_call(
        deep_kernel,
        grid=(steps,),
        in_specs=[
            pl.BlockSpec((STEP, rows, cols), lambda i: (2 * steps - 1 - i, 0, 0)),
            whole(rows, cols),
            whole(*row_weight.shape),
            whole(cols, cols),
            whole(cols, cols),
        ],
        out_specs=[pl.BlockSpec((STEP, inner, cols), lambda i: (steps - 1 - i, 0, 0))] + [whole(inner, cols)] * 3,
        out_shape=[shape(half, inner, cols)] + [shape(inner, cols)] * 3,
        scratch_shapes=[pltpu.VMEM((rows, cols), jnp.float32)],
        compiler_params=params(GRANT),
        cost_estimate=cost(6e9, 6e6),
    )(volume, flat, row_weight, col_high, col_low)


def shallow_call(volume, flat, row_weight, col_high, col_low, later, factor):
    planes, rows, cols = volume.shape
    inner, half = rows - 2 * RADIUS, planes // 2
    steps = half // STEP
    return pl.pallas_call(
        shallow_kernel,
        grid=(steps,),
        in_specs=[
            pl.BlockSpec((STEP, rows, cols), lambda i: (steps - 1 - i, 0, 0)),
            whole(rows, cols),
            whole(*row_weight.shape),
            whole(cols, cols),
            whole(cols, cols),
            whole(inner, cols),
            whole(inner, cols),
        ],
        out_specs=[pl.BlockSpec((STEP, inner, cols), lambda i: (steps - 1 - i, 0, 0))] + [whole(inner, cols)] * 2,
        out_shape=[shape(half, inner, cols)] + [shape(inner, cols)] * 2,
        scratch_shapes=[pltpu.VMEM((rows, cols), jnp.float32)],
        compiler_params=params(GRANT),
        cost_estimate=cost(6e9, 6e6),
    )(volume, flat, row_weight, col_high, col_low, later, factor)


def edge_call(volume, above, below, flat, row_weight, col_high, col_low):
    planes, rows, cols = volume.shape
    near = 2 * RADIUS
    ends = rows // near - 1
    steps = planes // EDGE_STEP
    halo = pl.BlockSpec((EDGE_STEP, RADIUS, cols), lambda i: (steps - 1 - i, 0, 0))
    return pl.pallas_call(
        edge_kernel,
        grid=(steps,),
        in_specs=[
            pl.BlockSpec((EDGE_STEP, near, cols), lambda i: (steps - 1 - i, 0, 0)),
            pl.BlockSpec((EDGE_STEP, near, cols), lambda i: (steps - 1 - i, ends, 0)),
            halo,
            halo,
            pl.BlockSpec((near, cols), lambda i: (0, 0)),
            pl.BlockSpec((near, cols), lambda i: (ends, 0)),
            whole(*row_weight.shape),
            whole(cols, cols),
            whole(cols, cols),
        ],
        out_specs=[pl.BlockSpec((EDGE_STEP, near, cols), lambda i: (steps - 1 - i, 0, 0))] + [whole(near, cols)] * 3,
        out_shape=[shape(planes, near, cols)] + [shape(near, cols)] * 3,
        scratch_shapes=[pltpu.VMEM((2 * near, cols), jnp.float32)],
        compiler_params=params(GRANT),
        cost_estimate=cost(4e9, 8e6),
    )(volume, volume, above, below, flat, flat, row_weight, col_high, col_low)


def final_call(shallow, deep, edge, pieces):
    half, inner, cols = deep.shape
    rows = inner + 2 * RADIUS
    group = 2
    steps = half // group
    return pl.pallas_call(
        final_kernel,
        grid=(2 * steps,),
        in_specs=[
            pl.BlockSpec((group, inner, cols), lambda i: (jnp.minimum(i, steps - 1), 0, 0)),
            pl.BlockSpec((group, inner, cols), lambda i: (jnp.maximum(i - steps, 0), 0, 0)),
            pl.BlockSpec((group, 2 * RADIUS, cols), lambda i: (i, 0, 0)),
            whole(*pieces.shape),
        ],
        out_specs=pl.BlockSpec((group, rows, cols), lambda i: (i, 0, 0)),
        out_shape=shape(2 * half, rows, cols),
        scratch_shapes=[pltpu.VMEM((rows, cols), jnp.float32)],
        compiler_params=params(GRANT),
    )(shallow, deep, edge, pieces)


def make_weights(rows, cols, tile_index, extent):
    base = tile_index * rows
    column = blur_weights(lax.iota(jnp.int32, cols), lax.iota(jnp.int32, cols), cols, RADIUS).T
    col_high, col_low = split_weights(column)
    ext = base - RADIUS + lax.iota(jnp.int32, rows + 2 * RADIUS)
    every = blur_weights(base + lax.iota(jnp.int32, rows), ext, extent, RADIUS)
    mid_high, mid_low = split_weights(every[RADIUS:rows - RADIUS, RADIUS:rows + RADIUS])
    near = 3 * RADIUS
    gap = jnp.zeros((RADIUS, near), jnp.float32)
    edge = jnp.concatenate(
        [
            jnp.concatenate([every[:RADIUS, :near], gap], axis=1),
            jnp.concatenate([gap, every[rows - RADIUS:, rows + 2 * RADIUS - near:]], axis=1),
        ],
        axis=0,
    )
    edge_high, edge_low = split_weights(edge)
    return (
        jnp.concatenate([mid_high, mid_low], axis=0),
        jnp.concatenate([edge_high, edge_low], axis=0),
        col_high,
        col_low,
    )


def body(volume, flat_field):
    planes, rows, cols = volume.shape
    tile_index = lax.axis_index("tile")
    depth_index = lax.axis_index("depth")
    tiles, slabs = lax.axis_size("tile"), lax.axis_size("depth")
    top = volume[:, :RADIUS] / flat_field[:RADIUS]
    bottom = volume[:, rows - RADIUS:] / flat_field[rows - RADIUS:]
    above = lax.ppermute(bottom, "tile", [(i, i + 1) for i in range(tiles - 1)])
    below = lax.ppermute(top, "tile", [(i + 1, i) for i in range(tiles - 1)])
    mid_weight, edge_weight, col_high, col_low = make_weights(rows, cols, tile_index, rows * tiles)
    deep, deepest_mid, later, factor = deep_call(volume, flat_field, mid_weight, col_high, col_low)
    edge, deepest_edge, first_edge, factor_edge = edge_call(volume, above, below, flat_field, edge_weight, col_high, col_low)
    deepest = jnp.concatenate([deepest_edge[:RADIUS], deepest_mid, deepest_edge[RADIUS:]], axis=0)
    before = lax.ppermute(deepest, "depth", [(i, i + 1) for i in range(slabs - 1)])
    shallow, first_mid, factor_mid = shallow_call(volume, flat_field, mid_weight, col_high, col_low, later, factor)
    at_start = (depth_index == 0).astype(jnp.int32).reshape(1)
    vmem = pl.BlockSpec(memory_space=pltpu.VMEM)
    traded = shape(slabs, RADIUS, cols // 4)
    pieces = pl.pallas_call(
        join_kernel,
        in_specs=[pl.BlockSpec(memory_space=pltpu.SMEM)] + [vmem] * 5,
        out_specs=vmem,
        out_shape=traded,
        compiler_params=params(GRANT),
    )(at_start, before, first_mid, first_edge, factor_mid, factor_edge)
    mine = lax.all_to_all(pieces, "depth", 0, 0, tiled=True)
    reached = pl.pallas_call(
        scan_kernel, in_specs=[vmem], out_specs=vmem, out_shape=traded, compiler_params=params(GRANT)
    )(mine)
    back = lax.all_to_all(reached, "depth", 0, 0, tiled=True)
    return final_call(shallow, deep, edge, back)


def solution(mesh):
    return jax.shard_map(
        body,
        mesh=mesh,
        in_specs=(P("depth", "tile", None), P("tile", None)),
        out_specs=P("depth", "tile", None),
        check_vma=False,
    )
```

time: 97.3 us -> 82.8 us (0.85)
  the two profiles are of different devices: /device:TPU:8 before, /device:TPU:32 now
where the time goes in v3:
time: 82.8 us; the launch traced here: 82.4 us
  blocking collectives  43.4 us (52%)
  Pallas kernels  15.1 us (18%)
  waiting for transfers between devices  8.7 us (11%)
  starting transfers between devices  7.78 us (9%)
  local copies, waits for them, and re-layouts  4.69 us (6%)
  other arithmetic  2.53 us (3%)
    all_to_all x1, blocking collectives, body(): mine = lax.all_to_all(pieces, 'depth', 0, 0, tiled=True)  24.7 us
    all_to_all x1, blocking collectives, body(): back = lax.all_to_all(reached, 'depth', 0, 0, tiled=True)  18.7 us
    ppermute x1, waiting for transfers between devices, body(): lax.ppermute(deepest, 'depth', [(i, i + 1) for i in range(slabs - 1)])  8.69 us
    pallas_call x1, Pallas kernels, final_call(): pl.pallas_call(final_kernel, grid=(2 * steps,), in_specs=[pl.BlockSpec((g...  4.08 us
    pallas_call x1, Pallas kernels, deep_call(): pl.pallas_call(deep_kernel, grid=(steps,), in_specs=[pl.BlockSpec((STEP,...  3.96 us
    unnamed x4, local copies, waits for them, and re-layouts  3.78 us
    pallas_call x1, Pallas kernels, shallow_call(): pl.pallas_call(shallow_kernel, grid=(steps,), in_specs=[pl.BlockSpec((STE...  3.63 us
    ppermute x1, starting transfers between devices, body(): lax.ppermute(deepest, 'depth', [(i, i + 1) for i in range(slabs - 1)])  3.41 us
  transfers between devices with their start and end apart: 3, of which 1 were waited for; matrix products, arithmetic and copies ran while one was open for 1% of the time, Pallas kernels for 9%

profile of v3, /device:TPU:32, one launch (start us, length us, event | category | flops | bytes accessed | tf_op | source)
XLA Modules:
  0.0 82.4 jit_solution(14005452792290189237)
XLA Ops:
  0.0 0.8 %fusion.23 = (f32[24,512]{1,0:T(8,128)S(1)}, f32[24,512]{1,0:T(8,128)S(1)}) fusion(f32[192,512]{1,0:T(8,128)} %flat_bottom.1), kind=kLoop, calls=%fused_computation.53 | loop fusion | bytes 196608 | tf_op jit(solution)/shard_map/slice | solution.py:338
  0.8 1.6 %slice_divide_fusion = (f32[16,24,512]{2,1,0:T(8,128)S(1)}, f32[16,24,512]{2,1,0:T(8,128)S(1)}) fusion(f32[16,192,512]{2,1,0:T(8,128)} %bottom.1, f32[24,512]{1,0:T(8,128)S(1)} %get-tuple-element.29, f32[24,512]{1,0:T(8,128)S(1)} %get-tuple-element.30), kind=kLoop, calls=%fused_computation.11 | loop fusion | flops 393216 | bytes 3244032 | tf_op jit(solution)/shard_map/div | solution.py:338
  2.5 1.3 %collective-permute-start.1 = (f32[16,24,512]{2,1,0:T(8,128)S(1)}, f32[16,24,512]{2,1,0:T(8,128)S(1)}, u32[]{:S(2)}, u32[]{:S(2)}) collective-permute-start(f32[16,24,512]{2,1,0:T(8,128)S(1)} %get-tuple-element.27), channel_id=1, source_target_pairs={{32,0},{64,32},{96,64},{128,96},{160,128},{192,160},{224,192},{33,... | collective-permute-start | bytes 2359304 | tf_op jit(solution)/shard_map/ppermute | solution.py:341
  3.8 3.1 %collective-permute-start = (f32[16,24,512]{2,1,0:T(8,128)S(1)}, f32[16,24,512]{2,1,0:T(8,128)S(1)}, u32[]{:S(2)}, u32[]{:S(2)}) collective-permute-start(f32[16,24,512]{2,1,0:T(8,128)S(1)} %get-tuple-element.28), channel_id=1, source_target_pairs={{0,32},{32,64},{64,96},{96,128},{128,160},{160,192},{192,224},{1,3... | collective-permute-start | bytes 2359304 | tf_op jit(solution)/shard_map/ppermute | solution.py:340
  6.9 0.1 select_reduce_fusion
  7.0 0.1 select_reduce_fusion.1
  7.1 0.2 fusion.10
  7.3 0.1 fusion.24
  7.4 0.1 reduce-precision_convert_fusion.1
  7.6 0.1 reduce-precision_convert_fusion.2
  7.6 0.2 fusion
  7.9 0.0 copy-start
  7.9 2.8 %copy-done = f32[16,192,512]{2,1,0:T(8,128)S(1)} copy-done((f32[16,192,512]{2,1,0:T(8,128)S(1)}, f32[16,192,512]{2,1,0:T(8,128)}, u32[]{:S(2)}) %copy-start) | copy-done | bytes 6291480
  10.7 0.0 copy-start.1
  10.7 1.0 %copy-done.1 = f32[192,512]{1,0:T(8,128)S(1)} copy-done((f32[192,512]{1,0:T(8,128)S(1)}, f32[192,512]{1,0:T(8,128)}, u32[]{:S(2)}) %copy-start.1) | copy-done | bytes 393240
  11.7 4.0 %shard_map.28 = (f32[8,144,512]{2,1,0:T(8,128)S(1)}, f32[144,512]{1,0:T(8,128)S(1)}, f32[144,512]{1,0:T(8,128)S(1)}, f32[144,512]{1,0:T(8,128)S(1)}) custom-call(f32[16,192,512]{2,1,0:T(8,128)S(1)} %copy-done, f32[192,512]{1,0:T(8,128)S(1)} %copy-done.1, bf16[288,192]{1,0:T(8,128)(2,1)S(1)} %pad_maximum_fusion.1.row_weight, ...), custom_call_target="tpu_custom_call" | custom-call | flops 6000000000 | bytes 6000000 | tf_op jit(solution)/shard_map/pallas_call | solution.py:217
  15.7 0.0 collective-permute-done.1.below
  15.7 0.0 collective-permute-done.above
  15.7 3.3 %shard_map.30 = (f32[16,48,512]{2,1,0:T(8,128)S(1)}, f32[48,512]{1,0:T(8,128)S(1)}, f32[48,512]{1,0:T(8,128)S(1)}, f32[48,512]{1,0:T(8,128)S(1)}) custom-call(f32[16,192,512]{2,1,0:T(8,128)S(1)} %copy-done, f32[16,192,512]{2,1,0:T(8,128)S(1)} %copy-done, f32[16,24,512]{2,1,0:T(8,128)S(1)} %collective-permute-done.above, ...), custom_call_target="tpu_custom_call" | custom-call | flops 4000000000 | bytes 8000000 | tf_op jit(solution)/shard_map/pallas_call | solution.py:265
  19.0 3.4 %collective-permute-start.2 = (f32[192,512]{1,0:T(8,128)S(1)}, f32[192,512]{1,0:T(8,128)S(1)}, u32[]{:S(2)}, u32[]{:S(2)}) collective-permute-start(f32[192,512]{1,0:T(8,128)S(1)} %pad_maximum_fusion), channel_id=1, source_target_pairs={{0,1},{1,2},{2,3},{3,4},{4,5},{5,6},{6,7},{7,8},{8,9},{9,10},{10,1... | collective-permute-start | bytes 1179656 | tf_op jit(solution)/shard_map/ppermute | solution.py:346
  22.5 3.6 %shard_map.29 = (f32[8,144,512]{2,1,0:T(8,128)S(1)}, f32[144,512]{1,0:T(8,128)S(1)}, f32[144,512]{1,0:T(8,128)S(1)}) custom-call(f32[16,192,512]{2,1,0:T(8,128)S(1)} %copy-done, f32[192,512]{1,0:T(8,128)S(1)} %copy-done.1, bf16[288,192]{1,0:T(8,128)(2,1)S(1)} %pad_maximum_fusion.1.row_weight, bf16[512,512]{1,0:T(8,128)(2,1)S(1)} %get-tuple-element.40.col_high, ...), custom_call_target="tpu_custom_call" | custom-call | flops 6000000000 | bytes 6000000 | tf_op jit(solution)/shard_map/pallas_call | solution.py:239
  26.1 8.7 %collective-permute-done.2.before = f32[192,512]{1,0:T(8,128)S(1)} collective-permute-done((f32[192,512]{1,0:T(8,128)S(1)}, f32[192,512]{1,0:T(8,128)S(1)}, u32[]{:S(2)}, u32[]{:S(2)}) %collective-permute-start.2) | collective-permute-done | bytes 393248 | tf_op jit(solution)/shard_map/ppermute | solution.py:346
  34.8 0.1 shard_map.31
  34.9 24.7 %all_to_all.10.pieces = f32[32,24,128]{2,1,0:T(8,128)S(1)} all-to-all(f32[32,24,128]{2,1,0:T(8,128)S(1)} %shard_map.31), channel_id=1, replica_groups=mesh['tile'=8,'depth'=32] {'depth'}, dimensions={0} | all-to-all | bytes 786432 | tf_op jit(solution)/shard_map/all_to_all | solution.py:358
  59.7 18.7 %all_to_all.11.pieces = f32[32,24,128]{2,1,0:T(8,128)S(1)} all-to-all(f32[32,24,128]{2,1,0:T(8,128)S(1)} %shard_map.32), channel_id=1, replica_groups=mesh['tile'=8,'depth'=32] {'depth'}, dimensions={0} | all-to-all | bytes 786432 | tf_op jit(solution)/shard_map/all_to_all | solution.py:362
  78.3 4.1 %shard_map.33 = f32[16,192,512]{2,1,0:T(8,128)} custom-call(f32[8,144,512]{2,1,0:T(8,128)S(1)} %get-tuple-element.18.shallow, f32[8,144,512]{2,1,0:T(8,128)S(1)} %get-tuple-element.19.deep, f32[16,48,512]{2,1,0:T(8,128)S(1)} %get-tuple-element.20.edge, f32[32,24,128]{2,1,0:T(8,128)S(1)} %all_to_all.11.pieces), custom_call_target="tpu_custom_call" | custom-call | tf_op jit(solution)/shard_map/pallas_call | solution.py:292
  (11 shorter events, 0.1 us)
Async XLA Ops:
  2.5 13.2 %collective-permute-start.1 = (f32[16,24,512]{2,1,0:T(8,128)S(1)}, f32[16,24,512]{2,1,0:T(8,128)S(1)}, u32[]{:S(2)}, u32[]{:S(2)}) collective-permute-start(f32[16,24,512]{2,1,0:T(8,128)S(1)} %get-tuple-element.27), channel_id=1, source_target_pairs={{32,0},{64,32},{96,64},{128,96},{160,128},{192,160},{224,192},{33,... | collective-permute-start | bytes 2359304 | tf_op jit(solution)/shard_map/ppermute | solution.py:341
  3.8 11.9 %collective-permute-start = (f32[16,24,512]{2,1,0:T(8,128)S(1)}, f32[16,24,512]{2,1,0:T(8,128)S(1)}, u32[]{:S(2)}, u32[]{:S(2)}) collective-permute-start(f32[16,24,512]{2,1,0:T(8,128)S(1)} %get-tuple-element.28), channel_id=1, source_target_pairs={{0,32},{32,64},{64,96},{96,128},{128,160},{160,192},{192,224},{1,3... | collective-permute-start | bytes 2359304 | tf_op jit(solution)/shard_map/ppermute | solution.py:340
  7.9 2.8 %copy-start = (f32[16,192,512]{2,1,0:T(8,128)S(1)}, f32[16,192,512]{2,1,0:T(8,128)}, u32[]{:S(2)}) copy-start(f32[16,192,512]{2,1,0:T(8,128)} %bottom.1) | copy-start | bytes 18874372
  10.7 1.0 %copy-start.1 = (f32[192,512]{1,0:T(8,128)S(1)}, f32[192,512]{1,0:T(8,128)}, u32[]{:S(2)}) copy-start(f32[192,512]{1,0:T(8,128)} %flat_bottom.1) | copy-start | bytes 1179652
  19.0 15.8 %collective-permute-start.2 = (f32[192,512]{1,0:T(8,128)S(1)}, f32[192,512]{1,0:T(8,128)S(1)}, u32[]{:S(2)}, u32[]{:S(2)}) collective-permute-start(f32[192,512]{1,0:T(8,128)S(1)} %pad_maximum_fusion), channel_id=1, source_target_pairs={{0,1},{1,2},{2,3},{3,4},{4,5},{5,6},{6,7},{7,8},{8,9},{9,10},{10,1... | collective-permute-start | bytes 1179656 | tf_op jit(solution)/shard_map/ppermute | solution.py:346

commit v4 on v3

--- a/solution.py
+++ b/solution.py
@@ -13,34 +13,46 @@
 MIB = 1 << 20
 STEP = 4
 EDGE_STEP = 8
+FINAL_STEP = 2
 GRANT = 20
+LARGE = 60
+STREAM = 48
+HALO_STEPS = 2
 TOGETHER = True
 
 
-def blur_weights(out_index, in_index, extent, radius):
-    spread = radius / 3.0
-    out_index = out_index[:, None]
-    in_index = in_index[None, :]
+def blur_weights(out_index, in_index, extent, axis):
+    spread = RADIUS / 3.0
     distance = (out_index - in_index).astype(jnp.float32)
-    inside = (jnp.abs(out_index - in_index) <= radius) & (in_index >= 0) & (in_index < extent)
+    inside = (jnp.abs(out_index - in_index) <= RADIUS) & (in_index >= 0) & (in_index < extent)
     kernel = jnp.where(inside, jnp.exp(-distance * distance / (2.0 * spread * spread)), 0.0)
-    reach = lax.iota(jnp.int32, 2 * radius + 1)[None, :] - radius
-    target = out_index + reach
-    valid = (target >= 0) & (target < extent)
-    reach_float = reach.astype(jnp.float32)
-    weights = jnp.where(valid, jnp.exp(-reach_float * reach_float / (2.0 * spread * spread)), 0.0)
-    normaliser = jnp.sum(weights, axis=1, keepdims=True)
-    return kernel / normaliser
+    return kernel / jnp.sum(kernel, axis=axis, keepdims=True)
+
+
+def numbered(rows, cols):
+    return lax.broadcasted_iota(jnp.int32, (rows, cols), 0), lax.broadcasted_iota(jnp.int32, (rows, cols), 1)
+
+
+def fill_weights(rows, mid_weight, edge_weight, col_high, col_low):
+    def put(ref, weights):
+        count = weights.shape[0]
+        ref[:count], ref[count:] = halves(weights)
+
+    base = lax.axis_index("tile") * rows
+    extent = lax.axis_size("tile") * rows
+    row, col = numbered(rows - 2 * RADIUS, rows)
+    put(mid_weight, blur_weights(base + RADIUS + row, base + col, extent, 1))
+    row, col = numbered(2 * RADIUS, 6 * RADIUS)
+    row = jnp.where(row < RADIUS, row, row + (rows - 2 * RADIUS))
+    col = jnp.where(col < 3 * RADIUS, col, col + (rows - 4 * RADIUS))
+    put(edge_weight, blur_weights(base + row, base - RADIUS + col, extent, 1))
+    row, col = numbered(*col_high.shape)
+    col_high[...], col_low[...] = halves(blur_weights(col, row, col_high.shape[0], 0))
 
 
 def halves(value):
     high = value.astype(jnp.bfloat16)
     return high, (value - high.astype(jnp.float32)).astype(jnp.bfloat16)
-
-
-def split_weights(weights):
-    high = lax.reduce_precision(weights, 8, 7)
-    return high.astype(jnp.bfloat16), (weights - high).astype(jnp.bfloat16)
 
 
 def mul(left, right):
@@ -96,16 +108,22 @@
     return levelled, parts
 
 
-def deep_kernel(volume, flat, row_weight, col_high, col_low, out, deepest, later, factor, inverse):
+def halo_kernel(upper, lower, flat_top, flat_bottom, top, bottom):
+    top[...] = upper[...] / flat_top[...]
+    bottom[...] = lower[...] / flat_bottom[...]
+
+
+def deep_kernel(volume, flat, out, deepest, later, factor, mid_weight, edge_weight, col_high, col_low, inverse):
     start = pl.program_id(0) == 0
 
     @pl.when(start)
     def _():
+        fill_weights(flat.shape[0], mid_weight, edge_weight, col_high, col_low)
         inverse[...] = 1.0 / flat[...]
         later[...] = jnp.ones_like(later)
         factor[...] = jnp.ones_like(factor)
 
-    levelled, parts = middle_planes(volume, inverse, row_weight)
+    levelled, parts = middle_planes(volume, inverse, mid_weight)
     retreat(blur_planes(parts, col_high, col_low, TOGETHER), levelled, start, later, factor, deepest, out)
 
 
@@ -142,20 +160,18 @@
     retreat(blur_planes(parts, col_high, col_low, True), levelled, start, later, factor, deepest, out)
 
 
-def join_kernel(at_start, before, first_mid, first_edge, factor_mid, factor_edge, pieces):
-    rows, cols = before.shape
-    groups = rows // RADIUS
-    lead = at_start[0] == 1
+def join_kernel(before_mid, before_edge, first_mid, first_edge, factor_mid, factor_edge, pieces):
+    inner, cols = before_mid.shape
+    groups = inner // RADIUS + 2
     wide = cols // 4
     for group in range(groups):
-        at = pl.ds(group * RADIUS, RADIUS)
         if group in (0, groups - 1):
-            edge = pl.ds(0 if group == 0 else RADIUS, RADIUS)
-            first, factor = first_edge[edge], factor_edge[edge]
+            at = pl.ds(0 if group == 0 else RADIUS, RADIUS)
+            before, first, factor = before_edge[at], first_edge[at], factor_edge[at]
         else:
-            inner = pl.ds((group - 1) * RADIUS, RADIUS)
-            first, factor = first_mid[inner], factor_mid[inner]
-        total = jnp.where(lead, 1.0, jnp.clip(before[at] / first, LOW, HIGH)) / factor
+            at = pl.ds((group - 1) * RADIUS, RADIUS)
+            before, first, factor = before_mid[at], first_mid[at], factor_mid[at]
+        total = jnp.where(before > 0.0, jnp.clip(before / first, LOW, HIGH), 1.0) / factor
         for part in range(4):
             pieces[group * 4 + part] = total[:, part * wide:(part + 1) * wide]
 
@@ -210,26 +226,46 @@
     return pl.CostEstimate(flops=int(flops), bytes_accessed=int(moved), transcendentals=0)
 
 
-def deep_call(volume, flat, row_weight, col_high, col_low):
-    planes, rows, cols = volume.shape
-    inner, half = rows - 2 * RADIUS, planes // 2
+def halo_call(volume, flat):
+    planes, rows, cols = volume.shape
+    ends = rows // RADIUS - 1
+    group = planes // HALO_STEPS
+    halo = pl.BlockSpec((group, RADIUS, cols), lambda i: (i, 0, 0))
+    return pl.pallas_call(
+        halo_kernel,
+        grid=(HALO_STEPS,),
+        in_specs=[
+            pl.BlockSpec((group, RADIUS, cols), lambda i: (i, 0, 0)),
+            pl.BlockSpec((group, RADIUS, cols), lambda i: (i, ends, 0)),
+            pl.BlockSpec((RADIUS, cols), lambda i: (0, 0)),
+            pl.BlockSpec((RADIUS, cols), lambda i: (ends, 0)),
+        ],
+        out_specs=[halo, halo],
+        out_shape=[shape(planes, RADIUS, cols)] * 2,
+        compiler_params=params(LARGE),
+        cost_estimate=cost(1e6, 4e6),
+    )(volume, volume, flat, flat)
+
+
+def deep_call(volume, flat):
+    planes, rows, cols = volume.shape
+    inner, near, half = rows - 2 * RADIUS, 2 * RADIUS, planes // 2
     steps = half // STEP
+    weights = [(2 * inner, rows), (2 * near, 3 * near), (cols, cols), (cols, cols)]
     return pl.pallas_call(
         deep_kernel,
         grid=(steps,),
-        in_specs=[
-            pl.BlockSpec((STEP, rows, cols), lambda i: (2 * steps - 1 - i, 0, 0)),
-            whole(rows, cols),
-            whole(*row_weight.shape),
-            whole(cols, cols),
-            whole(cols, cols),
-        ],
-        out_specs=[pl.BlockSpec((STEP, inner, cols), lambda i: (steps - 1 - i, 0, 0))] + [whole(inner, cols)] * 3,
-        out_shape=[shape(half, inner, cols)] + [shape(inner, cols)] * 3,
+        in_specs=[pl.BlockSpec((STEP, rows, cols), lambda i: (2 * steps - 1 - i, 0, 0)), whole(rows, cols)],
+        out_specs=[pl.BlockSpec((STEP, inner, cols), lambda i: (steps - 1 - i, 0, 0))]
+        + [whole(inner, cols)] * 3
+        + [whole(*dims) for dims in weights],
+        out_shape=[shape(half, inner, cols)]
+        + [shape(inner, cols)] * 3
+        + [jax.ShapeDtypeStruct(dims, jnp.bfloat16) for dims in weights],
         scratch_shapes=[pltpu.VMEM((rows, cols), jnp.float32)],
-        compiler_params=params(GRANT),
+        compiler_params=params(STREAM),
         cost_estimate=cost(6e9, 6e6),
-    )(volume, flat, row_weight, col_high, col_low)
+    )(volume, flat)
 
 
 def shallow_call(volume, flat, row_weight, col_high, col_low, later, factor):
@@ -251,7 +287,7 @@
         out_specs=[pl.BlockSpec((STEP, inner, cols), lambda i: (steps - 1 - i, 0, 0))] + [whole(inner, cols)] * 2,
         out_shape=[shape(half, inner, cols)] + [shape(inner, cols)] * 2,
         scratch_shapes=[pltpu.VMEM((rows, cols), jnp.float32)],
-        compiler_params=params(GRANT),
+        compiler_params=params(STREAM),
         cost_estimate=cost(6e9, 6e6),
     )(volume, flat, row_weight, col_high, col_low, later, factor)
 
@@ -279,7 +315,7 @@
         out_specs=[pl.BlockSpec((EDGE_STEP, near, cols), lambda i: (steps - 1 - i, 0, 0))] + [whole(near, cols)] * 3,
         out_shape=[shape(planes, near, cols)] + [shape(near, cols)] * 3,
         scratch_shapes=[pltpu.VMEM((2 * near, cols), jnp.float32)],
-        compiler_params=params(GRANT),
+        compiler_params=params(STREAM),
         cost_estimate=cost(4e9, 8e6),
     )(volume, volume, above, below, flat, flat, row_weight, col_high, col_low)
 
@@ -305,56 +341,23 @@
     )(shallow, deep, edge, pieces)
 
 
-def make_weights(rows, cols, tile_index, extent):
-    base = tile_index * rows
-    column = blur_weights(lax.iota(jnp.int32, cols), lax.iota(jnp.int32, cols), cols, RADIUS).T
-    col_high, col_low = split_weights(column)
-    ext = base - RADIUS + lax.iota(jnp.int32, rows + 2 * RADIUS)
-    every = blur_weights(base + lax.iota(jnp.int32, rows), ext, extent, RADIUS)
-    mid_high, mid_low = split_weights(every[RADIUS:rows - RADIUS, RADIUS:rows + RADIUS])
-    near = 3 * RADIUS
-    gap = jnp.zeros((RADIUS, near), jnp.float32)
-    edge = jnp.concatenate(
-        [
-            jnp.concatenate([every[:RADIUS, :near], gap], axis=1),
-            jnp.concatenate([gap, every[rows - RADIUS:, rows + 2 * RADIUS - near:]], axis=1),
-        ],
-        axis=0,
-    )
-    edge_high, edge_low = split_weights(edge)
-    return (
-        jnp.concatenate([mid_high, mid_low], axis=0),
-        jnp.concatenate([edge_high, edge_low], axis=0),
-        col_high,
-        col_low,
-    )
-
-
 def body(volume, flat_field):
     planes, rows, cols = volume.shape
-    tile_index = lax.axis_index("tile")
-    depth_index = lax.axis_index("depth")
     tiles, slabs = lax.axis_size("tile"), lax.axis_size("depth")
-    top = volume[:, :RADIUS] / flat_field[:RADIUS]
-    bottom = volume[:, rows - RADIUS:] / flat_field[rows - RADIUS:]
+    onward = [(i, i + 1) for i in range(slabs - 1)]
+    top, bottom = halo_call(volume, flat_field)
     above = lax.ppermute(bottom, "tile", [(i, i + 1) for i in range(tiles - 1)])
     below = lax.ppermute(top, "tile", [(i + 1, i) for i in range(tiles - 1)])
-    mid_weight, edge_weight, col_high, col_low = make_weights(rows, cols, tile_index, rows * tiles)
-    deep, deepest_mid, later, factor = deep_call(volume, flat_field, mid_weight, col_high, col_low)
+    deep, deepest, later, factor, mid_weight, edge_weight, col_high, col_low = deep_call(volume, flat_field)
+    before_mid = lax.ppermute(deepest, "depth", onward)
     edge, deepest_edge, first_edge, factor_edge = edge_call(volume, above, below, flat_field, edge_weight, col_high, col_low)
-    deepest = jnp.concatenate([deepest_edge[:RADIUS], deepest_mid, deepest_edge[RADIUS:]], axis=0)
-    before = lax.ppermute(deepest, "depth", [(i, i + 1) for i in range(slabs - 1)])
+    before_edge = lax.ppermute(deepest_edge, "depth", onward)
     shallow, first_mid, factor_mid = shallow_call(volume, flat_field, mid_weight, col_high, col_low, later, factor)
-    at_start = (depth_index == 0).astype(jnp.int32).reshape(1)
     vmem = pl.BlockSpec(memory_space=pltpu.VMEM)
     traded = shape(slabs, RADIUS, cols // 4)
     pieces = pl.pallas_call(
-        join_kernel,
-        in_specs=[pl.BlockSpec(memory_space=pltpu.SMEM)] + [vmem] * 5,
-        out_specs=vmem,
-        out_shape=traded,
-        compiler_params=params(GRANT),
-    )(at_start, before, first_mid, first_edge, factor_mid, factor_edge)
+        join_kernel, in_specs=[vmem] * 6, out_specs=vmem, out_shape=traded, compiler_params=params(GRANT)
+    )(before_mid, before_edge, first_mid, first_edge, factor_mid, factor_edge)
     mine = lax.all_to_all(pieces, "depth", 0, 0, tiled=True)
     reached = pl.pallas_call(
         scan_kernel, in_specs=[vmem], out_specs=vmem, out_shape=traded, compiler_params=params(GRANT)

time: 82.8 us -> 82.2 us (level)
  the two profiles are of different devices: /device:TPU:32 before, /device:TPU:8 now
where the time goes in v4:
time: 82.2 us; the launch traced here: 81.9 us
  blocking collectives  47 us (57%)
  Pallas kernels  22 us (27%)
  starting transfers between devices  12.4 us (15%)
    all_to_all x1, blocking collectives, body(): mine = lax.all_to_all(pieces, 'depth', 0, 0, tiled=True)  26.6 us
    all_to_all x1, blocking collectives, body(): back = lax.all_to_all(reached, 'depth', 0, 0, tiled=True)  20.4 us
    pallas_call x1, Pallas kernels, deep_call(): pl.pallas_call(deep_kernel, grid=(steps,), in_specs=[pl.BlockSpec((STEP,...  5.86 us
    pallas_call x1, Pallas kernels, shallow_call(): pl.pallas_call(shallow_kernel, grid=(steps,), in_specs=[pl.BlockSpec((STE...  5.05 us
    pallas_call x1, Pallas kernels, edge_call(): pl.pallas_call(edge_kernel, grid=(steps,), in_specs=[pl.BlockSpec((EDGE_S...  4.43 us
    pallas_call x1, Pallas kernels, final_call(): pl.pallas_call(final_kernel, grid=(2 * steps,), in_specs=[pl.BlockSpec((g...  4.08 us
    ppermute x1, starting transfers between devices, body(): below = lax.ppermute(top, 'tile', [(i + 1, i) for i in range(tiles - 1)])  3.64 us
    ppermute x1, starting transfers between devices, body(): before_mid = lax.ppermute(deepest, 'depth', onward)  3.41 us
  transfers between devices with their start and end apart: 4, of which 1 were waited for; matrix products, arithmetic and copies ran while one was open for 0% of the time, Pallas kernels for 19%

profile of v4, /device:TPU:8, one launch (start us, length us, event | category | flops | bytes accessed | tf_op | source)
XLA Modules:
  0.0 81.9 jit_solution(11858430773864219585)
XLA Ops:
  0.0 0.0 copy-start
  0.0 2.4 %shard_map.30 = (f32[16,24,512]{2,1,0:T(8,128)}, f32[16,24,512]{2,1,0:T(8,128)}) custom-call(f32[16,192,512]{2,1,0:T(8,128)} %bottom.1, f32[16,192,512]{2,1,0:T(8,128)} %bottom.1, f32[192,512]{1,0:T(8,128)} %flat_bottom.3, f32[192,512]{1,0:T(8,128)} %flat_bottom.3), custom_call_target="tpu_custom_call" | custom-call | flops 1000000 | bytes 4000000 | tf_op jit(solution)/shard_map/pallas_call | solution.py:234
  2.4 1.9 %collective-permute-start = (f32[16,24,512]{2,1,0:T(8,128)}, f32[16,24,512]{2,1,0:T(8,128)S(1)}, u32[]{:S(2)}, u32[]{:S(2)}) collective-permute-start(f32[16,24,512]{2,1,0:T(8,128)} %get-tuple-element.29), channel_id=1, source_target_pairs={{0,32},{32,64},{64,96},{96,128},{128,160},{160,192},{192,224},{1,3... | collective-permute-start | bytes 2359304 | tf_op jit(solution)/shard_map/ppermute | solution.py:349
  4.3 3.6 %collective-permute-start.1 = (f32[16,24,512]{2,1,0:T(8,128)}, f32[16,24,512]{2,1,0:T(8,128)S(1)}, u32[]{:S(2)}, u32[]{:S(2)}) collective-permute-start(f32[16,24,512]{2,1,0:T(8,128)} %get-tuple-element.30), channel_id=1, source_target_pairs={{32,0},{64,32},{96,64},{128,96},{160,128},{192,160},{224,192},{33,... | collective-permute-start | bytes 2359304 | tf_op jit(solution)/shard_map/ppermute | solution.py:350
  8.0 0.0 copy-done
  8.0 5.9 %shard_map.28 = (f32[8,144,512]{2,1,0:T(8,128)S(1)}, f32[144,512]{1,0:T(8,128)S(1)}, f32[144,512]{1,0:T(8,128)S(1)}, f32[144,512]{1,0:T(8,128)S(1)}, bf16[288,19...) custom-call(f32[16,192,512]{2,1,0:T(8,128)} %bottom.1, ...), custom_call_target="tpu_custom_call" | custom-call | flops 6000000000 | bytes 6000000 | tf_op jit(solution)/shard_map/pallas_call | solution.py:255
  13.8 3.4 %collective-permute-start.2 = (f32[144,512]{1,0:T(8,128)S(1)}, f32[144,512]{1,0:T(8,128)S(1)}, u32[]{:S(2)}, u32[]{:S(2)}) collective-permute-start(f32[144,512]{1,0:T(8,128)S(1)} %get-tuple-element.33), channel_id=1, source_target_pairs={{0,1},{1,2},{2,3},{3,4},{4,5},{5,6},{6,7},{7,8},{8,9},{9,10},{10,1... | collective-permute-start | bytes 884744 | tf_op jit(solution)/shard_map/ppermute | solution.py:352
  17.3 0.0 collective-permute-done.above
  17.3 0.5 collective-permute-done.1.below
  17.8 4.4 %shard_map.31 = (f32[16,48,512]{2,1,0:T(8,128)S(1)}, f32[48,512]{1,0:T(8,128)S(1)}, f32[48,512]{1,0:T(8,128)S(1)}, f32[48,512]{1,0:T(8,128)S(1)}) custom-call(f32[16,192,512]{2,1,0:T(8,128)} %bottom.1, f32[16,192,512]{2,1,0:T(8,128)} %bottom.1, f32[16,24,512]{2,1,0:T(8,128)S(1)} %collective-permute-done.above, ...), custom_call_target="tpu_custom_call" | custom-call | flops 4000000000 | bytes 8000000 | tf_op jit(solution)/shard_map/pallas_call | solution.py:301
  22.2 3.4 %collective-permute-start.3 = (f32[48,512]{1,0:T(8,128)S(1)}, f32[48,512]{1,0:T(8,128)S(1)}, u32[]{:S(2)}, u32[]{:S(2)}) collective-permute-start(f32[48,512]{1,0:T(8,128)S(1)} %get-tuple-element.34), channel_id=1, source_target_pairs={{0,1},{1,2},{2,3},{3,4},{4,5},{5,6},{6,7},{7,8},{8,9},{9,10},{10,1... | collective-permute-start | bytes 294920 | tf_op jit(solution)/shard_map/ppermute | solution.py:354
  25.6 5.0 %shard_map.29 = (f32[8,144,512]{2,1,0:T(8,128)S(1)}, f32[144,512]{1,0:T(8,128)S(1)}, f32[144,512]{1,0:T(8,128)S(1)}) custom-call(f32[16,192,512]{2,1,0:T(8,128)} %bottom.1, f32[192,512]{1,0:T(8,128)S(1)} %copy-done, bf16[288,192]{1,0:T(8,128)(2,1)S(1)} %get-tuple-element.22.row_weight, bf16[512,512]{1,0:T(8,128)(2,1)S(1)} %get-tuple-element.23.col_high, ...), custom_call_target="tpu_custom_call" | custom-call | flops 6000000000 | bytes 6000000 | tf_op jit(solution)/shard_map/pallas_call | solution.py:275
  30.7 0.0 collective-permute-done.2.before_mid
  30.7 0.0 collective-permute-done.3.before_edge
  30.7 0.1 shard_map.32
  30.8 26.6 %all_to_all.10.pieces = f32[32,24,128]{2,1,0:T(8,128)S(1)} all-to-all(f32[32,24,128]{2,1,0:T(8,128)S(1)} %shard_map.32), channel_id=1, replica_groups=mesh['tile'=8,'depth'=32] {'depth'}, dimensions={0} | all-to-all | bytes 786432 | tf_op jit(solution)/shard_map/all_to_all | solution.py:361
  57.5 20.4 %all_to_all.11.pieces = f32[32,24,128]{2,1,0:T(8,128)S(1)} all-to-all(f32[32,24,128]{2,1,0:T(8,128)S(1)} %shard_map.33), channel_id=1, replica_groups=mesh['tile'=8,'depth'=32] {'depth'}, dimensions={0} | all-to-all | bytes 786432 | tf_op jit(solution)/shard_map/all_to_all | solution.py:365
  77.8 4.1 %shard_map.34 = f32[16,192,512]{2,1,0:T(8,128)} custom-call(f32[8,144,512]{2,1,0:T(8,128)S(1)} %get-tuple-element.27.shallow, f32[8,144,512]{2,1,0:T(8,128)S(1)} %get-tuple-element.28.deep, f32[16,48,512]{2,1,0:T(8,128)S(1)} %get-tuple-element.32.edge, f32[32,24,128]{2,1,0:T(8,128)S(1)} %all_to_all.11.pieces), custom_call_target="tpu_custom_call" | custom-call | tf_op jit(solution)/shard_map/pallas_call | solution.py:328
  (1 shorter events, 0.0 us)
Async XLA Ops:
  0.0 8.0 %copy-start = (f32[192,512]{1,0:T(8,128)S(1)}, f32[192,512]{1,0:T(8,128)}, u32[]{:S(2)}) copy-start(f32[192,512]{1,0:T(8,128)} %flat_bottom.3) | copy-start | bytes 1179652
  2.4 14.9 %collective-permute-start = (f32[16,24,512]{2,1,0:T(8,128)}, f32[16,24,512]{2,1,0:T(8,128)S(1)}, u32[]{:S(2)}, u32[]{:S(2)}) collective-permute-start(f32[16,24,512]{2,1,0:T(8,128)} %get-tuple-element.29), channel_id=1, source_target_pairs={{0,32},{32,64},{64,96},{96,128},{128,160},{160,192},{192,224},{1,3... | collective-permute-start | bytes 2359304 | tf_op jit(solution)/shard_map/ppermute | solution.py:349
  4.3 13.5 %collective-permute-start.1 = (f32[16,24,512]{2,1,0:T(8,128)}, f32[16,24,512]{2,1,0:T(8,128)S(1)}, u32[]{:S(2)}, u32[]{:S(2)}) collective-permute-start(f32[16,24,512]{2,1,0:T(8,128)} %get-tuple-element.30), channel_id=1, source_target_pairs={{32,0},{64,32},{96,64},{128,96},{160,128},{192,160},{224,192},{33,... | collective-permute-start | bytes 2359304 | tf_op jit(solution)/shard_map/ppermute | solution.py:350
  13.8 16.8 %collective-permute-start.2 = (f32[144,512]{1,0:T(8,128)S(1)}, f32[144,512]{1,0:T(8,128)S(1)}, u32[]{:S(2)}, u32[]{:S(2)}) collective-permute-start(f32[144,512]{1,0:T(8,128)S(1)} %get-tuple-element.33), channel_id=1, source_target_pairs={{0,1},{1,2},{2,3},{3,4},{4,5},{5,6},{6,7},{7,8},{8,9},{9,10},{10,1... | collective-permute-start | bytes 884744 | tf_op jit(solution)/shard_map/ppermute | solution.py:352
  22.2 8.5 %collective-permute-start.3 = (f32[48,512]{1,0:T(8,128)S(1)}, f32[48,512]{1,0:T(8,128)S(1)}, u32[]{:S(2)}, u32[]{:S(2)}) collective-permute-start(f32[48,512]{1,0:T(8,128)S(1)} %get-tuple-element.34), channel_id=1, source_target_pairs={{0,1},{1,2},{2,3},{3,4},{4,5},{5,6},{6,7},{7,8},{8,9},{9,10},{10,1... | collective-permute-start | bytes 294920 | tf_op jit(solution)/shard_map/ppermute | solution.py:354

commit v5 on v4

v5 whole, which is shorter than its diff:
```python
import jax
import jax.numpy as jnp
from jax import lax
from jax.experimental import pallas as pl
from jax.experimental.pallas import tpu as pltpu
from jax.sharding import PartitionSpec as P
import math

RADIUS = 24
CLIP_LIMIT = 0.08
LOW = math.exp(-CLIP_LIMIT)
HIGH = math.exp(CLIP_LIMIT)
MIB = 1 << 20
STEP = 4
EDGE_STEP = 8
FINAL_STEP = 2
GRANT = 20
LARGE = 44


def blur_weights(out_index, in_index, extent, axis):
    spread = RADIUS / 3.0
    distance = (out_index - in_index).astype(jnp.float32)
    inside = (jnp.abs(out_index - in_index) <= RADIUS) & (in_index >= 0) & (in_index < extent)
    kernel = jnp.where(inside, jnp.exp(-distance * distance / (2.0 * spread * spread)), 0.0)
    return kernel / jnp.sum(kernel, axis=axis, keepdims=True)


def numbered(rows, cols):
    return lax.broadcasted_iota(jnp.int32, (rows, cols), 0), lax.broadcasted_iota(jnp.int32, (rows, cols), 1)


def fill_weights(rows, mid_weight, edge_weight, col_high, col_low):
    def put(ref, weights):
        count = weights.shape[0]
        ref[:count], ref[count:] = halves(weights)

    base = lax.axis_index("tile") * rows
    extent = lax.axis_size("tile") * rows
    row, col = numbered(rows - 2 * RADIUS, rows)
    put(mid_weight, blur_weights(base + RADIUS + row, base + col, extent, 1))
    row, col = numbered(2 * RADIUS, 6 * RADIUS)
    row = jnp.where(row < RADIUS, row, row + (rows - 2 * RADIUS))
    col = jnp.where(col < 3 * RADIUS, col, col + (rows - 4 * RADIUS))
    put(edge_weight, blur_weights(base + row, base - RADIUS + col, extent, 1))
    row, col = numbered(*col_high.shape)
    col_high[...], col_low[...] = halves(blur_weights(col, row, col_high.shape[0], 0))


def halves(value):
    high = value.astype(jnp.bfloat16)
    return high, (value - high.astype(jnp.float32)).astype(jnp.bfloat16)


def mul(left, right):
    return jnp.dot(left, right, preferred_element_type=jnp.float32)


def row_blur(high, low, weight):
    rows = weight.shape[0] // 2
    both = mul(weight[...], high)
    return both[:rows] + (both[rows:] + mul(weight[:rows], low))


def column_blur(value, weight_high, weight_low):
    high, low = halves(value)
    return mul(high, weight_high) + (mul(high, weight_low) + mul(low, weight_high))


def retreat(blurred, levelled, fresh, later, factor, put):
    after, running = later[...], factor[...]
    for plane in reversed(range(len(blurred))):
        now = blurred[plane]
        inverse = jnp.clip(after / now, LOW, HIGH)
        if plane == len(blurred) - 1 and fresh is not None:
            inverse = jnp.where(fresh, 1.0, inverse)
        running = running * inverse
        put(plane, levelled[plane] * running)
        after = now
    later[...] = after
    factor[...] = running


def blur_planes(parts, col_high, col_low):
    rows = parts[0].shape[0]
    blurred = column_blur(jnp.concatenate(parts, axis=0), col_high[...], col_low[...])
    return [blurred[plane * rows:(plane + 1) * rows] for plane in range(len(parts))]


def level_kernel(volume, flat, levelled, top, bottom, mid_weight, edge_weight, col_high, col_low, inverse, flat_sem, sems):
    planes, rows, _ = levelled.shape
    first = pltpu.make_async_copy(flat, inverse, flat_sem)
    first.start()
    copies = [pltpu.make_async_copy(volume.at[plane], levelled.at[plane], sems.at[plane]) for plane in range(planes)]
    for copy in copies:
        copy.start()
    fill_weights(rows, mid_weight, edge_weight, col_high, col_low)
    first.wait()
    inverse[...] = 1.0 / inverse[...]
    for plane in range(planes):
        copies[plane].wait()
        value = levelled[plane] * inverse[...]
        levelled[plane] = value
        top[plane] = value[:RADIUS]
        bottom[plane] = value[rows - RADIUS:]


def middle_steps(levelled, row_weight, col_high, col_low, out, later, factor, begin, fresh, deepest):
    rows = levelled.shape[1]
    steps = out.shape[0] // STEP

    def one(index, _):
        at = (steps - 1 - index) * STEP
        values, parts = [], []
        for plane in range(STEP):
            value = levelled[begin + at + plane]
            high, low = halves(value)
            parts.append(row_blur(high, low, row_weight))
            values.append(value[RADIUS:rows - RADIUS])
        blurred = blur_planes(parts, col_high, col_low)
        start = index == 0 if fresh else None
        if fresh:

            @pl.when(start)
            def _():
                deepest[...] = blurred[-1]

        def put(plane, value):
            out[at + plane] = value

        retreat(blurred, values, start, later, factor, put)
        return 0

    lax.fori_loop(0, steps, one, 0)


def deep_kernel(levelled, row_weight, col_high, col_low, out, deepest, later, factor):
    later[...] = jnp.ones_like(later)
    factor[...] = jnp.ones_like(factor)
    begin = levelled.shape[0] - out.shape[0]
    middle_steps(levelled, row_weight, col_high, col_low, out, later, factor, begin, True, deepest)


def shallow_kernel(levelled, row_weight, col_high, col_low, later_in, factor_in, out, later, factor):
    later[...] = later_in[...]
    factor[...] = factor_in[...]
    middle_steps(levelled, row_weight, col_high, col_low, out, later, factor, 0, False, None)


def edge_kernel(levelled, above, below, row_weight, col_high, col_low, out, deepest, later, factor):
    near = 2 * RADIUS
    planes, rows, _ = levelled.shape
    later[...] = jnp.ones_like(later)
    factor[...] = jnp.ones_like(factor)
    steps = planes // EDGE_STEP

    def one(index, _):
        at = (steps - 1 - index) * EDGE_STEP
        values, parts = [], []
        for plane in range(EDGE_STEP):
            upper = levelled[at + plane, :near]
            lower = levelled[at + plane, rows - near:]
            value = jnp.concatenate([above[at + plane], upper, lower, below[at + plane]], axis=0)
            high, low = halves(value)
            parts.append(row_blur(high, low, row_weight))
            values.append(jnp.concatenate([upper[:RADIUS], lower[RADIUS:]], axis=0))
        blurred = blur_planes(parts, col_high, col_low)
        start = index == 0

        @pl.when(start)
        def _():
            deepest[...] = blurred[-1]

        def put(plane, value):
            out[at + plane] = value

        retreat(blurred, values, start, later, factor, put)
        return 0

    lax.fori_loop(0, steps, one, 0)


def join_kernel(before_mid, before_edge, first_mid, first_edge, factor_mid, factor_edge, pieces):
    inner, cols = before_mid.shape
    groups = inner // RADIUS + 2
    wide = cols // 4
    for group in range(groups):
        if group in (0, groups - 1):
            at = pl.ds(0 if group == 0 else RADIUS, RADIUS)
            before, first, factor = before_edge[at], first_edge[at], factor_edge[at]
        else:
            at = pl.ds((group - 1) * RADIUS, RADIUS)
            before, first, factor = before_mid[at], first_mid[at], factor_mid[at]
        total = jnp.where(before > 0.0, jnp.clip(before / first, LOW, HIGH), 1.0) / factor
        for part in range(4):
            pieces[group * 4 + part] = total[:, part * wide:(part + 1) * wide]


def scan_kernel(pieces, out):
    running = jnp.ones(pieces.shape[1:], jnp.float32)
    for slab in range(pieces.shape[0]):
        running = running * pieces[slab]
        out[slab] = running


def final_kernel(shallow, deep, edge, pieces, out, factor):
    step, rows, cols = out.shape
    wide = cols // 4
    index = pl.program_id(0)
    begin = index * step
    half = shallow.shape[0]

    @pl.when(index == 0)
    def _():
        for group in range(rows // RADIUS):
            for part in range(4):
                factor[pl.ds(group * RADIUS, RADIUS), pl.ds(part * wide, wide)] = pieces[group * 4 + part]

    inner = pl.ds(RADIUS, rows - 2 * RADIUS)
    for plane in range(step):
        out[plane, :RADIUS] = edge[begin + plane, :RADIUS] * factor[:RADIUS]
        out[plane, rows - RADIUS:] = edge[begin + plane, RADIUS:] * factor[rows - RADIUS:]

    @pl.when(begin < half)
    def _():
        for plane in range(step):
            out[plane, inner] = shallow[begin + plane] * factor[inner]

    @pl.when(begin >= half)
    def _():
        for plane in range(step):
            out[plane, inner] = deep[begin - half + plane] * factor[inner]


def shape(*dims):
    return jax.ShapeDtypeStruct(dims, jnp.float32)


def params(mib):
    return pltpu.CompilerParams(vmem_limit_bytes=mib * MIB)


def cost(flops, moved):
    return pl.CostEstimate(flops=int(flops), bytes_accessed=int(moved), transcendentals=0)


def vmem_call(kernel, inputs, outputs, given):
    vmem = pl.BlockSpec(memory_space=pltpu.VMEM)
    return pl.pallas_call(
        kernel,
        in_specs=[vmem] * inputs,
        out_specs=[vmem] * len(outputs),
        out_shape=outputs,
        compiler_params=params(GRANT),
        cost_estimate=given,
    )


def level_call(volume, flat):
    planes, rows, cols = volume.shape
    inner, near = rows - 2 * RADIUS, 2 * RADIUS
    weights = [(2 * inner, rows), (2 * near, 3 * near), (cols, cols), (cols, cols)]
    outputs = [shape(planes, rows, cols)] + [shape(planes, RADIUS, cols)] * 2
    outputs += [jax.ShapeDtypeStruct(dims, jnp.bfloat16) for dims in weights]
    return pl.pallas_call(
        level_kernel,
        in_specs=[pl.BlockSpec(memory_space=pltpu.HBM)] * 2,
        out_specs=[pl.BlockSpec(memory_space=pltpu.VMEM)] * len(outputs),
        out_shape=outputs,
        scratch_shapes=[
            pltpu.VMEM((rows, cols), jnp.float32),
            pltpu.SemaphoreType.DMA,
            pltpu.SemaphoreType.DMA((planes,)),
        ],
        compiler_params=params(LARGE),
        cost_estimate=cost(1e7, 7e6),
    )(volume, flat)


def final_call(shallow, deep, edge, pieces):
    half, inner, cols = deep.shape
    rows = inner + 2 * RADIUS
    return pl.pallas_call(
        final_kernel,
        grid=(2 * half // FINAL_STEP,),
        in_specs=[pl.BlockSpec(memory_space=pltpu.VMEM)] * 4,
        out_specs=pl.BlockSpec((FINAL_STEP, rows, cols), lambda i: (i, 0, 0)),
        out_shape=shape(2 * half, rows, cols),
        scratch_shapes=[pltpu.VMEM((rows, cols), jnp.float32)],
        compiler_params=params(GRANT),
    )(shallow, deep, edge, pieces)


def body(volume, flat_field):
    planes, rows, cols = volume.shape
    tiles, slabs = lax.axis_size("tile"), lax.axis_size("depth")
    onward = [(i, i + 1) for i in range(slabs - 1)]
    inner, near, half = rows - 2 * RADIUS, 2 * RADIUS, planes // 2
    levelled, top, bottom, mid_weight, edge_weight, col_high, col_low = level_call(volume, flat_field)
    above = lax.ppermute(bottom, "tile", [(i, i + 1) for i in range(tiles - 1)])
    below = lax.ppermute(top, "tile", [(i + 1, i) for i in range(tiles - 1)])
    deep, deepest, later, factor = vmem_call(
        deep_kernel, 4, [shape(half, inner, cols)] + [shape(inner, cols)] * 3, cost(6e9, 6e6)
    )(levelled, mid_weight, col_high, col_low)
    before_mid = lax.ppermute(deepest, "depth", onward)
    edge, deepest_edge, first_edge, factor_edge = vmem_call(
        edge_kernel, 6, [shape(planes, near, cols)] + [shape(near, cols)] * 3, cost(4e9, 8e6)
    )(levelled, above, below, edge_weight, col_high, col_low)
    before_edge = lax.ppermute(deepest_edge, "depth", onward)
    shallow, first_mid, factor_mid = vmem_call(
        shallow_kernel, 6, [shape(half, inner, cols)] + [shape(inner, cols)] * 2, cost(6e9, 6e6)
    )(levelled, mid_weight, col_high, col_low, later, factor)
    traded = shape(slabs, RADIUS, cols // 4)
    (pieces,) = vmem_call(join_kernel, 6, [traded], cost(1e6, 2e6))(
        before_mid, before_edge, first_mid, first_edge, factor_mid, factor_edge
    )
    mine = lax.all_to_all(pieces, "depth", 0, 0, tiled=True)
    (reached,) = vmem_call(scan_kernel, 1, [traded], cost(1e6, 1e6))(mine)
    back = lax.all_to_all(reached, "depth", 0, 0, tiled=True)
    return final_call(shallow, deep, edge, back)


def solution(mesh):
    return jax.shard_map(
        body,
        mesh=mesh,
        in_specs=(P("depth", "tile", None), P("tile", None)),
        out_specs=P("depth", "tile", None),
        check_vma=False,
    )
```

time: 82.2 us -> 80.9 us (0.984)
  Pallas kernels: 22 us -> 17.6 us
  waiting for transfers between devices: 0.5 us -> 2.27 us
  local copies, waits for them, and re-layouts: 0.01 us -> 1 us
    pallas_call x7, Pallas kernels: 22 us -> 17.6 us  [the longest x1 4.09 us: final_call(): pl.pallas_call(final_kernel, grid=(2 * half // FINAL_STEP,), in_specs=[pl...]
    ppermute x1, waiting for transfers between devices: 0.49 us -> 1.76 us  [body(): below = lax.ppermute(top, 'tile', [(i + 1, i) for i in range(tiles - 1)])]
    all_to_all x1, blocking collectives: 26.6 us -> 27.7 us  [body(): mine = lax.all_to_all(pieces, 'depth', 0, 0, tiled=True)]
    unnamed x2, local copies, waits for them, and re-layouts: 0.01 us -> 1 us
  transfers between devices with their start and end apart: 4 -> 4, of which waited for: 1 -> 2; matrix products, arithmetic and copies ran while one was open for 0% -> 0% of each run, Pallas kernels for 19% -> 12%
where the time goes in v5:
time: 80.9 us; the launch traced here: 80.6 us
  blocking collectives  47.3 us (58%)
  Pallas kernels  17.6 us (22%)
  starting transfers between devices  12.4 us (15%)
  waiting for transfers between devices  2.27 us (3%)
  local copies, waits for them, and re-layouts  1 us (1%)
    all_to_all x1, blocking collectives, body(): mine = lax.all_to_all(pieces, 'depth', 0, 0, tiled=True)  27.7 us
    all_to_all x1, blocking collectives, body(): back = lax.all_to_all(reached, 'depth', 0, 0, tiled=True)  19.6 us
    pallas_call x1, Pallas kernels, final_call(): pl.pallas_call(final_kernel, grid=(2 * half // FINAL_STEP,), in_specs=[pl...  4.09 us
    pallas_call x1, Pallas kernels, body(): vmem_call(deep_kernel, 4, [shape(half, inner, cols)] + [shape(inner, cols...  3.8 us
    ppermute x1, starting transfers between devices, body(): below = lax.ppermute(top, 'tile', [(i + 1, i) for i in range(tiles - 1)])  3.64 us
    ppermute x1, starting transfers between devices, body(): before_mid = lax.ppermute(deepest, 'depth', onward)  3.41 us
    pallas_call x1, Pallas kernels, body(): vmem_call(shallow_kernel, 6, [shape(half, inner, cols)] + [shape(inner, c...  3.41 us
    ppermute x1, starting transfers between devices, body(): before_edge = lax.ppermute(deepest_edge, 'depth', onward)  3.4 us
  transfers between devices with their start and end apart: 4, of which 2 were waited for; matrix products, arithmetic and copies ran while one was open for 0% of the time, Pallas kernels for 12%

profile of v5, /device:TPU:8, one launch (start us, length us, event | category | flops | bytes accessed | tf_op | source)
XLA Modules:
  0.0 80.6 jit_solution(8558812505955125829)
XLA Ops:
  0.0 0.0 copy-start
  0.0 1.0 %copy-done = f32[192,512]{1,0:T(8,128)S(1)} copy-done((f32[192,512]{1,0:T(8,128)S(1)}, f32[192,512]{1,0:T(8,128)}, u32[]{:S(2)}) %copy-start) | copy-done | bytes 393240
  1.0 3.3 %shard_map.28 = (f32[16,192,512]{2,1,0:T(8,128)S(1)}, f32[16,24,512]{2,1,0:T(8,128)S(1)}, f32[16,24,512]{2,1,0:T(8,128)S(1)}, bf16[288,192]{1,0:T(8,128)(2,1)S(1...) custom-call(f32[16,192,512]{2,1,0:T(8,128)} %volume.1, ...), custom_call_target="tpu_custom_call" | custom-call | flops 10000000 | bytes 7000000 | tf_op jit(solution)/shard_map/pallas_call | solution.py:265
  4.3 1.9 %collective-permute-start = (f32[16,24,512]{2,1,0:T(8,128)S(1)}, f32[16,24,512]{2,1,0:T(8,128)S(1)}, u32[]{:S(2)}, u32[]{:S(2)}) collective-permute-start(f32[16,24,512]{2,1,0:T(8,128)S(1)} %get-tuple-element.31), channel_id=1, source_target_pairs={{0,32},{32,64},{64,96},{96,128},{128,160},{160,192},{192,224},{1,3... | collective-permute-start | bytes 2359304 | tf_op jit(solution)/shard_map/ppermute | solution.py:300
  6.3 3.6 %collective-permute-start.1 = (f32[16,24,512]{2,1,0:T(8,128)S(1)}, f32[16,24,512]{2,1,0:T(8,128)S(1)}, u32[]{:S(2)}, u32[]{:S(2)}) collective-permute-start(f32[16,24,512]{2,1,0:T(8,128)S(1)} %get-tuple-element.32), channel_id=1, source_target_pairs={{32,0},{64,32},{96,64},{128,96},{160,128},{192,160},{224,192},{33,... | collective-permute-start | bytes 2359304 | tf_op jit(solution)/shard_map/ppermute | solution.py:301
  9.9 3.8 %shard_map.29 = (f32[8,144,512]{2,1,0:T(8,128)S(1)}, f32[144,512]{1,0:T(8,128)S(1)}, f32[144,512]{1,0:T(8,128)S(1)}, f32[144,512]{1,0:T(8,128)S(1)}) custom-call(f32[16,192,512]{2,1,0:T(8,128)S(1)} %get-tuple-element.23.levelled, bf16[288,192]{1,0:T(8,128)(2,1)S(1)} %get-tuple-element.24.row_weight, bf16[512,512]{1,0:T(8,128)(2,1)S(1)} %get-tuple-element.25.col_high, ...), custom_call_target="tpu_custom_call" | custom-call | flops 6000000000 | bytes 6000000 | tf_op jit(solution)/shard_map/pallas_call | solution.py:302
  13.7 3.4 %collective-permute-start.2 = (f32[144,512]{1,0:T(8,128)S(1)}, f32[144,512]{1,0:T(8,128)S(1)}, u32[]{:S(2)}, u32[]{:S(2)}) collective-permute-start(f32[144,512]{1,0:T(8,128)S(1)} %get-tuple-element.35), channel_id=1, source_target_pairs={{0,1},{1,2},{2,3},{3,4},{4,5},{5,6},{6,7},{7,8},{8,9},{9,10},{10,1... | collective-permute-start | bytes 884744 | tf_op jit(solution)/shard_map/ppermute | solution.py:305
  17.1 0.5 collective-permute-done.above
  17.6 1.8 %collective-permute-done.1.below = f32[16,24,512]{2,1,0:T(8,128)S(1)} collective-permute-done((f32[16,24,512]{2,1,0:T(8,128)S(1)}, f32[16,24,512]{2,1,0:T(8,128)S(1)}, u32[]{:S(2)}, u32[]{:S(2)}) %collective-permute-start.1) | collective-permute-done | bytes 786464 | tf_op jit(solution)/shard_map/ppermute | solution.py:301
  19.4 2.9 %shard_map.31 = (f32[16,48,512]{2,1,0:T(8,128)S(1)}, f32[48,512]{1,0:T(8,128)S(1)}, f32[48,512]{1,0:T(8,128)S(1)}, f32[48,512]{1,0:T(8,128)S(1)}) custom-call(f32[16,192,512]{2,1,0:T(8,128)S(1)} %get-tuple-element.23.levelled, f32[16,24,512]{2,1,0:T(8,128)S(1)} %collective-permute-done.above, f32[16,24,512]{2,1,0:T(8,128)S(1)} %collective-permute-done.1.below, ...), custom_call_target="tpu_custom_call" | custom-call | flops 4000000000 | bytes 8000000 | tf_op jit(solution)/shard_map/pallas_call | solution.py:306
  22.3 3.4 %collective-permute-start.3 = (f32[48,512]{1,0:T(8,128)S(1)}, f32[48,512]{1,0:T(8,128)S(1)}, u32[]{:S(2)}, u32[]{:S(2)}) collective-permute-start(f32[48,512]{1,0:T(8,128)S(1)} %get-tuple-element.36), channel_id=1, source_target_pairs={{0,1},{1,2},{2,3},{3,4},{4,5},{5,6},{6,7},{7,8},{8,9},{9,10},{10,1... | collective-permute-start | bytes 294920 | tf_op jit(solution)/shard_map/ppermute | solution.py:309
  25.7 3.4 %shard_map.30 = (f32[8,144,512]{2,1,0:T(8,128)S(1)}, f32[144,512]{1,0:T(8,128)S(1)}, f32[144,512]{1,0:T(8,128)S(1)}) custom-call(f32[16,192,512]{2,1,0:T(8,128)S(1)} %get-tuple-element.23.levelled, bf16[288,192]{1,0:T(8,128)(2,1)S(1)} %get-tuple-element.24.row_weight, bf16[512,512]{1,0:T(8,128)(2,1)S(1)} %get-tuple-element.25.col_high, ...), custom_call_target="tpu_custom_call" | custom-call | flops 6000000000 | bytes 6000000 | tf_op jit(solution)/shard_map/pallas_call | solution.py:310
  29.1 0.0 collective-permute-done.2.before_mid
  29.1 0.0 collective-permute-done.3.before_edge
  29.1 0.1 shard_map.32
  29.3 27.7 %all_to_all.10.pieces = f32[32,24,128]{2,1,0:T(8,128)S(1)} all-to-all(f32[32,24,128]{2,1,0:T(8,128)S(1)} %shard_map.32), channel_id=1, replica_groups=mesh['tile'=8,'depth'=32] {'depth'}, dimensions={0} | all-to-all | bytes 786432 | tf_op jit(solution)/shard_map/all_to_all | solution.py:317
  57.0 19.6 %all_to_all.11.pieces = f32[32,24,128]{2,1,0:T(8,128)S(1)} all-to-all(f32[32,24,128]{2,1,0:T(8,128)S(1)} %shard_map.33), channel_id=1, replica_groups=mesh['tile'=8,'depth'=32] {'depth'}, dimensions={0} | all-to-all | bytes 786432 | tf_op jit(solution)/shard_map/all_to_all | solution.py:319
  76.6 4.1 %shard_map.34 = f32[16,192,512]{2,1,0:T(8,128)} custom-call(f32[8,144,512]{2,1,0:T(8,128)S(1)} %get-tuple-element.29.shallow, f32[8,144,512]{2,1,0:T(8,128)S(1)} %get-tuple-element.30.deep, f32[16,48,512]{2,1,0:T(8,128)S(1)} %get-tuple-element.34.edge, f32[32,24,128]{2,1,0:T(8,128)S(1)} %all_to_all.11.pieces), custom_call_target="tpu_custom_call" | custom-call | tf_op jit(solution)/shard_map/pallas_call | solution.py:283
  (1 shorter events, 0.0 us)
Async XLA Ops:
  0.0 1.0 %copy-start = (f32[192,512]{1,0:T(8,128)S(1)}, f32[192,512]{1,0:T(8,128)}, u32[]{:S(2)}) copy-start(f32[192,512]{1,0:T(8,128)} %flat.1) | copy-start | bytes 1179652
  4.3 13.3 %collective-permute-start = (f32[16,24,512]{2,1,0:T(8,128)S(1)}, f32[16,24,512]{2,1,0:T(8,128)S(1)}, u32[]{:S(2)}, u32[]{:S(2)}) collective-permute-start(f32[16,24,512]{2,1,0:T(8,128)S(1)} %get-tuple-element.31), channel_id=1, source_target_pairs={{0,32},{32,64},{64,96},{96,128},{128,160},{160,192},{192,224},{1,3... | collective-permute-start | bytes 2359304 | tf_op jit(solution)/shard_map/ppermute | solution.py:300
  6.3 13.1 %collective-permute-start.1 = (f32[16,24,512]{2,1,0:T(8,128)S(1)}, f32[16,24,512]{2,1,0:T(8,128)S(1)}, u32[]{:S(2)}, u32[]{:S(2)}) collective-permute-start(f32[16,24,512]{2,1,0:T(8,128)S(1)} %get-tuple-element.32), channel_id=1, source_target_pairs={{32,0},{64,32},{96,64},{128,96},{160,128},{192,160},{224,192},{33,... | collective-permute-start | bytes 2359304 | tf_op jit(solution)/shard_map/ppermute | solution.py:301
  13.7 15.4 %collective-permute-start.2 = (f32[144,512]{1,0:T(8,128)S(1)}, f32[144,512]{1,0:T(8,128)S(1)}, u32[]{:S(2)}, u32[]{:S(2)}) collective-permute-start(f32[144,512]{1,0:T(8,128)S(1)} %get-tuple-element.35), channel_id=1, source_target_pairs={{0,1},{1,2},{2,3},{3,4},{4,5},{5,6},{6,7},{7,8},{8,9},{9,10},{10,1... | collective-permute-start | bytes 884744 | tf_op jit(solution)/shard_map/ppermute | solution.py:305
  22.3 6.8 %collective-permute-start.3 = (f32[48,512]{1,0:T(8,128)S(1)}, f32[48,512]{1,0:T(8,128)S(1)}, u32[]{:S(2)}, u32[]{:S(2)}) collective-permute-start(f32[48,512]{1,0:T(8,128)S(1)} %get-tuple-element.36), channel_id=1, source_target_pairs={{0,1},{1,2},{2,3},{3,4},{4,5},{5,6},{6,7},{7,8},{8,9},{9,10},{10,1... | collective-permute-start | bytes 294920 | tf_op jit(solution)/shard_map/ppermute | solution.py:309

commit v6 on v5

--- a/solution.py
+++ b/solution.py
@@ -13,7 +13,6 @@
 MIB = 1 << 20
 STEP = 4
 EDGE_STEP = 8
-FINAL_STEP = 2
 GRANT = 20
 LARGE = 44
 
@@ -141,35 +140,29 @@
     middle_steps(levelled, row_weight, col_high, col_low, out, later, factor, begin, True, deepest)
 
 
-def shallow_kernel(levelled, row_weight, col_high, col_low, later_in, factor_in, out, later, factor):
-    later[...] = later_in[...]
-    factor[...] = factor_in[...]
-    middle_steps(levelled, row_weight, col_high, col_low, out, later, factor, 0, False, None)
-
-
-def edge_kernel(levelled, above, below, row_weight, col_high, col_low, out, deepest, later, factor):
+def edge_steps(levelled, above, below, row_weight, col_high, col_low, out, later, factor, begin, fresh, deepest):
     near = 2 * RADIUS
-    planes, rows, _ = levelled.shape
-    later[...] = jnp.ones_like(later)
-    factor[...] = jnp.ones_like(factor)
-    steps = planes // EDGE_STEP
+    rows = levelled.shape[1]
+    steps = out.shape[0] // EDGE_STEP
 
     def one(index, _):
         at = (steps - 1 - index) * EDGE_STEP
         values, parts = [], []
         for plane in range(EDGE_STEP):
-            upper = levelled[at + plane, :near]
-            lower = levelled[at + plane, rows - near:]
-            value = jnp.concatenate([above[at + plane], upper, lower, below[at + plane]], axis=0)
+            here = begin + at + plane
+            upper = levelled[here, :near]
+            lower = levelled[here, rows - near:]
+            value = jnp.concatenate([above[here], upper, lower, below[here]], axis=0)
             high, low = halves(value)
             parts.append(row_blur(high, low, row_weight))
             values.append(jnp.concatenate([upper[:RADIUS], lower[RADIUS:]], axis=0))
         blurred = blur_planes(parts, col_high, col_low)
-        start = index == 0
-
-        @pl.when(start)
-        def _():
-            deepest[...] = blurred[-1]
+        start = index == 0 if fresh else None
+        if fresh:
+
+            @pl.when(start)
+            def _():
+                deepest[...] = blurred[-1]
 
         def put(plane, value):
             out[at + plane] = value
@@ -178,6 +171,25 @@
         return 0
 
     lax.fori_loop(0, steps, one, 0)
+
+
+def edge_kernel(levelled, above, below, row_weight, col_high, col_low, out, deepest, later, factor):
+    later[...] = jnp.ones_like(later)
+    factor[...] = jnp.ones_like(factor)
+    begin = levelled.shape[0] - out.shape[0]
+    edge_steps(levelled, above, below, row_weight, col_high, col_low, out, later, factor, begin, True, deepest)
+
+
+def shallow_kernel(
+    levelled, above, below, mid_weight, edge_weight, col_high, col_low, later_mid, factor_mid, later_edge, factor_edge,
+    mid_out, mid_later, mid_factor, edge_out, edge_later, edge_factor,
+):
+    mid_later[...] = later_mid[...]
+    mid_factor[...] = factor_mid[...]
+    edge_later[...] = later_edge[...]
+    edge_factor[...] = factor_edge[...]
+    edge_steps(levelled, above, below, edge_weight, col_high, col_low, edge_out, edge_later, edge_factor, 0, False, None)
+    middle_steps(levelled, mid_weight, col_high, col_low, mid_out, mid_later, mid_factor, 0, False, None)
 
 
 def join_kernel(before_mid, before_edge, first_mid, first_edge, factor_mid, factor_edge, pieces):
@@ -203,33 +215,25 @@
         out[slab] = running
 
 
-def final_kernel(shallow, deep, edge, pieces, out, factor):
-    step, rows, cols = out.shape
+def final_kernel(shallow, deep, shallow_edge, deep_edge, pieces, out, factor, result, sems):
+    planes, rows, cols = result.shape
     wide = cols // 4
-    index = pl.program_id(0)
-    begin = index * step
-    half = shallow.shape[0]
-
-    @pl.when(index == 0)
-    def _():
-        for group in range(rows // RADIUS):
-            for part in range(4):
-                factor[pl.ds(group * RADIUS, RADIUS), pl.ds(part * wide, wide)] = pieces[group * 4 + part]
-
-    inner = pl.ds(RADIUS, rows - 2 * RADIUS)
-    for plane in range(step):
-        out[plane, :RADIUS] = edge[begin + plane, :RADIUS] * factor[:RADIUS]
-        out[plane, rows - RADIUS:] = edge[begin + plane, RADIUS:] * factor[rows - RADIUS:]
-
-    @pl.when(begin < half)
-    def _():
-        for plane in range(step):
-            out[plane, inner] = shallow[begin + plane] * factor[inner]
-
-    @pl.when(begin >= half)
-    def _():
-        for plane in range(step):
-            out[plane, inner] = deep[begin - half + plane] * factor[inner]
+    half = planes // 2
+    for group in range(rows // RADIUS):
+        for part in range(4):
+            factor[group * RADIUS:(group + 1) * RADIUS, part * wide:(part + 1) * wide] = pieces[group * 4 + part]
+    copies = []
+    for plane in range(planes):
+        middle, edge = (shallow, shallow_edge) if plane < half else (deep, deep_edge)
+        at = plane % half
+        result[plane, :RADIUS] = edge[at, :RADIUS] * factor[:RADIUS]
+        result[plane, RADIUS:rows - RADIUS] = middle[at] * factor[RADIUS:rows - RADIUS]
+        result[plane, rows - RADIUS:] = edge[at, RADIUS:] * factor[rows - RADIUS:]
+        copy = pltpu.make_async_copy(result.at[plane], out.at[plane], sems.at[plane])
+        copy.start()
+        copies.append(copy)
+    for copy in copies:
+        copy.wait()
 
 
 def shape(*dims):
@@ -277,18 +281,21 @@
     )(volume, flat)
 
 
-def final_call(shallow, deep, edge, pieces):
+def final_call(shallow, deep, shallow_edge, deep_edge, pieces):
     half, inner, cols = deep.shape
     rows = inner + 2 * RADIUS
     return pl.pallas_call(
         final_kernel,
-        grid=(2 * half // FINAL_STEP,),
-        in_specs=[pl.BlockSpec(memory_space=pltpu.VMEM)] * 4,
-        out_specs=pl.BlockSpec((FINAL_STEP, rows, cols), lambda i: (i, 0, 0)),
+        in_specs=[pl.BlockSpec(memory_space=pltpu.VMEM)] * 5,
+        out_specs=pl.BlockSpec(memory_space=pl.ANY),
         out_shape=shape(2 * half, rows, cols),
-        scratch_shapes=[pltpu.VMEM((rows, cols), jnp.float32)],
+        scratch_shapes=[
+            pltpu.VMEM((rows, cols), jnp.float32),
+            pltpu.VMEM((2 * half, rows, cols), jnp.float32),
+            pltpu.SemaphoreType.DMA((2 * half,)),
+        ],
         compiler_params=params(GRANT),
-    )(shallow, deep, edge, pieces)
+    )(shallow, deep, shallow_edge, deep_edge, pieces)
 
 
 def body(volume, flat_field):
@@ -303,13 +310,14 @@
         deep_kernel, 4, [shape(half, inner, cols)] + [shape(inner, cols)] * 3, cost(6e9, 6e6)
     )(levelled, mid_weight, col_high, col_low)
     before_mid = lax.ppermute(deepest, "depth", onward)
-    edge, deepest_edge, first_edge, factor_edge = vmem_call(
-        edge_kernel, 6, [shape(planes, near, cols)] + [shape(near, cols)] * 3, cost(4e9, 8e6)
+    deep_edge, deepest_edge, later_edge, factor_edge = vmem_call(
+        edge_kernel, 6, [shape(half, near, cols)] + [shape(near, cols)] * 3, cost(2e9, 4e6)
     )(levelled, above, below, edge_weight, col_high, col_low)
     before_edge = lax.ppermute(deepest_edge, "depth", onward)
-    shallow, first_mid, factor_mid = vmem_call(
-        shallow_kernel, 6, [shape(half, inner, cols)] + [shape(inner, cols)] * 2, cost(6e9, 6e6)
-    )(levelled, mid_weight, col_high, col_low, later, factor)
+    outputs = [shape(half, inner, cols)] + [shape(inner, cols)] * 2 + [shape(half, near, cols)] + [shape(near, cols)] * 2
+    shallow, first_mid, factor_mid, shallow_edge, first_edge, factor_edge = vmem_call(shallow_kernel, 11, outputs, cost(8e9, 1e7))(
+        levelled, above, below, mid_weight, edge_weight, col_high, col_low, later, factor, later_edge, factor_edge
+    )
     traded = shape(slabs, RADIUS, cols // 4)
     (pieces,) = vmem_call(join_kernel, 6, [traded], cost(1e6, 2e6))(
         before_mid, before_edge, first_mid, first_edge, factor_mid, factor_edge
@@ -317,7 +325,7 @@
     mine = lax.all_to_all(pieces, "depth", 0, 0, tiled=True)
     (reached,) = vmem_call(scan_kernel, 1, [traded], cost(1e6, 1e6))(mine)
     back = lax.all_to_all(reached, "depth", 0, 0, tiled=True)
-    return final_call(shallow, deep, edge, back)
+    return final_call(shallow, deep, shallow_edge, deep_edge, back)
 
 
 def solution(mesh):

time: 80.9 us -> 79.1 us (0.978)
  Pallas kernels: 17.6 us -> 16.1 us
    pallas_call x3, Pallas kernels: 10.4 us -> 8.83 us  [the longest x1 4.72 us: body(): vmem_call(shallow_kernel, 11, outputs, cost(8000000000.0, 10000000.0))]
    all_to_all x1, blocking collectives: 27.7 us -> 26.5 us  [body(): mine = lax.all_to_all(pieces, 'depth', 0, 0, tiled=True)]
    all_to_all x1, blocking collectives: 19.6 us -> 20.4 us  [body(): back = lax.all_to_all(reached, 'depth', 0, 0, tiled=True)]
where the time goes in v6:
time: 79.1 us; the launch traced here: 78.8 us
  blocking collectives  47 us (59%)
  Pallas kernels  16.1 us (20%)
  starting transfers between devices  12.4 us (16%)
  waiting for transfers between devices  2.27 us (3%)
  local copies, waits for them, and re-layouts  1 us (1%)
    all_to_all x1, blocking collectives, body(): mine = lax.all_to_all(pieces, 'depth', 0, 0, tiled=True)  26.5 us
    all_to_all x1, blocking collectives, body(): back = lax.all_to_all(reached, 'depth', 0, 0, tiled=True)  20.4 us
    pallas_call x1, Pallas kernels, body(): vmem_call(shallow_kernel, 11, outputs, cost(8000000000.0, 10000000.0))  4.72 us
    pallas_call x1, Pallas kernels, body(): vmem_call(deep_kernel, 4, [shape(half, inner, cols)] + [shape(inner, cols...  3.8 us
    ppermute x1, starting transfers between devices, body(): below = lax.ppermute(top, 'tile', [(i + 1, i) for i in range(tiles - 1)])  3.64 us
    ppermute x1, starting transfers between devices, body(): before_mid = lax.ppermute(deepest, 'depth', onward)  3.41 us
    ppermute x1, starting transfers between devices, body(): before_edge = lax.ppermute(deepest_edge, 'depth', onward)  3.4 us
    pallas_call x1, Pallas kernels, level_call(): pl.pallas_call(level_kernel, in_specs=[pl.BlockSpec(memory_space=pltpu.HB...  3.32 us
  transfers between devices with their start and end apart: 4, of which 2 were waited for; matrix products, arithmetic and copies ran while one was open for 0% of the time, Pallas kernels for 12%

profile of v6, /device:TPU:8, one launch (start us, length us, event | category | flops | bytes accessed | tf_op | source)
XLA Modules:
  0.0 78.8 jit_solution(14481394586334179117)
XLA Ops:
  0.0 0.0 copy-start
  0.0 1.0 %copy-done = f32[192,512]{1,0:T(8,128)S(1)} copy-done((f32[192,512]{1,0:T(8,128)S(1)}, f32[192,512]{1,0:T(8,128)}, u32[]{:S(2)}) %copy-start) | copy-done | bytes 393240
  1.0 3.3 %shard_map.28 = (f32[16,192,512]{2,1,0:T(8,128)S(1)}, f32[16,24,512]{2,1,0:T(8,128)S(1)}, f32[16,24,512]{2,1,0:T(8,128)S(1)}, bf16[288,192]{1,0:T(8,128)(2,1)S(1...) custom-call(f32[16,192,512]{2,1,0:T(8,128)} %volume.1, ...), custom_call_target="tpu_custom_call" | custom-call | flops 10000000 | bytes 7000000 | tf_op jit(solution)/shard_map/pallas_call | solution.py:269
  4.3 1.9 %collective-permute-start = (f32[16,24,512]{2,1,0:T(8,128)S(1)}, f32[16,24,512]{2,1,0:T(8,128)S(1)}, u32[]{:S(2)}, u32[]{:S(2)}) collective-permute-start(f32[16,24,512]{2,1,0:T(8,128)S(1)} %get-tuple-element.27), channel_id=1, source_target_pairs={{0,32},{32,64},{64,96},{96,128},{128,160},{160,192},{192,224},{1,3... | collective-permute-start | bytes 2359304 | tf_op jit(solution)/shard_map/ppermute | solution.py:307
  6.3 3.6 %collective-permute-start.1 = (f32[16,24,512]{2,1,0:T(8,128)S(1)}, f32[16,24,512]{2,1,0:T(8,128)S(1)}, u32[]{:S(2)}, u32[]{:S(2)}) collective-permute-start(f32[16,24,512]{2,1,0:T(8,128)S(1)} %get-tuple-element.28), channel_id=1, source_target_pairs={{32,0},{64,32},{96,64},{128,96},{160,128},{192,160},{224,192},{33,... | collective-permute-start | bytes 2359304 | tf_op jit(solution)/shard_map/ppermute | solution.py:308
  9.9 3.8 %shard_map.29 = (f32[8,144,512]{2,1,0:T(8,128)S(1)}, f32[144,512]{1,0:T(8,128)S(1)}, f32[144,512]{1,0:T(8,128)S(1)}, f32[144,512]{1,0:T(8,128)S(1)}) custom-call(f32[16,192,512]{2,1,0:T(8,128)S(1)} %get-tuple-element.26.levelled, bf16[288,192]{1,0:T(8,128)(2,1)S(1)} %get-tuple-element.29.row_weight.mid_weight, ...), custom_call_target="tpu_custom_call" | custom-call | flops 6000000000 | bytes 6000000 | tf_op jit(solution)/shard_map/pallas_call | solution.py:309
  13.7 3.4 %collective-permute-start.2 = (f32[144,512]{1,0:T(8,128)S(1)}, f32[144,512]{1,0:T(8,128)S(1)}, u32[]{:S(2)}, u32[]{:S(2)}) collective-permute-start(f32[144,512]{1,0:T(8,128)S(1)} %get-tuple-element.41), channel_id=1, source_target_pairs={{0,1},{1,2},{2,3},{3,4},{4,5},{5,6},{6,7},{7,8},{8,9},{9,10},{10,1... | collective-permute-start | bytes 884744 | tf_op jit(solution)/shard_map/ppermute | solution.py:312
  17.1 0.5 collective-permute-done.above
  17.6 1.8 %collective-permute-done.1.below = f32[16,24,512]{2,1,0:T(8,128)S(1)} collective-permute-done((f32[16,24,512]{2,1,0:T(8,128)S(1)}, f32[16,24,512]{2,1,0:T(8,128)S(1)}, u32[]{:S(2)}, u32[]{:S(2)}) %collective-permute-start.1) | collective-permute-done | bytes 786464 | tf_op jit(solution)/shard_map/ppermute | solution.py:308
  19.4 1.3 %shard_map.30 = (f32[8,48,512]{2,1,0:T(8,128)S(1)}, f32[48,512]{1,0:T(8,128)S(1)}, f32[48,512]{1,0:T(8,128)S(1)}, f32[48,512]{1,0:T(8,128)S(1)}) custom-call(f32[16,192,512]{2,1,0:T(8,128)S(1)} %get-tuple-element.26.levelled, f32[16,24,512]{2,1,0:T(8,128)S(1)} %collective-permute-done.above, f32[16,24,512]{2,1,0:T(8,128)S(1)} %collective-permute-done.1.below, ...), custom_call_target="tpu_custom_call" | custom-call | flops 2000000000 | bytes 4000000 | tf_op jit(solution)/shard_map/pallas_call | solution.py:313
  20.7 3.4 %collective-permute-start.3 = (f32[48,512]{1,0:T(8,128)S(1)}, f32[48,512]{1,0:T(8,128)S(1)}, u32[]{:S(2)}, u32[]{:S(2)}) collective-permute-start(f32[48,512]{1,0:T(8,128)S(1)} %get-tuple-element.42), channel_id=1, source_target_pairs={{0,1},{1,2},{2,3},{3,4},{4,5},{5,6},{6,7},{7,8},{8,9},{9,10},{10,1... | collective-permute-start | bytes 294920 | tf_op jit(solution)/shard_map/ppermute | solution.py:316
  24.1 4.7 %shard_map.31 = (f32[8,144,512]{2,1,0:T(8,128)S(1)}, f32[144,512]{1,0:T(8,128)S(1)}, f32[144,512]{1,0:T(8,128)S(1)}, f32[8,48,512]{2,1,0:T(8,128)S(1)}, f32[48,512]{1,0:T(8,128)S(1)}, /*index=5*/f32[48,512]{1,0:T(8,128)S(1)}) custom-call(f32[16,192,512]{2,1,0:T(8,128)S(1)} %get-tuple-element.26.levelled, f32[16,24,512]{2,1,0:T(8,128)S(1)} %collective-permute-done.above, ...), custom_call_target="tpu_custom_call" | custom-call | flops 8000000000 | bytes 10000000 | tf_op jit(solution)/shard_map/pallas_call | solution.py:318
  28.8 0.0 collective-permute-done.2.before_mid
  28.8 0.0 collective-permute-done.3.before_edge
  28.8 0.1 shard_map.32
  29.0 26.5 %all_to_all.10.pieces = f32[32,24,128]{2,1,0:T(8,128)S(1)} all-to-all(f32[32,24,128]{2,1,0:T(8,128)S(1)} %shard_map.32), channel_id=1, replica_groups=mesh['tile'=8,'depth'=32] {'depth'}, dimensions={0} | all-to-all | bytes 786432 | tf_op jit(solution)/shard_map/all_to_all | solution.py:325
  55.6 20.4 %all_to_all.11.pieces = f32[32,24,128]{2,1,0:T(8,128)S(1)} all-to-all(f32[32,24,128]{2,1,0:T(8,128)S(1)} %shard_map.33), channel_id=1, replica_groups=mesh['tile'=8,'depth'=32] {'depth'}, dimensions={0} | all-to-all | bytes 786432 | tf_op jit(solution)/shard_map/all_to_all | solution.py:327
  76.0 2.8 %shard_map.34 = f32[16,192,512]{2,1,0:T(8,128)} custom-call(f32[8,144,512]{2,1,0:T(8,128)S(1)} %get-tuple-element.37.shallow, f32[8,144,512]{2,1,0:T(8,128)S(1)} %get-tuple-element.38.deep, f32[8,48,512]{2,1,0:T(8,128)S(1)} %get-tuple-element.39.shallow_edge, f32[8,48,512]{2,1,0:T(8,128)S(1)} %get-tuple-element.40.deep_edge, ...), custom_call_target="tpu_custom_call" | custom-call | tf_op jit(solution)/shard_map/pallas_call | solution.py:287
  (1 shorter events, 0.0 us)
Async XLA Ops:
  0.0 1.0 %copy-start = (f32[192,512]{1,0:T(8,128)S(1)}, f32[192,512]{1,0:T(8,128)}, u32[]{:S(2)}) copy-start(f32[192,512]{1,0:T(8,128)} %flat.1) | copy-start | bytes 1179652
  4.3 13.3 %collective-permute-start = (f32[16,24,512]{2,1,0:T(8,128)S(1)}, f32[16,24,512]{2,1,0:T(8,128)S(1)}, u32[]{:S(2)}, u32[]{:S(2)}) collective-permute-start(f32[16,24,512]{2,1,0:T(8,128)S(1)} %get-tuple-element.27), channel_id=1, source_target_pairs={{0,32},{32,64},{64,96},{96,128},{128,160},{160,192},{192,224},{1,3... | collective-permute-start | bytes 2359304 | tf_op jit(solution)/shard_map/ppermute | solution.py:307
  6.3 13.1 %collective-permute-start.1 = (f32[16,24,512]{2,1,0:T(8,128)S(1)}, f32[16,24,512]{2,1,0:T(8,128)S(1)}, u32[]{:S(2)}, u32[]{:S(2)}) collective-permute-start(f32[16,24,512]{2,1,0:T(8,128)S(1)} %get-tuple-element.28), channel_id=1, source_target_pairs={{32,0},{64,32},{96,64},{128,96},{160,128},{192,160},{224,192},{33,... | collective-permute-start | bytes 2359304 | tf_op jit(solution)/shard_map/ppermute | solution.py:308
  13.7 15.1 %collective-permute-start.2 = (f32[144,512]{1,0:T(8,128)S(1)}, f32[144,512]{1,0:T(8,128)S(1)}, u32[]{:S(2)}, u32[]{:S(2)}) collective-permute-start(f32[144,512]{1,0:T(8,128)S(1)} %get-tuple-element.41), channel_id=1, source_target_pairs={{0,1},{1,2},{2,3},{3,4},{4,5},{5,6},{6,7},{7,8},{8,9},{9,10},{10,1... | collective-permute-start | bytes 884744 | tf_op jit(solution)/shard_map/ppermute | solution.py:312
  20.7 8.1 %collective-permute-start.3 = (f32[48,512]{1,0:T(8,128)S(1)}, f32[48,512]{1,0:T(8,128)S(1)}, u32[]{:S(2)}, u32[]{:S(2)}) collective-permute-start(f32[48,512]{1,0:T(8,128)S(1)} %get-tuple-element.42), channel_id=1, source_target_pairs={{0,1},{1,2},{2,3},{3,4},{4,5},{5,6},{6,7},{7,8},{8,9},{9,10},{10,1... | collective-permute-start | bytes 294920 | tf_op jit(solution)/shard_map/ppermute | solution.py:316

commit v7 on v6

--- a/solution.py
+++ b/solution.py
@@ -86,7 +86,7 @@
     return [blurred[plane * rows:(plane + 1) * rows] for plane in range(len(parts))]
 
 
-def level_kernel(volume, flat, levelled, top, bottom, mid_weight, edge_weight, col_high, col_low, inverse, flat_sem, sems):
+def level_kernel(volume, flat, levelled, outward, inward, mid_weight, edge_weight, col_high, col_low, inverse, flat_sem, sems):
     planes, rows, _ = levelled.shape
     first = pltpu.make_async_copy(flat, inverse, flat_sem)
     first.start()
@@ -96,12 +96,14 @@
     fill_weights(rows, mid_weight, edge_weight, col_high, col_low)
     first.wait()
     inverse[...] = 1.0 / inverse[...]
+    odd = lax.axis_index("tile") % 2 == 1
     for plane in range(planes):
         copies[plane].wait()
         value = levelled[plane] * inverse[...]
         levelled[plane] = value
-        top[plane] = value[:RADIUS]
-        bottom[plane] = value[rows - RADIUS:]
+        top, bottom = value[:RADIUS], value[rows - RADIUS:]
+        outward[plane] = jnp.where(odd, bottom, top)
+        inward[plane] = jnp.where(odd, top, bottom)
 
 
 def middle_steps(levelled, row_weight, col_high, col_low, out, later, factor, begin, fresh, deepest):
@@ -140,10 +142,11 @@
     middle_steps(levelled, row_weight, col_high, col_low, out, later, factor, begin, True, deepest)
 
 
-def edge_steps(levelled, above, below, row_weight, col_high, col_low, out, later, factor, begin, fresh, deepest):
+def edge_steps(levelled, outer, inner, row_weight, col_high, col_low, out, later, factor, begin, fresh, deepest):
     near = 2 * RADIUS
     rows = levelled.shape[1]
     steps = out.shape[0] // EDGE_STEP
+    odd = lax.axis_index("tile") % 2 == 1
 
     def one(index, _):
         at = (steps - 1 - index) * EDGE_STEP
@@ -152,7 +155,9 @@
             here = begin + at + plane
             upper = levelled[here, :near]
             lower = levelled[here, rows - near:]
-            value = jnp.concatenate([above[here], upper, lower, below[here]], axis=0)
+            above = jnp.where(odd, inner[here], outer[here])
+            below = jnp.where(odd, outer[here], inner[here])
+            value = jnp.concatenate([above, upper, lower, below], axis=0)
             high, low = halves(value)
             parts.append(row_blur(high, low, row_weight))
             values.append(jnp.concatenate([upper[:RADIUS], lower[RADIUS:]], axis=0))
@@ -173,22 +178,22 @@
     lax.fori_loop(0, steps, one, 0)
 
 
-def edge_kernel(levelled, above, below, row_weight, col_high, col_low, out, deepest, later, factor):
+def edge_kernel(levelled, outer, inner, row_weight, col_high, col_low, out, deepest, later, factor):
     later[...] = jnp.ones_like(later)
     factor[...] = jnp.ones_like(factor)
     begin = levelled.shape[0] - out.shape[0]
-    edge_steps(levelled, above, below, row_weight, col_high, col_low, out, later, factor, begin, True, deepest)
+    edge_steps(levelled, outer, inner, row_weight, col_high, col_low, out, later, factor, begin, True, deepest)
 
 
 def shallow_kernel(
-    levelled, above, below, mid_weight, edge_weight, col_high, col_low, later_mid, factor_mid, later_edge, factor_edge,
+    levelled, outer, inner, mid_weight, edge_weight, col_high, col_low, later_mid, factor_mid, later_edge, factor_edge,
     mid_out, mid_later, mid_factor, edge_out, edge_later, edge_factor,
 ):
     mid_later[...] = later_mid[...]
     mid_factor[...] = factor_mid[...]
     edge_later[...] = later_edge[...]
     edge_factor[...] = factor_edge[...]
-    edge_steps(levelled, above, below, edge_weight, col_high, col_low, edge_out, edge_later, edge_factor, 0, False, None)
+    edge_steps(levelled, outer, inner, edge_weight, col_high, col_low, edge_out, edge_later, edge_factor, 0, False, None)
     middle_steps(levelled, mid_weight, col_high, col_low, mid_out, mid_later, mid_factor, 0, False, None)
 
 
@@ -298,25 +303,29 @@
     )(shallow, deep, shallow_edge, deep_edge, pieces)
 
 
+def swapped(begin, count):
+    return [pair for i in range(begin, count - 1, 2) for pair in ((i, i + 1), (i + 1, i))]
+
+
 def body(volume, flat_field):
     planes, rows, cols = volume.shape
     tiles, slabs = lax.axis_size("tile"), lax.axis_size("depth")
     onward = [(i, i + 1) for i in range(slabs - 1)]
     inner, near, half = rows - 2 * RADIUS, 2 * RADIUS, planes // 2
-    levelled, top, bottom, mid_weight, edge_weight, col_high, col_low = level_call(volume, flat_field)
-    above = lax.ppermute(bottom, "tile", [(i, i + 1) for i in range(tiles - 1)])
-    below = lax.ppermute(top, "tile", [(i + 1, i) for i in range(tiles - 1)])
+    levelled, outward, inward, mid_weight, edge_weight, col_high, col_low = level_call(volume, flat_field)
+    outer = lax.ppermute(outward, "tile", swapped(1, tiles))
+    inner_halo = lax.ppermute(inward, "tile", swapped(0, tiles))
     deep, deepest, later, factor = vmem_call(
         deep_kernel, 4, [shape(half, inner, cols)] + [shape(inner, cols)] * 3, cost(6e9, 6e6)
     )(levelled, mid_weight, col_high, col_low)
     before_mid = lax.ppermute(deepest, "depth", onward)
     deep_edge, deepest_edge, later_edge, factor_edge = vmem_call(
         edge_kernel, 6, [shape(half, near, cols)] + [shape(near, cols)] * 3, cost(2e9, 4e6)
-    )(levelled, above, below, edge_weight, col_high, col_low)
+    )(levelled, outer, inner_halo, edge_weight, col_high, col_low)
     before_edge = lax.ppermute(deepest_edge, "depth", onward)
     outputs = [shape(half, inner, cols)] + [shape(inner, cols)] * 2 + [shape(half, near, cols)] + [shape(near, cols)] * 2
     shallow, first_mid, factor_mid, shallow_edge, first_edge, factor_edge = vmem_call(shallow_kernel, 11, outputs, cost(8e9, 1e7))(
-        levelled, above, below, mid_weight, edge_weight, col_high, col_low, later, factor, later_edge, factor_edge
+        levelled, outer, inner_halo, mid_weight, edge_weight, col_high, col_low, later, factor, later_edge, factor_edge
     )
     traded = shape(slabs, RADIUS, cols // 4)
     (pieces,) = vmem_call(join_kernel, 6, [traded], cost(1e6, 2e6))(

time: 79.1 us -> 75.4 us (0.953)
  blocking collectives: 47 us -> 44.9 us
  starting transfers between devices: 12.4 us -> 10.5 us
    all_to_all x1, blocking collectives: 20.4 us -> 18.6 us  [body(): back = lax.all_to_all(reached, 'depth', 0, 0, tiled=True)]
    ppermute x2, starting transfers between devices: 5.56 us -> 3.69 us  [the longest x1 1.92 us: body(): outer = lax.ppermute(outward, 'tile', swapped(1, tiles))]
  transfers between devices with their start and end apart: 4 -> 4, of which waited for: 2 -> 1; matrix products, arithmetic and copies ran while one was open for 0% -> 0% of each run, Pallas kernels for 12% -> 13%
where the time goes in v7:
time: 75.4 us; the launch traced here: 75.1 us
  blocking collectives  44.9 us (60%)
  Pallas kernels  16.2 us (21%)
  starting transfers between devices  10.5 us (14%)
  waiting for transfers between devices  2.4 us (3%)
  local copies, waits for them, and re-layouts  1 us (1%)
    all_to_all x1, blocking collectives, body(): mine = lax.all_to_all(pieces, 'depth', 0, 0, tiled=True)  26.3 us
    all_to_all x1, blocking collectives, body(): back = lax.all_to_all(reached, 'depth', 0, 0, tiled=True)  18.6 us
    pallas_call x1, Pallas kernels, body(): vmem_call(shallow_kernel, 11, outputs, cost(8000000000.0, 10000000.0))  4.81 us
    pallas_call x1, Pallas kernels, body(): vmem_call(deep_kernel, 4, [shape(half, inner, cols)] + [shape(inner, cols...  3.79 us
    ppermute x1, starting transfers between devices, body(): before_edge = lax.ppermute(deepest_edge, 'depth', onward)  3.44 us
    ppermute x1, starting transfers between devices, body(): before_mid = lax.ppermute(deepest, 'depth', onward)  3.42 us
    pallas_call x1, Pallas kernels, level_call(): pl.pallas_call(level_kernel, in_specs=[pl.BlockSpec(memory_space=pltpu.HB...  3.25 us
    pallas_call x1, Pallas kernels, final_call(): pl.pallas_call(final_kernel, in_specs=[pl.BlockSpec(memory_space=pltpu.VM...  2.82 us
  transfers between devices with their start and end apart: 4, of which 1 were waited for; matrix products, arithmetic and copies ran while one was open for 0% of the time, Pallas kernels for 13%

profile of v7, /device:TPU:8, one launch (start us, length us, event | category | flops | bytes accessed | tf_op | source)
XLA Modules:
  0.0 75.1 jit_solution(1476962677755686565)
XLA Ops:
  0.0 0.0 copy-start
  0.0 1.0 %copy-done = f32[192,512]{1,0:T(8,128)S(1)} copy-done((f32[192,512]{1,0:T(8,128)S(1)}, f32[192,512]{1,0:T(8,128)}, u32[]{:S(2)}) %copy-start) | copy-done | bytes 393240
  1.0 3.3 %shard_map.28 = (f32[16,192,512]{2,1,0:T(8,128)S(1)}, f32[16,24,512]{2,1,0:T(8,128)S(1)}, f32[16,24,512]{2,1,0:T(8,128)S(1)}, bf16[288,192]{1,0:T(8,128)(2,1)S(1...) custom-call(f32[16,192,512]{2,1,0:T(8,128)} %volume.1, ...), custom_call_target="tpu_custom_call" | custom-call | flops 10000000 | bytes 7000000 | tf_op jit(solution)/shard_map/pallas_call | solution.py:274
  4.3 1.9 %collective-permute-start = (f32[16,24,512]{2,1,0:T(8,128)S(1)}, f32[16,24,512]{2,1,0:T(8,128)S(1)}, u32[]{:S(2)}, u32[]{:S(2)}) collective-permute-start(f32[16,24,512]{2,1,0:T(8,128)S(1)} %get-tuple-element.27), channel_id=1, source_target_pairs={{32,64},{64,32},{96,128},{128,96},{160,192},{192,160},{33,65},{65,... | collective-permute-start | bytes 2359304 | tf_op jit(solution)/shard_map/ppermute | solution.py:316
  6.2 1.8 %collective-permute-start.1 = (f32[16,24,512]{2,1,0:T(8,128)S(1)}, f32[16,24,512]{2,1,0:T(8,128)S(1)}, u32[]{:S(2)}, u32[]{:S(2)}) collective-permute-start(f32[16,24,512]{2,1,0:T(8,128)S(1)} %get-tuple-element.28), channel_id=1, source_target_pairs={{0,32},{32,0},{64,96},{96,64},{128,160},{160,128},{192,224},{224,1... | collective-permute-start | bytes 2359304 | tf_op jit(solution)/shard_map/ppermute | solution.py:317
  8.0 3.8 %shard_map.29 = (f32[8,144,512]{2,1,0:T(8,128)S(1)}, f32[144,512]{1,0:T(8,128)S(1)}, f32[144,512]{1,0:T(8,128)S(1)}, f32[144,512]{1,0:T(8,128)S(1)}) custom-call(f32[16,192,512]{2,1,0:T(8,128)S(1)} %get-tuple-element.26.levelled, bf16[288,192]{1,0:T(8,128)(2,1)S(1)} %get-tuple-element.29.row_weight.mid_weight, ...), custom_call_target="tpu_custom_call" | custom-call | flops 6000000000 | bytes 6000000 | tf_op jit(solution)/shard_map/pallas_call | solution.py:318
  11.8 3.4 %collective-permute-start.2 = (f32[144,512]{1,0:T(8,128)S(1)}, f32[144,512]{1,0:T(8,128)S(1)}, u32[]{:S(2)}, u32[]{:S(2)}) collective-permute-start(f32[144,512]{1,0:T(8,128)S(1)} %get-tuple-element.41), channel_id=1, source_target_pairs={{0,1},{1,2},{2,3},{3,4},{4,5},{5,6},{6,7},{7,8},{8,9},{9,10},{10,1... | collective-permute-start | bytes 884744 | tf_op jit(solution)/shard_map/ppermute | solution.py:321
  15.2 2.4 %collective-permute-done.outer = f32[16,24,512]{2,1,0:T(8,128)S(1)} collective-permute-done((f32[16,24,512]{2,1,0:T(8,128)S(1)}, f32[16,24,512]{2,1,0:T(8,128)S(1)}, u32[]{:S(2)}, u32[]{:S(2)}) %collective-permute-start) | collective-permute-done | bytes 786464 | tf_op jit(solution)/shard_map/ppermute | solution.py:316
  17.6 0.0 collective-permute-done.1.inner
  17.6 1.4 %shard_map.30 = (f32[8,48,512]{2,1,0:T(8,128)S(1)}, f32[48,512]{1,0:T(8,128)S(1)}, f32[48,512]{1,0:T(8,128)S(1)}, f32[48,512]{1,0:T(8,128)S(1)}) custom-call(f32[16,192,512]{2,1,0:T(8,128)S(1)} %get-tuple-element.26.levelled, f32[16,24,512]{2,1,0:T(8,128)S(1)} %collective-permute-done.outer, f32[16,24,512]{2,1,0:T(8,128)S(1)} %collective-permute-done.1.inner, ...), custom_call_target="tpu_custom_call" | custom-call | flops 2000000000 | bytes 4000000 | tf_op jit(solution)/shard_map/pallas_call | solution.py:322
  18.9 3.4 %collective-permute-start.3 = (f32[48,512]{1,0:T(8,128)S(1)}, f32[48,512]{1,0:T(8,128)S(1)}, u32[]{:S(2)}, u32[]{:S(2)}) collective-permute-start(f32[48,512]{1,0:T(8,128)S(1)} %get-tuple-element.42), channel_id=1, source_target_pairs={{0,1},{1,2},{2,3},{3,4},{4,5},{5,6},{6,7},{7,8},{8,9},{9,10},{10,1... | collective-permute-start | bytes 294920 | tf_op jit(solution)/shard_map/ppermute | solution.py:325
  22.4 4.8 %shard_map.31 = (f32[8,144,512]{2,1,0:T(8,128)S(1)}, f32[144,512]{1,0:T(8,128)S(1)}, f32[144,512]{1,0:T(8,128)S(1)}, f32[8,48,512]{2,1,0:T(8,128)S(1)}, f32[48,512]{1,0:T(8,128)S(1)}, /*index=5*/f32[48,512]{1,0:T(8,128)S(1)}) custom-call(f32[16,192,512]{2,1,0:T(8,128)S(1)} %get-tuple-element.26.levelled, f32[16,24,512]{2,1,0:T(8,128)S(1)} %collective-permute-done.outer, ...), custom_call_target="tpu_custom_call" | custom-call | flops 8000000000 | bytes 10000000 | tf_op jit(solution)/shard_map/pallas_call | solution.py:327
  27.2 0.0 collective-permute-done.2.before_mid
  27.2 0.0 collective-permute-done.3.before_edge
  27.2 0.1 shard_map.32
  27.4 26.3 %all_to_all.10.pieces = f32[32,24,128]{2,1,0:T(8,128)S(1)} all-to-all(f32[32,24,128]{2,1,0:T(8,128)S(1)} %shard_map.32), channel_id=1, replica_groups=mesh['tile'=8,'depth'=32] {'depth'}, dimensions={0} | all-to-all | bytes 786432 | tf_op jit(solution)/shard_map/all_to_all | solution.py:334
  53.7 18.6 %all_to_all.11.pieces = f32[32,24,128]{2,1,0:T(8,128)S(1)} all-to-all(f32[32,24,128]{2,1,0:T(8,128)S(1)} %shard_map.33), channel_id=1, replica_groups=mesh['tile'=8,'depth'=32] {'depth'}, dimensions={0} | all-to-all | bytes 786432 | tf_op jit(solution)/shard_map/all_to_all | solution.py:336
  72.3 2.8 %shard_map.34 = f32[16,192,512]{2,1,0:T(8,128)} custom-call(f32[8,144,512]{2,1,0:T(8,128)S(1)} %get-tuple-element.37.shallow, f32[8,144,512]{2,1,0:T(8,128)S(1)} %get-tuple-element.38.deep, f32[8,48,512]{2,1,0:T(8,128)S(1)} %get-tuple-element.39.shallow_edge, f32[8,48,512]{2,1,0:T(8,128)S(1)} %get-tuple-element.40.deep_edge, ...), custom_call_target="tpu_custom_call" | custom-call | tf_op jit(solution)/shard_map/pallas_call | solution.py:292
  (1 shorter events, 0.0 us)
Async XLA Ops:
  0.0 1.0 %copy-start = (f32[192,512]{1,0:T(8,128)S(1)}, f32[192,512]{1,0:T(8,128)}, u32[]{:S(2)}) copy-start(f32[192,512]{1,0:T(8,128)} %flat.1) | copy-start | bytes 1179652
  4.3 13.3 %collective-permute-start = (f32[16,24,512]{2,1,0:T(8,128)S(1)}, f32[16,24,512]{2,1,0:T(8,128)S(1)}, u32[]{:S(2)}, u32[]{:S(2)}) collective-permute-start(f32[16,24,512]{2,1,0:T(8,128)S(1)} %get-tuple-element.27), channel_id=1, source_target_pairs={{32,64},{64,32},{96,128},{128,96},{160,192},{192,160},{33,65},{65,... | collective-permute-start | bytes 2359304 | tf_op jit(solution)/shard_map/ppermute | solution.py:316
  6.2 11.4 %collective-permute-start.1 = (f32[16,24,512]{2,1,0:T(8,128)S(1)}, f32[16,24,512]{2,1,0:T(8,128)S(1)}, u32[]{:S(2)}, u32[]{:S(2)}) collective-permute-start(f32[16,24,512]{2,1,0:T(8,128)S(1)} %get-tuple-element.28), channel_id=1, source_target_pairs={{0,32},{32,0},{64,96},{96,64},{128,160},{160,128},{192,224},{224,1... | collective-permute-start | bytes 2359304 | tf_op jit(solution)/shard_map/ppermute | solution.py:317
  11.8 15.4 %collective-permute-start.2 = (f32[144,512]{1,0:T(8,128)S(1)}, f32[144,512]{1,0:T(8,128)S(1)}, u32[]{:S(2)}, u32[]{:S(2)}) collective-permute-start(f32[144,512]{1,0:T(8,128)S(1)} %get-tuple-element.41), channel_id=1, source_target_pairs={{0,1},{1,2},{2,3},{3,4},{4,5},{5,6},{6,7},{7,8},{8,9},{9,10},{10,1... | collective-permute-start | bytes 884744 | tf_op jit(solution)/shard_map/ppermute | solution.py:321
  18.9 8.3 %collective-permute-start.3 = (f32[48,512]{1,0:T(8,128)S(1)}, f32[48,512]{1,0:T(8,128)S(1)}, u32[]{:S(2)}, u32[]{:S(2)}) collective-permute-start(f32[48,512]{1,0:T(8,128)S(1)} %get-tuple-element.42), channel_id=1, source_target_pairs={{0,1},{1,2},{2,3},{3,4},{4,5},{5,6},{6,7},{7,8},{8,9},{9,10},{10,1... | collective-permute-start | bytes 294920 | tf_op jit(solution)/shard_map/ppermute | solution.py:325

commit v8 on v7

--- a/solution.py
+++ b/solution.py
@@ -178,14 +178,7 @@
     lax.fori_loop(0, steps, one, 0)
 
 
-def edge_kernel(levelled, outer, inner, row_weight, col_high, col_low, out, deepest, later, factor):
-    later[...] = jnp.ones_like(later)
-    factor[...] = jnp.ones_like(factor)
-    begin = levelled.shape[0] - out.shape[0]
-    edge_steps(levelled, outer, inner, row_weight, col_high, col_low, out, later, factor, begin, True, deepest)
-
-
-def shallow_kernel(
+def shallow_planes(
     levelled, outer, inner, mid_weight, edge_weight, col_high, col_low, later_mid, factor_mid, later_edge, factor_edge,
     mid_out, mid_later, mid_factor, edge_out, edge_later, edge_factor,
 ):
@@ -195,6 +188,27 @@
     edge_factor[...] = factor_edge[...]
     edge_steps(levelled, outer, inner, edge_weight, col_high, col_low, edge_out, edge_later, edge_factor, 0, False, None)
     middle_steps(levelled, mid_weight, col_high, col_low, mid_out, mid_later, mid_factor, 0, False, None)
+
+
+def edge_kernel(levelled, outer, inner, mid_weight, edge_weight, col_high, col_low, later_mid, factor_mid, out, deepest, later, factor, *shallow):
+    later[...] = jnp.ones_like(later)
+    factor[...] = jnp.ones_like(factor)
+    begin = levelled.shape[0] - out.shape[0]
+    edge_steps(levelled, outer, inner, edge_weight, col_high, col_low, out, later, factor, begin, True, deepest)
+
+    @pl.when(lax.axis_index("tile") % 2 == 1)
+    def _():
+        shallow_planes(
+            levelled, outer, inner, mid_weight, edge_weight, col_high, col_low, later_mid, factor_mid, later, factor, *shallow
+        )
+
+
+def shallow_kernel(*refs):
+    given, shallow = refs[:11], refs[17:]
+
+    @pl.when(lax.axis_index("tile") % 2 == 0)
+    def _():
+        shallow_planes(*given, *shallow)
 
 
 def join_kernel(before_mid, before_edge, first_mid, first_edge, factor_mid, factor_edge, pieces):
@@ -253,13 +267,14 @@
     return pl.CostEstimate(flops=int(flops), bytes_accessed=int(moved), transcendentals=0)
 
 
-def vmem_call(kernel, inputs, outputs, given):
+def vmem_call(kernel, inputs, outputs, given, aliases={}):
     vmem = pl.BlockSpec(memory_space=pltpu.VMEM)
     return pl.pallas_call(
         kernel,
         in_specs=[vmem] * inputs,
         out_specs=[vmem] * len(outputs),
         out_shape=outputs,
+        input_output_aliases=aliases,
         compiler_params=params(GRANT),
         cost_estimate=given,
     )
@@ -319,13 +334,16 @@
         deep_kernel, 4, [shape(half, inner, cols)] + [shape(inner, cols)] * 3, cost(6e9, 6e6)
     )(levelled, mid_weight, col_high, col_low)
     before_mid = lax.ppermute(deepest, "depth", onward)
-    deep_edge, deepest_edge, later_edge, factor_edge = vmem_call(
-        edge_kernel, 6, [shape(half, near, cols)] + [shape(near, cols)] * 3, cost(2e9, 4e6)
-    )(levelled, outer, inner_halo, edge_weight, col_high, col_low)
+    outputs = [shape(half, inner, cols)] + [shape(inner, cols)] * 2 + [shape(half, near, cols)] + [shape(near, cols)] * 2
+    deep_edge, deepest_edge, later_edge, factor_edge, *shallow_parts = vmem_call(
+        edge_kernel, 9, [shape(half, near, cols)] + [shape(near, cols)] * 3 + outputs, cost(2e9, 4e6)
+    )(levelled, outer, inner_halo, mid_weight, edge_weight, col_high, col_low, later, factor)
     before_edge = lax.ppermute(deepest_edge, "depth", onward)
-    outputs = [shape(half, inner, cols)] + [shape(inner, cols)] * 2 + [shape(half, near, cols)] + [shape(near, cols)] * 2
-    shallow, first_mid, factor_mid, shallow_edge, first_edge, factor_edge = vmem_call(shallow_kernel, 11, outputs, cost(8e9, 1e7))(
-        levelled, outer, inner_halo, mid_weight, edge_weight, col_high, col_low, later, factor, later_edge, factor_edge
+    shallow, first_mid, factor_mid, shallow_edge, first_edge, factor_edge = vmem_call(
+        shallow_kernel, 17, outputs, cost(8e9, 1e7), {11 + i: i for i in range(6)}
+    )(
+        levelled, outer, inner_halo, mid_weight, edge_weight, col_high, col_low, later, factor, later_edge, factor_edge,
+        *shallow_parts,
     )
     traded = shape(slabs, RADIUS, cols // 4)
     (pieces,) = vmem_call(join_kernel, 6, [traded], cost(1e6, 2e6))(

time: 75.4 us -> 77 us (1.021)
  blocking collectives: 44.9 us -> 46.2 us
    all_to_all x1, blocking collectives: 18.6 us -> 20.9 us  [body(): back = lax.all_to_all(reached, 'depth', 0, 0, tiled=True)]
    all_to_all x1, blocking collectives: 26.3 us -> 25.3 us  [body(): mine = lax.all_to_all(pieces, 'depth', 0, 0, tiled=True)]
where the time goes in v8:
time: 77 us; the launch traced here: 76.5 us
  blocking collectives  46.2 us (60%)
  Pallas kernels  16.2 us (21%)
  starting transfers between devices  10.5 us (14%)
  waiting for transfers between devices  2.4 us (3%)
  local copies, waits for them, and re-layouts  1 us (1%)
    all_to_all x1, blocking collectives, body(): mine = lax.all_to_all(pieces, 'depth', 0, 0, tiled=True)  25.3 us
    all_to_all x1, blocking collectives, body(): back = lax.all_to_all(reached, 'depth', 0, 0, tiled=True)  20.9 us
    pallas_call x1, Pallas kernels, body(): vmem_call(shallow_kernel, 17, outputs, cost(8000000000.0, 10000000.0), {1...  4.82 us
    pallas_call x1, Pallas kernels, body(): vmem_call(deep_kernel, 4, [shape(half, inner, cols)] + [shape(inner, cols...  3.79 us
    ppermute x1, starting transfers between devices, body(): before_edge = lax.ppermute(deepest_edge, 'depth', onward)  3.44 us
    ppermute x1, starting transfers between devices, body(): before_mid = lax.ppermute(deepest, 'depth', onward)  3.42 us
    pallas_call x1, Pallas kernels, level_call(): pl.pallas_call(level_kernel, in_specs=[pl.BlockSpec(memory_space=pltpu.HB...  3.25 us
    pallas_call x1, Pallas kernels, final_call(): pl.pallas_call(final_kernel, in_specs=[pl.BlockSpec(memory_space=pltpu.VM...  2.82 us
  transfers between devices with their start and end apart: 4, of which 1 were waited for; matrix products, arithmetic and copies ran while one was open for 0% of the time, Pallas kernels for 13%

profile of v8, /device:TPU:8, one launch (start us, length us, event | category | flops | bytes accessed | tf_op | source)
XLA Modules:
  0.0 76.5 jit_solution(18106948445233198693)
XLA Ops:
  0.0 0.0 copy-start
  0.0 1.0 %copy-done = f32[192,512]{1,0:T(8,128)S(1)} copy-done((f32[192,512]{1,0:T(8,128)S(1)}, f32[192,512]{1,0:T(8,128)}, u32[]{:S(2)}) %copy-start) | copy-done | bytes 393240
  1.0 3.3 %shard_map.28 = (f32[16,192,512]{2,1,0:T(8,128)S(1)}, f32[16,24,512]{2,1,0:T(8,128)S(1)}, f32[16,24,512]{2,1,0:T(8,128)S(1)}, bf16[288,192]{1,0:T(8,128)(2,1)S(1...) custom-call(f32[16,192,512]{2,1,0:T(8,128)} %volume.1, ...), custom_call_target="tpu_custom_call" | custom-call | flops 10000000 | bytes 7000000 | tf_op jit(solution)/shard_map/pallas_call | solution.py:289
  4.3 1.9 %collective-permute-start = (f32[16,24,512]{2,1,0:T(8,128)S(1)}, f32[16,24,512]{2,1,0:T(8,128)S(1)}, u32[]{:S(2)}, u32[]{:S(2)}) collective-permute-start(f32[16,24,512]{2,1,0:T(8,128)S(1)} %get-tuple-element.33), channel_id=1, source_target_pairs={{32,64},{64,32},{96,128},{128,96},{160,192},{192,160},{33,65},{65,... | collective-permute-start | bytes 2359304 | tf_op jit(solution)/shard_map/ppermute | solution.py:331
  6.2 1.8 %collective-permute-start.1 = (f32[16,24,512]{2,1,0:T(8,128)S(1)}, f32[16,24,512]{2,1,0:T(8,128)S(1)}, u32[]{:S(2)}, u32[]{:S(2)}) collective-permute-start(f32[16,24,512]{2,1,0:T(8,128)S(1)} %get-tuple-element.34), channel_id=1, source_target_pairs={{0,32},{32,0},{64,96},{96,64},{128,160},{160,128},{192,224},{224,1... | collective-permute-start | bytes 2359304 | tf_op jit(solution)/shard_map/ppermute | solution.py:332
  8.0 3.8 %shard_map.29 = (f32[8,144,512]{2,1,0:T(8,128)S(1)}, f32[144,512]{1,0:T(8,128)S(1)}, f32[144,512]{1,0:T(8,128)S(1)}, f32[144,512]{1,0:T(8,128)S(1)}) custom-call(f32[16,192,512]{2,1,0:T(8,128)S(1)} %get-tuple-element.32.levelled.refs_0_, bf16[288,192]{1,0:T(8,128)(2,1)S(1)} %get-tuple-element.35.row_weight.mid_weight.refs_3_, ...), custom_call_target="tpu_custom_call" | custom-call | flops 6000000000 | bytes 6000000 | tf_op jit(solution)/shard_map/pallas_call | solution.py:333
  11.8 3.4 %collective-permute-start.2 = (f32[144,512]{1,0:T(8,128)S(1)}, f32[144,512]{1,0:T(8,128)S(1)}, u32[]{:S(2)}, u32[]{:S(2)}) collective-permute-start(f32[144,512]{1,0:T(8,128)S(1)} %get-tuple-element.53), channel_id=1, source_target_pairs={{0,1},{1,2},{2,3},{3,4},{4,5},{5,6},{6,7},{7,8},{8,9},{9,10},{10,1... | collective-permute-start | bytes 884744 | tf_op jit(solution)/shard_map/ppermute | solution.py:336
  15.2 2.4 %collective-permute-done.outer.refs_1_ = f32[16,24,512]{2,1,0:T(8,128)S(1)} collective-permute-done((f32[16,24,512]{2,1,0:T(8,128)S(1)}, f32[16,24,512]{2,1,0:T(8,128)S(1)}, u32[]{:S(2)}, u32[]{:S(2)}) %collective-permute-start) | collective-permute-done | bytes 786464 | tf_op jit(solution)/shard_map/ppermute | solution.py:331
  17.6 0.0 collective-permute-done.1.inner.refs_2_
  17.6 1.4 %shard_map.30 = (f32[8,48,512]{2,1,0:T(8,128)S(1)}, f32[48,512]{1,0:T(8,128)S(1)}, f32[48,512]{1,0:T(8,128)S(1)}, f32[48,512]{1,0:T(8,128)S(1)}, f32[8,144,512]{...) custom-call(f32[16,192,512]{2,1,0:T(8,128)S(1)} %get-tuple-element.3, ...), custom_call_target="tpu_custom_call" | custom-call | flops 2000000000 | bytes 4000000 | tf_op jit(solution)/shard_map/pallas_call | solution.py:338
  18.9 3.4 %collective-permute-start.3 = (f32[48,512]{1,0:T(8,128)S(1)}, f32[48,512]{1,0:T(8,128)S(1)}, u32[]{:S(2)}, u32[]{:S(2)}) collective-permute-start(f32[48,512]{1,0:T(8,128)S(1)} %get-tuple-element.54), channel_id=1, source_target_pairs={{0,1},{1,2},{2,3},{3,4},{4,5},{5,6},{6,7},{7,8},{8,9},{9,10},{10,1... | collective-permute-start | bytes 294920 | tf_op jit(solution)/shard_map/ppermute | solution.py:341
  22.4 4.8 %shard_map.31 = (f32[8,144,512]{2,1,0:T(8,128)S(1)}, f32[144,512]{1,0:T(8,128)S(1)}, f32[144,512]{1,0:T(8,128)S(1)}, f32[8,48,512]{2,1,0:T(8,128)S(1)}, f32[48,512]{1,0:T(8,128)S(1)}, /*index=5*/f32[48,512]{1,0:T(8,128)S(1)}) custom-call(f32[16,192,512]{2,1,0:T(8,128)S(1)} %get-tuple-element.3, ...), custom_call_target="tpu_custom_call", output_to_operand_aliasing={{0}: (11, {}), {1}: (12, {}), {2}: (13, {}), {3}: (14, {}),... | custom-call | flops 8000000000 | bytes 10000000 | tf_op jit(solution)/shard_map/pallas_call | solution.py:342
  27.2 0.0 collective-permute-done.2.before_mid
  27.2 0.0 collective-permute-done.3.before_edge
  27.2 0.1 shard_map.32
  27.4 25.3 %all_to_all.10.pieces = f32[32,24,128]{2,1,0:T(8,128)S(1)} all-to-all(f32[32,24,128]{2,1,0:T(8,128)S(1)} %shard_map.32), channel_id=1, replica_groups=mesh['tile'=8,'depth'=32] {'depth'}, dimensions={0} | all-to-all | bytes 786432 | tf_op jit(solution)/shard_map/all_to_all | solution.py:352
  52.7 20.9 %all_to_all.11.pieces = f32[32,24,128]{2,1,0:T(8,128)S(1)} all-to-all(f32[32,24,128]{2,1,0:T(8,128)S(1)} %shard_map.33), channel_id=1, replica_groups=mesh['tile'=8,'depth'=32] {'depth'}, dimensions={0} | all-to-all | bytes 786432 | tf_op jit(solution)/shard_map/all_to_all | solution.py:354
  73.7 2.8 %shard_map.34 = f32[16,192,512]{2,1,0:T(8,128)} custom-call(f32[8,144,512]{2,1,0:T(8,128)S(1)} %get-tuple-element.49.shallow, f32[8,144,512]{2,1,0:T(8,128)S(1)} %get-tuple-element.50.deep, f32[8,48,512]{2,1,0:T(8,128)S(1)} %get-tuple-element.51.shallow_edge, f32[8,48,512]{2,1,0:T(8,128)S(1)} %get-tuple-element.52.deep_edge, ...), custom_call_target="tpu_custom_call" | custom-call | tf_op jit(solution)/shard_map/pallas_call | solution.py:307
  (1 shorter events, 0.0 us)
Async XLA Ops:
  0.0 1.0 %copy-start = (f32[192,512]{1,0:T(8,128)S(1)}, f32[192,512]{1,0:T(8,128)}, u32[]{:S(2)}) copy-start(f32[192,512]{1,0:T(8,128)} %flat.1) | copy-start | bytes 1179652
  4.3 13.3 %collective-permute-start = (f32[16,24,512]{2,1,0:T(8,128)S(1)}, f32[16,24,512]{2,1,0:T(8,128)S(1)}, u32[]{:S(2)}, u32[]{:S(2)}) collective-permute-start(f32[16,24,512]{2,1,0:T(8,128)S(1)} %get-tuple-element.33), channel_id=1, source_target_pairs={{32,64},{64,32},{96,128},{128,96},{160,192},{192,160},{33,65},{65,... | collective-permute-start | bytes 2359304 | tf_op jit(solution)/shard_map/ppermute | solution.py:331
  6.2 11.4 %collective-permute-start.1 = (f32[16,24,512]{2,1,0:T(8,128)S(1)}, f32[16,24,512]{2,1,0:T(8,128)S(1)}, u32[]{:S(2)}, u32[]{:S(2)}) collective-permute-start(f32[16,24,512]{2,1,0:T(8,128)S(1)} %get-tuple-element.34), channel_id=1, source_target_pairs={{0,32},{32,0},{64,96},{96,64},{128,160},{160,128},{192,224},{224,1... | collective-permute-start | bytes 2359304 | tf_op jit(solution)/shard_map/ppermute | solution.py:332
  11.8 15.5 %collective-permute-start.2 = (f32[144,512]{1,0:T(8,128)S(1)}, f32[144,512]{1,0:T(8,128)S(1)}, u32[]{:S(2)}, u32[]{:S(2)}) collective-permute-start(f32[144,512]{1,0:T(8,128)S(1)} %get-tuple-element.53), channel_id=1, source_target_pairs={{0,1},{1,2},{2,3},{3,4},{4,5},{5,6},{6,7},{7,8},{8,9},{9,10},{10,1... | collective-permute-start | bytes 884744 | tf_op jit(solution)/shard_map/ppermute | solution.py:336
  18.9 8.3 %collective-permute-start.3 = (f32[48,512]{1,0:T(8,128)S(1)}, f32[48,512]{1,0:T(8,128)S(1)}, u32[]{:S(2)}, u32[]{:S(2)}) collective-permute-start(f32[48,512]{1,0:T(8,128)S(1)} %get-tuple-element.54), channel_id=1, source_target_pairs={{0,1},{1,2},{2,3},{3,4},{4,5},{5,6},{6,7},{7,8},{8,9},{9,10},{10,1... | collective-permute-start | bytes 294920 | tf_op jit(solution)/shard_map/ppermute | solution.py:341

commit v9 on v7

--- a/solution.py
+++ b/solution.py
@@ -14,7 +14,8 @@
 STEP = 4
 EDGE_STEP = 8
 GRANT = 20
-LARGE = 44
+LARGE = 36
+FIRST = 56
 
 
 def blur_weights(out_index, in_index, extent, axis):
@@ -86,60 +87,86 @@
     return [blurred[plane * rows:(plane + 1) * rows] for plane in range(len(parts))]
 
 
-def level_kernel(volume, flat, levelled, outward, inward, mid_weight, edge_weight, col_high, col_low, inverse, flat_sem, sems):
+def halo_kernel(volume, flat, outward, inward, shade, sems):
+    rows = flat.shape[0]
+    odd = lax.axis_index("tile") % 2
+    near = rows - RADIUS
+    copies = []
+    for index, (start, ref) in enumerate(((odd * near, outward), (near - odd * near, inward))):
+        at = pl.ds(pl.multiple_of(start, RADIUS), RADIUS)
+        copies.append(pltpu.make_async_copy(flat.at[at], shade.at[index], sems.at[2 * index]))
+        copies.append(pltpu.make_async_copy(volume.at[:, at], ref, sems.at[2 * index + 1]))
+    for copy in copies:
+        copy.start()
+    for copy in copies:
+        copy.wait()
+    for index, ref in enumerate((outward, inward)):
+        inverse = 1.0 / shade[index]
+        for plane in range(ref.shape[0]):
+            ref[plane] = ref[plane] * inverse
+
+
+def middle_step(levelled, row_weight, col_high, col_low, begin):
+    rows = levelled.shape[1]
+    values, parts = [], []
+    for plane in range(STEP):
+        value = levelled[begin + plane]
+        high, low = halves(value)
+        parts.append(row_blur(high, low, row_weight))
+        values.append(value[RADIUS:rows - RADIUS])
+    return values, blur_planes(parts, col_high, col_low)
+
+
+def deep_kernel(
+    volume, flat, levelled, mid_weight, edge_weight, col_high, col_low, out, deepest, later, factor, inverse, flat_sem, sems
+):
     planes, rows, _ = levelled.shape
     first = pltpu.make_async_copy(flat, inverse, flat_sem)
     first.start()
     copies = [pltpu.make_async_copy(volume.at[plane], levelled.at[plane], sems.at[plane]) for plane in range(planes)]
-    for copy in copies:
+    for copy in reversed(copies):
         copy.start()
     fill_weights(rows, mid_weight, edge_weight, col_high, col_low)
     first.wait()
     inverse[...] = 1.0 / inverse[...]
-    odd = lax.axis_index("tile") % 2 == 1
-    for plane in range(planes):
+    later[...] = jnp.ones_like(later)
+    factor[...] = jnp.ones_like(factor)
+
+    def level(plane):
         copies[plane].wait()
-        value = levelled[plane] * inverse[...]
-        levelled[plane] = value
-        top, bottom = value[:RADIUS], value[rows - RADIUS:]
-        outward[plane] = jnp.where(odd, bottom, top)
-        inward[plane] = jnp.where(odd, top, bottom)
-
-
-def middle_steps(levelled, row_weight, col_high, col_low, out, later, factor, begin, fresh, deepest):
-    rows = levelled.shape[1]
+        levelled[plane] = levelled[plane] * inverse[...]
+
+    begin = planes - out.shape[0]
+    for at in reversed(range(0, out.shape[0], STEP)):
+        for plane in range(STEP):
+            level(begin + at + plane)
+        values, blurred = middle_step(levelled, mid_weight, col_high, col_low, begin + at)
+        fresh = at + STEP == out.shape[0]
+        if fresh:
+            deepest[...] = blurred[-1]
+
+        def put(plane, value):
+            out[at + plane] = value
+
+        retreat(blurred, values, True if fresh else None, later, factor, put)
+    for plane in range(begin):
+        level(plane)
+
+
+def middle_steps(levelled, row_weight, col_high, col_low, out, later, factor):
     steps = out.shape[0] // STEP
 
     def one(index, _):
         at = (steps - 1 - index) * STEP
-        values, parts = [], []
-        for plane in range(STEP):
-            value = levelled[begin + at + plane]
-            high, low = halves(value)
-            parts.append(row_blur(high, low, row_weight))
-            values.append(value[RADIUS:rows - RADIUS])
-        blurred = blur_planes(parts, col_high, col_low)
-        start = index == 0 if fresh else None
-        if fresh:
-
-            @pl.when(start)
-            def _():
-                deepest[...] = blurred[-1]
+        values, blurred = middle_step(levelled, row_weight, col_high, col_low, at)
 
         def put(plane, value):
             out[at + plane] = value
 
-        retreat(blurred, values, start, later, factor, put)
+        retreat(blurred, values, None, later, factor, put)
         return 0
 
     lax.fori_loop(0, steps, one, 0)
-
-
-def deep_kernel(levelled, row_weight, col_high, col_low, out, deepest, later, factor):
-    later[...] = jnp.ones_like(later)
-    factor[...] = jnp.ones_like(factor)
-    begin = levelled.shape[0] - out.shape[0]
-    middle_steps(levelled, row_weight, col_high, col_low, out, later, factor, begin, True, deepest)
 
 
 def edge_steps(levelled, outer, inner, row_weight, col_high, col_low, out, later, factor, begin, fresh, deepest):
@@ -194,7 +221,7 @@
     edge_later[...] = later_edge[...]
     edge_factor[...] = factor_edge[...]
     edge_steps(levelled, outer, inner, edge_weight, col_high, col_low, edge_out, edge_later, edge_factor, 0, False, None)
-    middle_steps(levelled, mid_weight, col_high, col_low, mid_out, mid_later, mid_factor, 0, False, None)
+    middle_steps(levelled, mid_weight, col_high, col_low, mid_out, mid_later, mid_factor)
 
 
 def join_kernel(before_mid, before_edge, first_mid, first_edge, factor_mid, factor_edge, pieces):
@@ -265,15 +292,29 @@
     )
 
 
-def level_call(volume, flat):
+def halo_call(volume, flat):
     planes, rows, cols = volume.shape
-    inner, near = rows - 2 * RADIUS, 2 * RADIUS
+    return pl.pallas_call(
+        halo_kernel,
+        in_specs=[pl.BlockSpec(memory_space=pl.ANY)] * 2,
+        out_specs=[pl.BlockSpec(memory_space=pltpu.VMEM)] * 2,
+        out_shape=[shape(planes, RADIUS, cols)] * 2,
+        scratch_shapes=[pltpu.VMEM((2, RADIUS, cols), jnp.float32), pltpu.SemaphoreType.DMA((4,))],
+        compiler_params=params(FIRST),
+        cost_estimate=cost(1e6, 2e6),
+    )(volume, flat)
+
+
+def deep_call(volume, flat):
+    planes, rows, cols = volume.shape
+    inner, near, half = rows - 2 * RADIUS, 2 * RADIUS, planes // 2
     weights = [(2 * inner, rows), (2 * near, 3 * near), (cols, cols), (cols, cols)]
-    outputs = [shape(planes, rows, cols)] + [shape(planes, RADIUS, cols)] * 2
+    outputs = [shape(planes, rows, cols)]
     outputs += [jax.ShapeDtypeStruct(dims, jnp.bfloat16) for dims in weights]
+    outputs += [shape(half, inner, cols)] + [shape(inner, cols)] * 3
     return pl.pallas_call(
-        level_kernel,
-        in_specs=[pl.BlockSpec(memory_space=pltpu.HBM)] * 2,
+        deep_kernel,
+        in_specs=[pl.BlockSpec(memory_space=pl.ANY)] * 2,
         out_specs=[pl.BlockSpec(memory_space=pltpu.VMEM)] * len(outputs),
         out_shape=outputs,
         scratch_shapes=[
@@ -282,7 +323,7 @@
             pltpu.SemaphoreType.DMA((planes,)),
         ],
         compiler_params=params(LARGE),
-        cost_estimate=cost(1e7, 7e6),
+        cost_estimate=cost(6e9, 7e6),
     )(volume, flat)
 
 
@@ -312,12 +353,10 @@
     tiles, slabs = lax.axis_size("tile"), lax.axis_size("depth")
     onward = [(i, i + 1) for i in range(slabs - 1)]
     inner, near, half = rows - 2 * RADIUS, 2 * RADIUS, planes // 2
-    levelled, outward, inward, mid_weight, edge_weight, col_high, col_low = level_call(volume, flat_field)
+    outward, inward = halo_call(volume, flat_field)
     outer = lax.ppermute(outward, "tile", swapped(1, tiles))
     inner_halo = lax.ppermute(inward, "tile", swapped(0, tiles))
-    deep, deepest, later, factor = vmem_call(
-        deep_kernel, 4, [shape(half, inner, cols)] + [shape(inner, cols)] * 3, cost(6e9, 6e6)
-    )(levelled, mid_weight, col_high, col_low)
+    levelled, mid_weight, edge_weight, col_high, col_low, deep, deepest, later, factor = deep_call(volume, flat_field)
     before_mid = lax.ppermute(deepest, "depth", onward)
     deep_edge, deepest_edge, later_edge, factor_edge = vmem_call(
         edge_kernel, 6, [shape(half, near, cols)] + [shape(near, cols)] * 3, cost(2e9, 4e6)

time: 75.4 us -> 75.6 us (level)
  Pallas kernels: 16.2 us -> 19.9 us
  waiting for transfers between devices: 2.4 us -> 0.01 us
  local copies, waits for them, and re-layouts: 1 us -> 0.01 us
    pallas_call x2, Pallas kernels: 7.05 us -> 10.7 us  [the longest x1 7.86 us: deep_call(): pl.pallas_call(deep_kernel, in_specs=[pl.BlockSpec(memory_space=pl.ANY)]...]
    ppermute x1, waiting for transfers between devices: 2.39 us -> 0.01 us  [body(): outer = lax.ppermute(outward, 'tile', swapped(1, tiles))]
    unnamed x2 -> x4, local copies, waits for them, and re-layouts: 1 us -> 0.01 us
  transfers between devices with their start and end apart: 4 -> 4, of which waited for: 1 -> 0; matrix products, arithmetic and copies ran while one was open for 0% -> 0% of each run, Pallas kernels for 13% -> 19%
where the time goes in v9:
time: 75.6 us; the launch traced here: 75.4 us
  blocking collectives  44.8 us (59%)
  Pallas kernels  19.9 us (26%)
  starting transfers between devices  10.6 us (14%)
    all_to_all x1, blocking collectives, body(): mine = lax.all_to_all(pieces, 'depth', 0, 0, tiled=True)  26.5 us
    all_to_all x1, blocking collectives, body(): back = lax.all_to_all(reached, 'depth', 0, 0, tiled=True)  18.3 us
    pallas_call x1, Pallas kernels, deep_call(): pl.pallas_call(deep_kernel, in_specs=[pl.BlockSpec(memory_space=pl.ANY)]...  7.86 us
    pallas_call x1, Pallas kernels, body(): vmem_call(shallow_kernel, 11, outputs, cost(8000000000.0, 10000000.0))  4.81 us
    ppermute x1, starting transfers between devices, body(): before_mid = lax.ppermute(deepest, 'depth', onward)  3.41 us
    ppermute x1, starting transfers between devices, body(): before_edge = lax.ppermute(deepest_edge, 'depth', onward)  3.36 us
    pallas_call x1, Pallas kernels, final_call(): pl.pallas_call(final_kernel, in_specs=[pl.BlockSpec(memory_space=pltpu.VM...  2.82 us
    pallas_call x1, Pallas kernels, halo_call(): pl.pallas_call(halo_kernel, in_specs=[pl.BlockSpec(memory_space=pl.ANY)]...  2.8 us
  transfers between devices with their start and end apart: 4, of which 0 were waited for; matrix products, arithmetic and copies ran while one was open for 0% of the time, Pallas kernels for 19%

profile of v9, /device:TPU:8, one launch (start us, length us, event | category | flops | bytes accessed | tf_op | source)
XLA Modules:
  0.0 75.4 jit_solution(4199091669052490647)
XLA Ops:
  0.0 0.0 copy-start.1
  0.0 0.0 copy-start
  0.0 2.8 %shard_map.29 = (f32[16,24,512]{2,1,0:T(8,128)}, f32[16,24,512]{2,1,0:T(8,128)}) custom-call(f32[16,192,512]{2,1,0:T(8,128)} %volume.3, f32[192,512]{1,0:T(8,128)} %flat.3), custom_call_target="tpu_custom_call" | custom-call | flops 1000000 | bytes 2000000 | tf_op jit(solution)/shard_map/pallas_call | solution.py:297
  2.8 2.1 %collective-permute-start = (f32[16,24,512]{2,1,0:T(8,128)}, f32[16,24,512]{2,1,0:T(8,128)S(1)}, u32[]{:S(2)}, u32[]{:S(2)}) collective-permute-start(f32[16,24,512]{2,1,0:T(8,128)} %get-tuple-element.27), channel_id=1, source_target_pairs={{32,64},{64,32},{96,128},{128,96},{160,192},{192,160},{33,65},{65,... | collective-permute-start | bytes 2359304 | tf_op jit(solution)/shard_map/ppermute | solution.py:357
  4.9 1.8 %collective-permute-start.1 = (f32[16,24,512]{2,1,0:T(8,128)}, f32[16,24,512]{2,1,0:T(8,128)S(1)}, u32[]{:S(2)}, u32[]{:S(2)}) collective-permute-start(f32[16,24,512]{2,1,0:T(8,128)} %get-tuple-element.28), channel_id=1, source_target_pairs={{0,32},{32,0},{64,96},{96,64},{128,160},{160,128},{192,224},{224,1... | collective-permute-start | bytes 2359304 | tf_op jit(solution)/shard_map/ppermute | solution.py:358
  6.6 0.0 copy-done.1
  6.6 0.0 copy-done
  6.6 7.9 %shard_map.28 = (f32[16,192,512]{2,1,0:T(8,128)S(1)}, bf16[288,192]{1,0:T(8,128)(2,1)S(1)}, bf16[96,144]{1,0:T(8,128)(2,1)S(1)}, bf16[512,512]{1,0:T(8,128)(2,1)...) custom-call(f32[16,192,512]{2,1,0:T(8,128)S(1)} %copy-done, ...), custom_call_target="tpu_custom_call" | custom-call | flops 6000000000 | bytes 7000000 | tf_op jit(solution)/shard_map/pallas_call | solution.py:315
  14.5 3.4 %collective-permute-start.2 = (f32[144,512]{1,0:T(8,128)S(1)}, f32[144,512]{1,0:T(8,128)S(1)}, u32[]{:S(2)}, u32[]{:S(2)}) collective-permute-start(f32[144,512]{1,0:T(8,128)S(1)} %get-tuple-element.41), channel_id=1, source_target_pairs={{0,1},{1,2},{2,3},{3,4},{4,5},{5,6},{6,7},{7,8},{8,9},{9,10},{10,1... | collective-permute-start | bytes 884744 | tf_op jit(solution)/shard_map/ppermute | solution.py:360
  17.9 0.0 collective-permute-done.outer
  17.9 0.0 collective-permute-done.1.inner
  18.0 1.4 %shard_map.30 = (f32[8,48,512]{2,1,0:T(8,128)S(1)}, f32[48,512]{1,0:T(8,128)S(1)}, f32[48,512]{1,0:T(8,128)S(1)}, f32[48,512]{1,0:T(8,128)S(1)}) custom-call(f32[16,192,512]{2,1,0:T(8,128)S(1)} %get-tuple-element.26.levelled, f32[16,24,512]{2,1,0:T(8,128)S(1)} %collective-permute-done.outer, f32[16,24,512]{2,1,0:T(8,128)S(1)} %collective-permute-done.1.inner, ...), custom_call_target="tpu_custom_call" | custom-call | flops 2000000000 | bytes 4000000 | tf_op jit(solution)/shard_map/pallas_call | solution.py:361
  19.4 3.4 %collective-permute-start.3 = (f32[48,512]{1,0:T(8,128)S(1)}, f32[48,512]{1,0:T(8,128)S(1)}, u32[]{:S(2)}, u32[]{:S(2)}) collective-permute-start(f32[48,512]{1,0:T(8,128)S(1)} %get-tuple-element.42), channel_id=1, source_target_pairs={{0,1},{1,2},{2,3},{3,4},{4,5},{5,6},{6,7},{7,8},{8,9},{9,10},{10,1... | collective-permute-start | bytes 294920 | tf_op jit(solution)/shard_map/ppermute | solution.py:364
  22.7 4.8 %shard_map.31 = (f32[8,144,512]{2,1,0:T(8,128)S(1)}, f32[144,512]{1,0:T(8,128)S(1)}, f32[144,512]{1,0:T(8,128)S(1)}, f32[8,48,512]{2,1,0:T(8,128)S(1)}, f32[48,512]{1,0:T(8,128)S(1)}, /*index=5*/f32[48,512]{1,0:T(8,128)S(1)}) custom-call(f32[16,192,512]{2,1,0:T(8,128)S(1)} %get-tuple-element.26.levelled, f32[16,24,512]{2,1,0:T(8,128)S(1)} %collective-permute-done.outer, ...), custom_call_target="tpu_custom_call" | custom-call | flops 8000000000 | bytes 10000000 | tf_op jit(solution)/shard_map/pallas_call | solution.py:366
  27.5 0.0 collective-permute-done.2.before_mid
  27.6 0.0 collective-permute-done.3.before_edge
  27.6 0.1 shard_map.32
  27.7 26.5 %all_to_all.10.pieces = f32[32,24,128]{2,1,0:T(8,128)S(1)} all-to-all(f32[32,24,128]{2,1,0:T(8,128)S(1)} %shard_map.32), channel_id=1, replica_groups=mesh['tile'=8,'depth'=32] {'depth'}, dimensions={0} | all-to-all | bytes 786432 | tf_op jit(solution)/shard_map/all_to_all | solution.py:373
  54.3 18.3 %all_to_all.11.pieces = f32[32,24,128]{2,1,0:T(8,128)S(1)} all-to-all(f32[32,24,128]{2,1,0:T(8,128)S(1)} %shard_map.33), channel_id=1, replica_groups=mesh['tile'=8,'depth'=32] {'depth'}, dimensions={0} | all-to-all | bytes 786432 | tf_op jit(solution)/shard_map/all_to_all | solution.py:375
  72.6 2.8 %shard_map.34 = f32[16,192,512]{2,1,0:T(8,128)} custom-call(f32[8,144,512]{2,1,0:T(8,128)S(1)} %get-tuple-element.37.shallow, f32[8,144,512]{2,1,0:T(8,128)S(1)} %get-tuple-element.38.deep, f32[8,48,512]{2,1,0:T(8,128)S(1)} %get-tuple-element.39.shallow_edge, f32[8,48,512]{2,1,0:T(8,128)S(1)} %get-tuple-element.40.deep_edge, ...), custom_call_target="tpu_custom_call" | custom-call | tf_op jit(solution)/shard_map/pallas_call | solution.py:333
  (1 shorter events, 0.0 us)
Async XLA Ops:
  0.0 6.6 %copy-start.1 = (f32[192,512]{1,0:T(8,128)S(1)}, f32[192,512]{1,0:T(8,128)}, u32[]{:S(2)}) copy-start(f32[192,512]{1,0:T(8,128)} %flat.3) | copy-start | bytes 1179652
  0.0 6.6 %copy-start = (f32[16,192,512]{2,1,0:T(8,128)S(1)}, f32[16,192,512]{2,1,0:T(8,128)}, u32[]{:S(2)}) copy-start(f32[16,192,512]{2,1,0:T(8,128)} %volume.3) | copy-start | bytes 18874372
  2.8 15.1 %collective-permute-start = (f32[16,24,512]{2,1,0:T(8,128)}, f32[16,24,512]{2,1,0:T(8,128)S(1)}, u32[]{:S(2)}, u32[]{:S(2)}) collective-permute-start(f32[16,24,512]{2,1,0:T(8,128)} %get-tuple-element.27), channel_id=1, source_target_pairs={{32,64},{64,32},{96,128},{128,96},{160,192},{192,160},{33,65},{65,... | collective-permute-start | bytes 2359304 | tf_op jit(solution)/shard_map/ppermute | solution.py:357
  4.9 13.1 %collective-permute-start.1 = (f32[16,24,512]{2,1,0:T(8,128)}, f32[16,24,512]{2,1,0:T(8,128)S(1)}, u32[]{:S(2)}, u32[]{:S(2)}) collective-permute-start(f32[16,24,512]{2,1,0:T(8,128)} %get-tuple-element.28), channel_id=1, source_target_pairs={{0,32},{32,0},{64,96},{96,64},{128,160},{160,128},{192,224},{224,1... | collective-permute-start | bytes 2359304 | tf_op jit(solution)/shard_map/ppermute | solution.py:358
  14.5 13.0 %collective-permute-start.2 = (f32[144,512]{1,0:T(8,128)S(1)}, f32[144,512]{1,0:T(8,128)S(1)}, u32[]{:S(2)}, u32[]{:S(2)}) collective-permute-start(f32[144,512]{1,0:T(8,128)S(1)} %get-tuple-element.41), channel_id=1, source_target_pairs={{0,1},{1,2},{2,3},{3,4},{4,5},{5,6},{6,7},{7,8},{8,9},{9,10},{10,1... | collective-permute-start | bytes 884744 | tf_op jit(solution)/shard_map/ppermute | solution.py:360
  19.4 8.2 %collective-permute-start.3 = (f32[48,512]{1,0:T(8,128)S(1)}, f32[48,512]{1,0:T(8,128)S(1)}, u32[]{:S(2)}, u32[]{:S(2)}) collective-permute-start(f32[48,512]{1,0:T(8,128)S(1)} %get-tuple-element.42), channel_id=1, source_target_pairs={{0,1},{1,2},{2,3},{3,4},{4,5},{5,6},{6,7},{7,8},{8,9},{9,10},{10,1... | collective-permute-start | bytes 294920 | tf_op jit(solution)/shard_map/ppermute | solution.py:364

commit v10 on v9

--- a/solution.py
+++ b/solution.py
@@ -14,7 +14,6 @@
 STEP = 4
 EDGE_STEP = 8
 GRANT = 20
-LARGE = 36
 FIRST = 56
 
 
@@ -106,41 +105,26 @@
             ref[plane] = ref[plane] * inverse
 
 
-def middle_step(levelled, row_weight, col_high, col_low, begin):
-    rows = levelled.shape[1]
+def middle_step(volume, inverse, row_weight, col_high, col_low, begin):
+    rows = volume.shape[1]
     values, parts = [], []
     for plane in range(STEP):
-        value = levelled[begin + plane]
+        value = volume[begin + plane] * inverse[...]
         high, low = halves(value)
         parts.append(row_blur(high, low, row_weight))
         values.append(value[RADIUS:rows - RADIUS])
     return values, blur_planes(parts, col_high, col_low)
 
 
-def deep_kernel(
-    volume, flat, levelled, mid_weight, edge_weight, col_high, col_low, out, deepest, later, factor, inverse, flat_sem, sems
-):
-    planes, rows, _ = levelled.shape
-    first = pltpu.make_async_copy(flat, inverse, flat_sem)
-    first.start()
-    copies = [pltpu.make_async_copy(volume.at[plane], levelled.at[plane], sems.at[plane]) for plane in range(planes)]
-    for copy in reversed(copies):
-        copy.start()
+def deep_kernel(volume, flat, inverse, mid_weight, edge_weight, col_high, col_low, out, deepest, later, factor):
+    planes, rows, _ = volume.shape
     fill_weights(rows, mid_weight, edge_weight, col_high, col_low)
-    first.wait()
-    inverse[...] = 1.0 / inverse[...]
+    inverse[...] = 1.0 / flat[...]
     later[...] = jnp.ones_like(later)
     factor[...] = jnp.ones_like(factor)
-
-    def level(plane):
-        copies[plane].wait()
-        levelled[plane] = levelled[plane] * inverse[...]
-
     begin = planes - out.shape[0]
     for at in reversed(range(0, out.shape[0], STEP)):
-        for plane in range(STEP):
-            level(begin + at + plane)
-        values, blurred = middle_step(levelled, mid_weight, col_high, col_low, begin + at)
+        values, blurred = middle_step(volume, inverse, mid_weight, col_high, col_low, begin + at)
         fresh = at + STEP == out.shape[0]
         if fresh:
             deepest[...] = blurred[-1]
@@ -149,16 +133,14 @@
             out[at + plane] = value
 
         retreat(blurred, values, True if fresh else None, later, factor, put)
-    for plane in range(begin):
-        level(plane)
-
-
-def middle_steps(levelled, row_weight, col_high, col_low, out, later, factor):
+
+
+def middle_steps(volume, inverse, row_weight, col_high, col_low, out, later, factor):
     steps = out.shape[0] // STEP
 
     def one(index, _):
         at = (steps - 1 - index) * STEP
-        values, blurred = middle_step(levelled, row_weight, col_high, col_low, at)
+        values, blurred = middle_step(volume, inverse, row_weight, col_high, col_low, at)
 
         def put(plane, value):
             out[at + plane] = value
@@ -169,9 +151,9 @@
     lax.fori_loop(0, steps, one, 0)
 
 
-def edge_steps(levelled, outer, inner, row_weight, col_high, col_low, out, later, factor, begin, fresh, deepest):
+def edge_steps(volume, inverse, outer, inner, row_weight, col_high, col_low, out, later, factor, begin, fresh, deepest):
     near = 2 * RADIUS
-    rows = levelled.shape[1]
+    rows = volume.shape[1]
     steps = out.shape[0] // EDGE_STEP
     odd = lax.axis_index("tile") % 2 == 1
 
@@ -180,8 +162,8 @@
         values, parts = [], []
         for plane in range(EDGE_STEP):
             here = begin + at + plane
-            upper = levelled[here, :near]
-            lower = levelled[here, rows - near:]
+            upper = volume[here, :near] * inverse[:near]
+            lower = volume[here, rows - near:] * inverse[rows - near:]
             above = jnp.where(odd, inner[here], outer[here])
             below = jnp.where(odd, outer[here], inner[here])
             value = jnp.concatenate([above, upper, lower, below], axis=0)
@@ -205,23 +187,23 @@
     lax.fori_loop(0, steps, one, 0)
 
 
-def edge_kernel(levelled, outer, inner, row_weight, col_high, col_low, out, deepest, later, factor):
+def edge_kernel(volume, inverse, outer, inner, row_weight, col_high, col_low, out, deepest, later, factor):
     later[...] = jnp.ones_like(later)
     factor[...] = jnp.ones_like(factor)
-    begin = levelled.shape[0] - out.shape[0]
-    edge_steps(levelled, outer, inner, row_weight, col_high, col_low, out, later, factor, begin, True, deepest)
+    begin = volume.shape[0] - out.shape[0]
+    edge_steps(volume, inverse, outer, inner, row_weight, col_high, col_low, out, later, factor, begin, True, deepest)
 
 
 def shallow_kernel(
-    levelled, outer, inner, mid_weight, edge_weight, col_high, col_low, later_mid, factor_mid, later_edge, factor_edge,
+    volume, inverse, outer, inner, mid_weight, edge_weight, col_high, col_low, later_mid, factor_mid, later_edge, factor_edge,
     mid_out, mid_later, mid_factor, edge_out, edge_later, edge_factor,
 ):
     mid_later[...] = later_mid[...]
     mid_factor[...] = factor_mid[...]
     edge_later[...] = later_edge[...]
     edge_factor[...] = factor_edge[...]
-    edge_steps(levelled, outer, inner, edge_weight, col_high, col_low, edge_out, edge_later, edge_factor, 0, False, None)
-    middle_steps(levelled, mid_weight, col_high, col_low, mid_out, mid_later, mid_factor)
+    edge_steps(volume, inverse, outer, inner, edge_weight, col_high, col_low, edge_out, edge_later, edge_factor, 0, False, None)
+    middle_steps(volume, inverse, mid_weight, col_high, col_low, mid_out, mid_later, mid_factor)
 
 
 def join_kernel(before_mid, before_edge, first_mid, first_edge, factor_mid, factor_edge, pieces):
@@ -309,22 +291,10 @@
     planes, rows, cols = volume.shape
     inner, near, half = rows - 2 * RADIUS, 2 * RADIUS, planes // 2
     weights = [(2 * inner, rows), (2 * near, 3 * near), (cols, cols), (cols, cols)]
-    outputs = [shape(planes, rows, cols)]
+    outputs = [shape(rows, cols)]
     outputs += [jax.ShapeDtypeStruct(dims, jnp.bfloat16) for dims in weights]
     outputs += [shape(half, inner, cols)] + [shape(inner, cols)] * 3
-    return pl.pallas_call(
-        deep_kernel,
-        in_specs=[pl.BlockSpec(memory_space=pl.ANY)] * 2,
-        out_specs=[pl.BlockSpec(memory_space=pltpu.VMEM)] * len(outputs),
-        out_shape=outputs,
-        scratch_shapes=[
-            pltpu.VMEM((rows, cols), jnp.float32),
-            pltpu.SemaphoreType.DMA,
-            pltpu.SemaphoreType.DMA((planes,)),
-        ],
-        compiler_params=params(LARGE),
-        cost_estimate=cost(6e9, 7e6),
-    )(volume, flat)
+    return vmem_call(deep_kernel, 2, outputs, cost(6e9, 7e6))(volume, flat)
 
 
 def final_call(shallow, deep, shallow_edge, deep_edge, pieces):
@@ -356,15 +326,15 @@
     outward, inward = halo_call(volume, flat_field)
     outer = lax.ppermute(outward, "tile", swapped(1, tiles))
     inner_halo = lax.ppermute(inward, "tile", swapped(0, tiles))
-    levelled, mid_weight, edge_weight, col_high, col_low, deep, deepest, later, factor = deep_call(volume, flat_field)
+    inverse, mid_weight, edge_weight, col_high, col_low, deep, deepest, later, factor = deep_call(volume, flat_field)
     before_mid = lax.ppermute(deepest, "depth", onward)
     deep_edge, deepest_edge, later_edge, factor_edge = vmem_call(
-        edge_kernel, 6, [shape(half, near, cols)] + [shape(near, cols)] * 3, cost(2e9, 4e6)
-    )(levelled, outer, inner_halo, edge_weight, col_high, col_low)
+        edge_kernel, 7, [shape(half, near, cols)] + [shape(near, cols)] * 3, cost(2e9, 4e6)
+    )(volume, inverse, outer, inner_halo, edge_weight, col_high, col_low)
     before_edge = lax.ppermute(deepest_edge, "depth", onward)
     outputs = [shape(half, inner, cols)] + [shape(inner, cols)] * 2 + [shape(half, near, cols)] + [shape(near, cols)] * 2
-    shallow, first_mid, factor_mid, shallow_edge, first_edge, factor_edge = vmem_call(shallow_kernel, 11, outputs, cost(8e9, 1e7))(
-        levelled, outer, inner_halo, mid_weight, edge_weight, col_high, col_low, later, factor, later_edge, factor_edge
+    shallow, first_mid, factor_mid, shallow_edge, first_edge, factor_edge = vmem_call(shallow_kernel, 12, outputs, cost(8e9, 1e7))(
+        volume, inverse, outer, inner_halo, mid_weight, edge_weight, col_high, col_low, later, factor, later_edge, factor_edge
     )
     traded = shape(slabs, RADIUS, cols // 4)
     (pieces,) = vmem_call(join_kernel, 6, [traded], cost(1e6, 2e6))(

time: 75.6 us -> 74.5 us (0.985)
  Pallas kernels: 19.9 us -> 15.9 us
  waiting for transfers between devices: 0.01 us -> 2.75 us
    pallas_call x3, Pallas kernels: 14.1 us -> 10.1 us  [the longest x1 5.04 us: body(): vmem_call(shallow_kernel, 12, outputs, cost(8000000000.0, 10000000.0))]
    ppermute x1, waiting for transfers between devices: 0.01 us -> 2.74 us  [body(): outer = lax.ppermute(outward, 'tile', swapped(1, tiles))]
  transfers between devices with their start and end apart: 4 -> 4, of which waited for: 0 -> 1; matrix products, arithmetic and copies ran while one was open for 0% -> 0% of each run, Pallas kernels for 19% -> 14%
where the time goes in v10:
time: 74.5 us; the launch traced here: 74.3 us
  blocking collectives  44.9 us (60%)
  Pallas kernels  15.9 us (21%)
  starting transfers between devices  10.6 us (14%)
  waiting for transfers between devices  2.75 us (4%)
    all_to_all x1, blocking collectives, body(): mine = lax.all_to_all(pieces, 'depth', 0, 0, tiled=True)  26.3 us
    all_to_all x1, blocking collectives, body(): back = lax.all_to_all(reached, 'depth', 0, 0, tiled=True)  18.6 us
    pallas_call x1, Pallas kernels, body(): vmem_call(shallow_kernel, 12, outputs, cost(8000000000.0, 10000000.0))  5.04 us
    pallas_call x1, Pallas kernels, deep_call(): vmem_call(deep_kernel, 2, outputs, cost(6000000000.0, 7000000.0))  3.65 us
    ppermute x1, starting transfers between devices, body(): before_mid = lax.ppermute(deepest, 'depth', onward)  3.41 us
    ppermute x1, starting transfers between devices, body(): before_edge = lax.ppermute(deepest_edge, 'depth', onward)  3.4 us
    pallas_call x1, Pallas kernels, final_call(): pl.pallas_call(final_kernel, in_specs=[pl.BlockSpec(memory_space=pltpu.VM...  2.82 us
    pallas_call x1, Pallas kernels, halo_call(): pl.pallas_call(halo_kernel, in_specs=[pl.BlockSpec(memory_space=pl.ANY)]...  2.8 us
  transfers between devices with their start and end apart: 4, of which 1 were waited for; matrix products, arithmetic and copies ran while one was open for 0% of the time, Pallas kernels for 14%

profile of v10, /device:TPU:8, one launch (start us, length us, event | category | flops | bytes accessed | tf_op | source)
XLA Modules:
  0.0 74.3 jit_solution(15427808412433567440)
XLA Ops:
  0.0 0.0 copy-start
  0.0 0.0 copy-start.1
  0.0 2.8 %shard_map.29 = (f32[16,24,512]{2,1,0:T(8,128)}, f32[16,24,512]{2,1,0:T(8,128)}) custom-call(f32[16,192,512]{2,1,0:T(8,128)} %volume.7, f32[192,512]{1,0:T(8,128)} %flat.3), custom_call_target="tpu_custom_call" | custom-call | flops 1000000 | bytes 2000000 | tf_op jit(solution)/shard_map/pallas_call | solution.py:279
  2.8 2.1 %collective-permute-start = (f32[16,24,512]{2,1,0:T(8,128)}, f32[16,24,512]{2,1,0:T(8,128)S(1)}, u32[]{:S(2)}, u32[]{:S(2)}) collective-permute-start(f32[16,24,512]{2,1,0:T(8,128)} %get-tuple-element.27), channel_id=1, source_target_pairs={{32,64},{64,32},{96,128},{128,96},{160,192},{192,160},{33,65},{65,... | collective-permute-start | bytes 2359304 | tf_op jit(solution)/shard_map/ppermute | solution.py:327
  4.9 1.8 %collective-permute-start.1 = (f32[16,24,512]{2,1,0:T(8,128)}, f32[16,24,512]{2,1,0:T(8,128)S(1)}, u32[]{:S(2)}, u32[]{:S(2)}) collective-permute-start(f32[16,24,512]{2,1,0:T(8,128)} %get-tuple-element.28), channel_id=1, source_target_pairs={{0,32},{32,0},{64,96},{96,64},{128,160},{160,128},{192,224},{224,1... | collective-permute-start | bytes 2359304 | tf_op jit(solution)/shard_map/ppermute | solution.py:328
  6.6 0.0 copy-done
  6.6 0.0 copy-done.1
  6.6 3.7 %shard_map.28 = (f32[192,512]{1,0:T(8,128)S(1)}, bf16[288,192]{1,0:T(8,128)(2,1)S(1)}, bf16[96,144]{1,0:T(8,128)(2,1)S(1)}, bf16[512,512]{1,0:T(8,128)(2,1)S(1)}...) custom-call(f32[16,192,512]{2,1,0:T(8,128)S(1)} %copy-done, ...), custom_call_target="tpu_custom_call" | custom-call | flops 6000000000 | bytes 7000000 | tf_op jit(solution)/shard_map/pallas_call | solution.py:297
  10.3 3.4 %collective-permute-start.2 = (f32[144,512]{1,0:T(8,128)S(1)}, f32[144,512]{1,0:T(8,128)S(1)}, u32[]{:S(2)}, u32[]{:S(2)}) collective-permute-start(f32[144,512]{1,0:T(8,128)S(1)} %get-tuple-element.41), channel_id=1, source_target_pairs={{0,1},{1,2},{2,3},{3,4},{4,5},{5,6},{6,7},{7,8},{8,9},{9,10},{10,1... | collective-permute-start | bytes 884744 | tf_op jit(solution)/shard_map/ppermute | solution.py:330
  13.7 2.7 %collective-permute-done.outer = f32[16,24,512]{2,1,0:T(8,128)S(1)} collective-permute-done((f32[16,24,512]{2,1,0:T(8,128)}, f32[16,24,512]{2,1,0:T(8,128)S(1)}, u32[]{:S(2)}, u32[]{:S(2)}) %collective-permute-start) | collective-permute-done | bytes 786464 | tf_op jit(solution)/shard_map/ppermute | solution.py:327
  16.5 0.0 collective-permute-done.1.inner
  16.5 1.4 %shard_map.30 = (f32[8,48,512]{2,1,0:T(8,128)S(1)}, f32[48,512]{1,0:T(8,128)S(1)}, f32[48,512]{1,0:T(8,128)S(1)}, f32[48,512]{1,0:T(8,128)S(1)}) custom-call(f32[16,192,512]{2,1,0:T(8,128)S(1)} %copy-done, f32[192,512]{1,0:T(8,128)S(1)} %get-tuple-element.26.inverse, f32[16,24,512]{2,1,0:T(8,128)S(1)} %collective-permute-done.outer, ...), custom_call_target="tpu_custom_call" | custom-call | flops 2000000000 | bytes 4000000 | tf_op jit(solution)/shard_map/pallas_call | solution.py:331
  17.9 3.4 %collective-permute-start.3 = (f32[48,512]{1,0:T(8,128)S(1)}, f32[48,512]{1,0:T(8,128)S(1)}, u32[]{:S(2)}, u32[]{:S(2)}) collective-permute-start(f32[48,512]{1,0:T(8,128)S(1)} %get-tuple-element.42), channel_id=1, source_target_pairs={{0,1},{1,2},{2,3},{3,4},{4,5},{5,6},{6,7},{7,8},{8,9},{9,10},{10,1... | collective-permute-start | bytes 294920 | tf_op jit(solution)/shard_map/ppermute | solution.py:334
  21.3 5.0 %shard_map.31 = (f32[8,144,512]{2,1,0:T(8,128)S(1)}, f32[144,512]{1,0:T(8,128)S(1)}, f32[144,512]{1,0:T(8,128)S(1)}, f32[8,48,512]{2,1,0:T(8,128)S(1)}, f32[48,512]{1,0:T(8,128)S(1)}, /*index=5*/f32[48,512]{1,0:T(8,128)S(1)}) custom-call(f32[16,192,512]{2,1,0:T(8,128)S(1)} %copy-done, f32[192,512]{1,0:T(8,128)S(1)} %get-tuple-element.26.inverse, ...), custom_call_target="tpu_custom_call" | custom-call | flops 8000000000 | bytes 10000000 | tf_op jit(solution)/shard_map/pallas_call | solution.py:336
  26.4 0.0 collective-permute-done.2.before_mid
  26.4 0.0 collective-permute-done.3.before_edge
  26.4 0.1 shard_map.32
  26.5 26.3 %all_to_all.10.pieces = f32[32,24,128]{2,1,0:T(8,128)S(1)} all-to-all(f32[32,24,128]{2,1,0:T(8,128)S(1)} %shard_map.32), channel_id=1, replica_groups=mesh['tile'=8,'depth'=32] {'depth'}, dimensions={0} | all-to-all | bytes 786432 | tf_op jit(solution)/shard_map/all_to_all | solution.py:343
  52.9 18.6 %all_to_all.11.pieces = f32[32,24,128]{2,1,0:T(8,128)S(1)} all-to-all(f32[32,24,128]{2,1,0:T(8,128)S(1)} %shard_map.33), channel_id=1, replica_groups=mesh['tile'=8,'depth'=32] {'depth'}, dimensions={0} | all-to-all | bytes 786432 | tf_op jit(solution)/shard_map/all_to_all | solution.py:345
  71.4 2.8 %shard_map.34 = f32[16,192,512]{2,1,0:T(8,128)} custom-call(f32[8,144,512]{2,1,0:T(8,128)S(1)} %get-tuple-element.37.shallow, f32[8,144,512]{2,1,0:T(8,128)S(1)} %get-tuple-element.38.deep, f32[8,48,512]{2,1,0:T(8,128)S(1)} %get-tuple-element.39.shallow_edge, f32[8,48,512]{2,1,0:T(8,128)S(1)} %get-tuple-element.40.deep_edge, ...), custom_call_target="tpu_custom_call" | custom-call | tf_op jit(solution)/shard_map/pallas_call | solution.py:303
  (1 shorter events, 0.0 us)
Async XLA Ops:
  0.0 6.6 %copy-start = (f32[16,192,512]{2,1,0:T(8,128)S(1)}, f32[16,192,512]{2,1,0:T(8,128)}, u32[]{:S(2)}) copy-start(f32[16,192,512]{2,1,0:T(8,128)} %volume.7) | copy-start | bytes 18874372
  0.0 6.6 %copy-start.1 = (f32[192,512]{1,0:T(8,128)S(1)}, f32[192,512]{1,0:T(8,128)}, u32[]{:S(2)}) copy-start(f32[192,512]{1,0:T(8,128)} %flat.3) | copy-start | bytes 1179652
  2.8 13.7 %collective-permute-start = (f32[16,24,512]{2,1,0:T(8,128)}, f32[16,24,512]{2,1,0:T(8,128)S(1)}, u32[]{:S(2)}, u32[]{:S(2)}) collective-permute-start(f32[16,24,512]{2,1,0:T(8,128)} %get-tuple-element.27), channel_id=1, source_target_pairs={{32,64},{64,32},{96,128},{128,96},{160,192},{192,160},{33,65},{65,... | collective-permute-start | bytes 2359304 | tf_op jit(solution)/shard_map/ppermute | solution.py:327
  4.9 11.6 %collective-permute-start.1 = (f32[16,24,512]{2,1,0:T(8,128)}, f32[16,24,512]{2,1,0:T(8,128)S(1)}, u32[]{:S(2)}, u32[]{:S(2)}) collective-permute-start(f32[16,24,512]{2,1,0:T(8,128)} %get-tuple-element.28), channel_id=1, source_target_pairs={{0,32},{32,0},{64,96},{96,64},{128,160},{160,128},{192,224},{224,1... | collective-permute-start | bytes 2359304 | tf_op jit(solution)/shard_map/ppermute | solution.py:328
  10.3 16.1 %collective-permute-start.2 = (f32[144,512]{1,0:T(8,128)S(1)}, f32[144,512]{1,0:T(8,128)S(1)}, u32[]{:S(2)}, u32[]{:S(2)}) collective-permute-start(f32[144,512]{1,0:T(8,128)S(1)} %get-tuple-element.41), channel_id=1, source_target_pairs={{0,1},{1,2},{2,3},{3,4},{4,5},{5,6},{6,7},{7,8},{8,9},{9,10},{10,1... | collective-permute-start | bytes 884744 | tf_op jit(solution)/shard_map/ppermute | solution.py:330
  17.9 8.5 %collective-permute-start.3 = (f32[48,512]{1,0:T(8,128)S(1)}, f32[48,512]{1,0:T(8,128)S(1)}, u32[]{:S(2)}, u32[]{:S(2)}) collective-permute-start(f32[48,512]{1,0:T(8,128)S(1)} %get-tuple-element.42), channel_id=1, source_target_pairs={{0,1},{1,2},{2,3},{3,4},{4,5},{5,6},{6,7},{7,8},{8,9},{9,10},{10,1... | collective-permute-start | bytes 294920 | tf_op jit(solution)/shard_map/ppermute | solution.py:334

commit v11 on v10

--- a/solution.py
+++ b/solution.py
@@ -1,3 +1,4 @@
+import functools
 import jax
 import jax.numpy as jnp
 from jax import lax
@@ -86,23 +87,18 @@
     return [blurred[plane * rows:(plane + 1) * rows] for plane in range(len(parts))]
 
 
-def halo_kernel(volume, flat, outward, inward, shade, sems):
+def halo_kernel(lower, volume, flat, out, shade, sems):
     rows = flat.shape[0]
-    odd = lax.axis_index("tile") % 2
-    near = rows - RADIUS
-    copies = []
-    for index, (start, ref) in enumerate(((odd * near, outward), (near - odd * near, inward))):
-        at = pl.ds(pl.multiple_of(start, RADIUS), RADIUS)
-        copies.append(pltpu.make_async_copy(flat.at[at], shade.at[index], sems.at[2 * index]))
-        copies.append(pltpu.make_async_copy(volume.at[:, at], ref, sems.at[2 * index + 1]))
+    start = jnp.where(lax.axis_index("tile") % 2 == lower, rows - RADIUS, 0)
+    at = pl.ds(pl.multiple_of(start, RADIUS), RADIUS)
+    copies = [pltpu.make_async_copy(flat.at[at], shade, sems.at[0]), pltpu.make_async_copy(volume.at[:, at], out, sems.at[1])]
     for copy in copies:
         copy.start()
     for copy in copies:
         copy.wait()
-    for index, ref in enumerate((outward, inward)):
-        inverse = 1.0 / shade[index]
-        for plane in range(ref.shape[0]):
-            ref[plane] = ref[plane] * inverse
+    inverse = 1.0 / shade[...]
+    for plane in range(out.shape[0]):
+        out[plane] = out[plane] * inverse
 
 
 def middle_step(volume, inverse, row_weight, col_high, col_low, begin):
@@ -274,14 +270,14 @@
     )
 
 
-def halo_call(volume, flat):
+def halo_call(volume, flat, lower):
     planes, rows, cols = volume.shape
     return pl.pallas_call(
-        halo_kernel,
+        functools.partial(halo_kernel, lower),
         in_specs=[pl.BlockSpec(memory_space=pl.ANY)] * 2,
-        out_specs=[pl.BlockSpec(memory_space=pltpu.VMEM)] * 2,
-        out_shape=[shape(planes, RADIUS, cols)] * 2,
-        scratch_shapes=[pltpu.VMEM((2, RADIUS, cols), jnp.float32), pltpu.SemaphoreType.DMA((4,))],
+        out_specs=pl.BlockSpec(memory_space=pltpu.VMEM),
+        out_shape=shape(planes, RADIUS, cols),
+        scratch_shapes=[pltpu.VMEM((RADIUS, cols), jnp.float32), pltpu.SemaphoreType.DMA((2,))],
         compiler_params=params(FIRST),
         cost_estimate=cost(1e6, 2e6),
     )(volume, flat)
@@ -323,9 +319,8 @@
     tiles, slabs = lax.axis_size("tile"), lax.axis_size("depth")
     onward = [(i, i + 1) for i in range(slabs - 1)]
     inner, near, half = rows - 2 * RADIUS, 2 * RADIUS, planes // 2
-    outward, inward = halo_call(volume, flat_field)
-    outer = lax.ppermute(outward, "tile", swapped(1, tiles))
-    inner_halo = lax.ppermute(inward, "tile", swapped(0, tiles))
+    outer = lax.ppermute(halo_call(volume, flat_field, 1), "tile", swapped(1, tiles))
+    inner_halo = lax.ppermute(halo_call(volume, flat_field, 0), "tile", swapped(0, tiles))
     inverse, mid_weight, edge_weight, col_high, col_low, deep, deepest, later, factor = deep_call(volume, flat_field)
     before_mid = lax.ppermute(deepest, "depth", onward)
     deep_edge, deepest_edge, later_edge, factor_edge = vmem_call(

time: 74.5 us -> 73.8 us (level)
  waiting for transfers between devices: 2.75 us -> 0.6 us
  Pallas kernels: 15.9 us -> 17.5 us
    ppermute x2, waiting for transfers between devices: 2.74 us -> 0.59 us  [the longest x1 0.59 us: body(): lax.ppermute(halo_call(volume, flat_field, 1), 'tile', swapped(1, tiles))]
    pallas_call x1 -> x2, Pallas kernels: 2.8 us -> 4.4 us  [halo_call(): pl.pallas_call(functools.partial(halo_kernel, lower), in_specs=[pl.BlockS...]
  transfers between devices with their start and end apart: 4 -> 4, of which waited for: 1 -> 1; matrix products, arithmetic and copies ran while one was open for 0% -> 0% of each run, Pallas kernels for 14% -> 17%
where the time goes in v11:
time: 73.8 us; the launch traced here: 73.5 us
  blocking collectives  44.7 us (61%)
  Pallas kernels  17.5 us (24%)
  starting transfers between devices  10.6 us (14%)
    all_to_all x1, blocking collectives, body(): mine = lax.all_to_all(pieces, 'depth', 0, 0, tiled=True)  26.2 us
    all_to_all x1, blocking collectives, body(): back = lax.all_to_all(reached, 'depth', 0, 0, tiled=True)  18.5 us
    pallas_call x1, Pallas kernels, body(): vmem_call(shallow_kernel, 12, outputs, cost(8000000000.0, 10000000.0))  5.03 us
    pallas_call x2, Pallas kernels, halo_call(): pl.pallas_call(functools.partial(halo_kernel, lower), in_specs=[pl.BlockS...  4.4 us
    pallas_call x1, Pallas kernels, deep_call(): vmem_call(deep_kernel, 2, outputs, cost(6000000000.0, 7000000.0))  3.66 us
    ppermute x1, starting transfers between devices, body(): before_mid = lax.ppermute(deepest, 'depth', onward)  3.41 us
    ppermute x1, starting transfers between devices, body(): before_edge = lax.ppermute(deepest_edge, 'depth', onward)  3.41 us
    pallas_call x1, Pallas kernels, final_call(): pl.pallas_call(final_kernel, in_specs=[pl.BlockSpec(memory_space=pltpu.VM...  2.82 us
  transfers between devices with their start and end apart: 4, of which 1 were waited for; matrix products, arithmetic and copies ran while one was open for 0% of the time, Pallas kernels for 17%

profile of v11, /device:TPU:8, one launch (start us, length us, event | category | flops | bytes accessed | tf_op | source)
XLA Modules:
  0.0 73.5 jit_solution(15722133362425104762)
XLA Ops:
  0.0 0.0 copy-start
  0.0 0.0 copy-start.1
  0.0 2.3 %shard_map.29 = f32[16,24,512]{2,1,0:T(8,128)} custom-call(f32[16,192,512]{2,1,0:T(8,128)} %volume.9, f32[192,512]{1,0:T(8,128)} %flat.5), custom_call_target="tpu_custom_call" | custom-call | flops 1000000 | bytes 2000000 | tf_op jit(solution)/shard_map/pallas_call | solution.py:275
  2.3 2.1 %collective-permute-start = (f32[16,24,512]{2,1,0:T(8,128)}, f32[16,24,512]{2,1,0:T(8,128)S(1)}, u32[]{:S(2)}, u32[]{:S(2)}) collective-permute-start(f32[16,24,512]{2,1,0:T(8,128)} %shard_map.29), channel_id=1, source_target_pairs={{32,64},{64,32},{96,128},{128,96},{160,192},{192,160},{33,65},{65,... | collective-permute-start | bytes 2359304 | tf_op jit(solution)/shard_map/ppermute | solution.py:322
  4.3 2.1 %shard_map.30 = f32[16,24,512]{2,1,0:T(8,128)} custom-call(f32[16,192,512]{2,1,0:T(8,128)} %volume.9, f32[192,512]{1,0:T(8,128)} %flat.5), custom_call_target="tpu_custom_call" | custom-call | flops 1000000 | bytes 2000000 | tf_op jit(solution)/shard_map/pallas_call | solution.py:275
  6.5 1.8 %collective-permute-start.1 = (f32[16,24,512]{2,1,0:T(8,128)}, f32[16,24,512]{2,1,0:T(8,128)S(1)}, u32[]{:S(2)}, u32[]{:S(2)}) collective-permute-start(f32[16,24,512]{2,1,0:T(8,128)} %shard_map.30), channel_id=1, source_target_pairs={{0,32},{32,0},{64,96},{96,64},{128,160},{160,128},{192,224},{224,1... | collective-permute-start | bytes 2359304 | tf_op jit(solution)/shard_map/ppermute | solution.py:323
  8.2 0.0 copy-done
  8.2 0.0 copy-done.1
  8.2 3.7 %shard_map.28 = (f32[192,512]{1,0:T(8,128)S(1)}, bf16[288,192]{1,0:T(8,128)(2,1)S(1)}, bf16[96,144]{1,0:T(8,128)(2,1)S(1)}, bf16[512,512]{1,0:T(8,128)(2,1)S(1)}...) custom-call(f32[16,192,512]{2,1,0:T(8,128)S(1)} %copy-done, ...), custom_call_target="tpu_custom_call" | custom-call | flops 6000000000 | bytes 7000000 | tf_op jit(solution)/shard_map/pallas_call | solution.py:293
  11.9 3.4 %collective-permute-start.2 = (f32[144,512]{1,0:T(8,128)S(1)}, f32[144,512]{1,0:T(8,128)S(1)}, u32[]{:S(2)}, u32[]{:S(2)}) collective-permute-start(f32[144,512]{1,0:T(8,128)S(1)} %get-tuple-element.37), channel_id=1, source_target_pairs={{0,1},{1,2},{2,3},{3,4},{4,5},{5,6},{6,7},{7,8},{8,9},{9,10},{10,1... | collective-permute-start | bytes 884744 | tf_op jit(solution)/shard_map/ppermute | solution.py:325
  15.3 0.6 collective-permute-done.outer
  15.9 0.0 collective-permute-done.1.inner
  15.9 1.4 %shard_map.31 = (f32[8,48,512]{2,1,0:T(8,128)S(1)}, f32[48,512]{1,0:T(8,128)S(1)}, f32[48,512]{1,0:T(8,128)S(1)}, f32[48,512]{1,0:T(8,128)S(1)}) custom-call(f32[16,192,512]{2,1,0:T(8,128)S(1)} %copy-done, f32[192,512]{1,0:T(8,128)S(1)} %get-tuple-element.24.inverse, f32[16,24,512]{2,1,0:T(8,128)S(1)} %collective-permute-done.outer, ...), custom_call_target="tpu_custom_call" | custom-call | flops 2000000000 | bytes 4000000 | tf_op jit(solution)/shard_map/pallas_call | solution.py:326
  17.4 3.4 %collective-permute-start.3 = (f32[48,512]{1,0:T(8,128)S(1)}, f32[48,512]{1,0:T(8,128)S(1)}, u32[]{:S(2)}, u32[]{:S(2)}) collective-permute-start(f32[48,512]{1,0:T(8,128)S(1)} %get-tuple-element.38), channel_id=1, source_target_pairs={{0,1},{1,2},{2,3},{3,4},{4,5},{5,6},{6,7},{7,8},{8,9},{9,10},{10,1... | collective-permute-start | bytes 294920 | tf_op jit(solution)/shard_map/ppermute | solution.py:329
  20.8 5.0 %shard_map.32 = (f32[8,144,512]{2,1,0:T(8,128)S(1)}, f32[144,512]{1,0:T(8,128)S(1)}, f32[144,512]{1,0:T(8,128)S(1)}, f32[8,48,512]{2,1,0:T(8,128)S(1)}, f32[48,512]{1,0:T(8,128)S(1)}, /*index=5*/f32[48,512]{1,0:T(8,128)S(1)}) custom-call(f32[16,192,512]{2,1,0:T(8,128)S(1)} %copy-done, f32[192,512]{1,0:T(8,128)S(1)} %get-tuple-element.24.inverse, ...), custom_call_target="tpu_custom_call" | custom-call | flops 8000000000 | bytes 10000000 | tf_op jit(solution)/shard_map/pallas_call | solution.py:331
  25.8 0.0 collective-permute-done.2.before_mid
  25.8 0.0 collective-permute-done.3.before_edge
  25.8 0.1 shard_map.33
  26.0 26.2 %all_to_all.10.pieces = f32[32,24,128]{2,1,0:T(8,128)S(1)} all-to-all(f32[32,24,128]{2,1,0:T(8,128)S(1)} %shard_map.33), channel_id=1, replica_groups=mesh['tile'=8,'depth'=32] {'depth'}, dimensions={0} | all-to-all | bytes 786432 | tf_op jit(solution)/shard_map/all_to_all | solution.py:338
  52.3 18.5 %all_to_all.11.pieces = f32[32,24,128]{2,1,0:T(8,128)S(1)} all-to-all(f32[32,24,128]{2,1,0:T(8,128)S(1)} %shard_map.34), channel_id=1, replica_groups=mesh['tile'=8,'depth'=32] {'depth'}, dimensions={0} | all-to-all | bytes 786432 | tf_op jit(solution)/shard_map/all_to_all | solution.py:340
  70.7 2.8 %shard_map.35 = f32[16,192,512]{2,1,0:T(8,128)} custom-call(f32[8,144,512]{2,1,0:T(8,128)S(1)} %get-tuple-element.33.shallow, f32[8,144,512]{2,1,0:T(8,128)S(1)} %get-tuple-element.34.deep, f32[8,48,512]{2,1,0:T(8,128)S(1)} %get-tuple-element.35.shallow_edge, f32[8,48,512]{2,1,0:T(8,128)S(1)} %get-tuple-element.36.deep_edge, ...), custom_call_target="tpu_custom_call" | custom-call | tf_op jit(solution)/shard_map/pallas_call | solution.py:299
  (1 shorter events, 0.0 us)
Async XLA Ops:
  0.0 8.2 %copy-start = (f32[16,192,512]{2,1,0:T(8,128)S(1)}, f32[16,192,512]{2,1,0:T(8,128)}, u32[]{:S(2)}) copy-start(f32[16,192,512]{2,1,0:T(8,128)} %volume.9) | copy-start | bytes 18874372
  0.0 8.2 %copy-start.1 = (f32[192,512]{1,0:T(8,128)S(1)}, f32[192,512]{1,0:T(8,128)}, u32[]{:S(2)}) copy-start(f32[192,512]{1,0:T(8,128)} %flat.5) | copy-start | bytes 1179652
  2.3 13.7 %collective-permute-start = (f32[16,24,512]{2,1,0:T(8,128)}, f32[16,24,512]{2,1,0:T(8,128)S(1)}, u32[]{:S(2)}, u32[]{:S(2)}) collective-permute-start(f32[16,24,512]{2,1,0:T(8,128)} %shard_map.29), channel_id=1, source_target_pairs={{32,64},{64,32},{96,128},{128,96},{160,192},{192,160},{33,65},{65,... | collective-permute-start | bytes 2359304 | tf_op jit(solution)/shard_map/ppermute | solution.py:322
  6.5 9.4 %collective-permute-start.1 = (f32[16,24,512]{2,1,0:T(8,128)}, f32[16,24,512]{2,1,0:T(8,128)S(1)}, u32[]{:S(2)}, u32[]{:S(2)}) collective-permute-start(f32[16,24,512]{2,1,0:T(8,128)} %shard_map.30), channel_id=1, source_target_pairs={{0,32},{32,0},{64,96},{96,64},{128,160},{160,128},{192,224},{224,1... | collective-permute-start | bytes 2359304 | tf_op jit(solution)/shard_map/ppermute | solution.py:323
  11.9 13.9 %collective-permute-start.2 = (f32[144,512]{1,0:T(8,128)S(1)}, f32[144,512]{1,0:T(8,128)S(1)}, u32[]{:S(2)}, u32[]{:S(2)}) collective-permute-start(f32[144,512]{1,0:T(8,128)S(1)} %get-tuple-element.37), channel_id=1, source_target_pairs={{0,1},{1,2},{2,3},{3,4},{4,5},{5,6},{6,7},{7,8},{8,9},{9,10},{10,1... | collective-permute-start | bytes 884744 | tf_op jit(solution)/shard_map/ppermute | solution.py:325
  17.4 8.5 %collective-permute-start.3 = (f32[48,512]{1,0:T(8,128)S(1)}, f32[48,512]{1,0:T(8,128)S(1)}, u32[]{:S(2)}, u32[]{:S(2)}) collective-permute-start(f32[48,512]{1,0:T(8,128)S(1)} %get-tuple-element.38), channel_id=1, source_target_pairs={{0,1},{1,2},{2,3},{3,4},{4,5},{5,6},{6,7},{7,8},{8,9},{9,10},{10,1... | collective-permute-start | bytes 294920 | tf_op jit(solution)/shard_map/ppermute | solution.py:329

commit v12 on v11

--- a/solution.py
+++ b/solution.py
@@ -13,7 +13,8 @@
 HIGH = math.exp(CLIP_LIMIT)
 MIB = 1 << 20
 STEP = 4
-EDGE_STEP = 8
+EDGE_STEP = 4
+DEEP = 4
 GRANT = 20
 FIRST = 56
 
@@ -228,14 +229,13 @@
 def final_kernel(shallow, deep, shallow_edge, deep_edge, pieces, out, factor, result, sems):
     planes, rows, cols = result.shape
     wide = cols // 4
-    half = planes // 2
+    rest = shallow.shape[0]
     for group in range(rows // RADIUS):
         for part in range(4):
             factor[group * RADIUS:(group + 1) * RADIUS, part * wide:(part + 1) * wide] = pieces[group * 4 + part]
     copies = []
     for plane in range(planes):
-        middle, edge = (shallow, shallow_edge) if plane < half else (deep, deep_edge)
-        at = plane % half
+        middle, edge, at = (shallow, shallow_edge, plane) if plane < rest else (deep, deep_edge, plane - rest)
         result[plane, :RADIUS] = edge[at, :RADIUS] * factor[:RADIUS]
         result[plane, RADIUS:rows - RADIUS] = middle[at] * factor[RADIUS:rows - RADIUS]
         result[plane, rows - RADIUS:] = edge[at, RADIUS:] * factor[rows - RADIUS:]
@@ -285,26 +285,26 @@
 
 def deep_call(volume, flat):
     planes, rows, cols = volume.shape
-    inner, near, half = rows - 2 * RADIUS, 2 * RADIUS, planes // 2
+    inner, near = rows - 2 * RADIUS, 2 * RADIUS
     weights = [(2 * inner, rows), (2 * near, 3 * near), (cols, cols), (cols, cols)]
     outputs = [shape(rows, cols)]
     outputs += [jax.ShapeDtypeStruct(dims, jnp.bfloat16) for dims in weights]
-    outputs += [shape(half, inner, cols)] + [shape(inner, cols)] * 3
+    outputs += [shape(DEEP, inner, cols)] + [shape(inner, cols)] * 3
     return vmem_call(deep_kernel, 2, outputs, cost(6e9, 7e6))(volume, flat)
 
 
 def final_call(shallow, deep, shallow_edge, deep_edge, pieces):
-    half, inner, cols = deep.shape
-    rows = inner + 2 * RADIUS
+    _, inner, cols = deep.shape
+    planes, rows = shallow.shape[0] + deep.shape[0], inner + 2 * RADIUS
     return pl.pallas_call(
         final_kernel,
         in_specs=[pl.BlockSpec(memory_space=pltpu.VMEM)] * 5,
         out_specs=pl.BlockSpec(memory_space=pl.ANY),
-        out_shape=shape(2 * half, rows, cols),
+        out_shape=shape(planes, rows, cols),
         scratch_shapes=[
             pltpu.VMEM((rows, cols), jnp.float32),
-            pltpu.VMEM((2 * half, rows, cols), jnp.float32),
-            pltpu.SemaphoreType.DMA((2 * half,)),
+            pltpu.VMEM((planes, rows, cols), jnp.float32),
+            pltpu.SemaphoreType.DMA((planes,)),
         ],
         compiler_params=params(GRANT),
     )(shallow, deep, shallow_edge, deep_edge, pieces)
@@ -318,16 +318,16 @@
     planes, rows, cols = volume.shape
     tiles, slabs = lax.axis_size("tile"), lax.axis_size("depth")
     onward = [(i, i + 1) for i in range(slabs - 1)]
-    inner, near, half = rows - 2 * RADIUS, 2 * RADIUS, planes // 2
+    inner, near, rest = rows - 2 * RADIUS, 2 * RADIUS, planes - DEEP
     outer = lax.ppermute(halo_call(volume, flat_field, 1), "tile", swapped(1, tiles))
     inner_halo = lax.ppermute(halo_call(volume, flat_field, 0), "tile", swapped(0, tiles))
     inverse, mid_weight, edge_weight, col_high, col_low, deep, deepest, later, factor = deep_call(volume, flat_field)
     before_mid = lax.ppermute(deepest, "depth", onward)
     deep_edge, deepest_edge, later_edge, factor_edge = vmem_call(
-        edge_kernel, 7, [shape(half, near, cols)] + [shape(near, cols)] * 3, cost(2e9, 4e6)
+        edge_kernel, 7, [shape(DEEP, near, cols)] + [shape(near, cols)] * 3, cost(2e9, 4e6)
     )(volume, inverse, outer, inner_halo, edge_weight, col_high, col_low)
     before_edge = lax.ppermute(deepest_edge, "depth", onward)
-    outputs = [shape(half, inner, cols)] + [shape(inner, cols)] * 2 + [shape(half, near, cols)] + [shape(near, cols)] * 2
+    outputs = [shape(rest, inner, cols)] + [shape(inner, cols)] * 2 + [shape(rest, near, cols)] + [shape(near, cols)] * 2
     shallow, first_mid, factor_mid, shallow_edge, first_edge, factor_edge = vmem_call(shallow_kernel, 12, outputs, cost(8e9, 1e7))(
         volume, inverse, outer, inner_halo, mid_weight, edge_weight, col_high, col_low, later, factor, later_edge, factor_edge
     )

time: 73.8 us -> 76.3 us (1.034)
  waiting for transfers between devices: 0.6 us -> 2.26 us
    pallas_call x1, Pallas kernels: 5.03 us -> 7.85 us  [body(): vmem_call(shallow_kernel, 12, outputs, cost(8000000000.0, 10000000.0))]
    pallas_call x1, Pallas kernels: 3.66 us -> 1.98 us  [deep_call(): vmem_call(deep_kernel, 2, outputs, cost(6000000000.0, 7000000.0))]
    ppermute x1, waiting for transfers between devices: 0.59 us -> 2.25 us  [body(): lax.ppermute(halo_call(volume, flat_field, 1), 'tile', swapped(1, tiles))]
where the time goes in v12:
time: 76.3 us; the launch traced here: 76.1 us
  blocking collectives  45 us (59%)
  Pallas kernels  17.9 us (23%)
  starting transfers between devices  10.8 us (14%)
  waiting for transfers between devices  2.26 us (3%)
    all_to_all x1, blocking collectives, body(): mine = lax.all_to_all(pieces, 'depth', 0, 0, tiled=True)  26.4 us
    all_to_all x1, blocking collectives, body(): back = lax.all_to_all(reached, 'depth', 0, 0, tiled=True)  18.6 us
    pallas_call x1, Pallas kernels, body(): vmem_call(shallow_kernel, 12, outputs, cost(8000000000.0, 10000000.0))  7.85 us
    pallas_call x2, Pallas kernels, halo_call(): pl.pallas_call(functools.partial(halo_kernel, lower), in_specs=[pl.BlockS...  4.25 us
    ppermute x1, starting transfers between devices, body(): before_edge = lax.ppermute(deepest_edge, 'depth', onward)  3.42 us
    ppermute x1, starting transfers between devices, body(): before_mid = lax.ppermute(deepest, 'depth', onward)  3.42 us
    pallas_call x1, Pallas kernels, final_call(): pl.pallas_call(final_kernel, in_specs=[pl.BlockSpec(memory_space=pltpu.VM...  2.82 us
    ppermute x1, starting transfers between devices, body(): lax.ppermute(halo_call(volume, flat_field, 1), 'tile', swapped(1, tiles))  2.31 us
  transfers between devices with their start and end apart: 4, of which 1 were waited for; matrix products, arithmetic and copies ran while one was open for 0% of the time, Pallas kernels for 17%

profile of v12, /device:TPU:8, one launch (start us, length us, event | category | flops | bytes accessed | tf_op | source)
XLA Modules:
  0.0 76.1 jit_solution(1855257512214719443)
XLA Ops:
  0.0 2.1 %shard_map.29 = f32[16,24,512]{2,1,0:T(8,128)} custom-call(f32[16,192,512]{2,1,0:T(8,128)} %volume.9, f32[192,512]{1,0:T(8,128)} %flat.5), custom_call_target="tpu_custom_call" | custom-call | flops 1000000 | bytes 2000000 | tf_op jit(solution)/shard_map/pallas_call | solution.py:275
  2.1 0.0 copy-start
  2.1 0.0 copy-start.1
  2.1 2.3 %collective-permute-start = (f32[16,24,512]{2,1,0:T(8,128)}, f32[16,24,512]{2,1,0:T(8,128)S(1)}, u32[]{:S(2)}, u32[]{:S(2)}) collective-permute-start(f32[16,24,512]{2,1,0:T(8,128)} %shard_map.29), channel_id=1, source_target_pairs={{32,64},{64,32},{96,128},{128,96},{160,192},{192,160},{33,65},{65,... | collective-permute-start | bytes 2359304 | tf_op jit(solution)/shard_map/ppermute | solution.py:322
  4.5 2.1 %shard_map.30 = f32[16,24,512]{2,1,0:T(8,128)} custom-call(f32[16,192,512]{2,1,0:T(8,128)} %volume.9, f32[192,512]{1,0:T(8,128)} %flat.5), custom_call_target="tpu_custom_call" | custom-call | flops 1000000 | bytes 2000000 | tf_op jit(solution)/shard_map/pallas_call | solution.py:275
  6.6 1.6 %collective-permute-start.1 = (f32[16,24,512]{2,1,0:T(8,128)}, f32[16,24,512]{2,1,0:T(8,128)S(1)}, u32[]{:S(2)}, u32[]{:S(2)}) collective-permute-start(f32[16,24,512]{2,1,0:T(8,128)} %shard_map.30), channel_id=1, source_target_pairs={{0,32},{32,0},{64,96},{96,64},{128,160},{160,128},{192,224},{224,1... | collective-permute-start | bytes 2359304 | tf_op jit(solution)/shard_map/ppermute | solution.py:323
  8.3 0.0 copy-done
  8.3 0.0 copy-done.1
  8.3 2.0 %shard_map.28 = (f32[192,512]{1,0:T(8,128)S(1)}, bf16[288,192]{1,0:T(8,128)(2,1)S(1)}, bf16[96,144]{1,0:T(8,128)(2,1)S(1)}, bf16[512,512]{1,0:T(8,128)(2,1)S(1)}...) custom-call(f32[16,192,512]{2,1,0:T(8,128)S(1)} %copy-done, ...), custom_call_target="tpu_custom_call" | custom-call | flops 6000000000 | bytes 7000000 | tf_op jit(solution)/shard_map/pallas_call | solution.py:293
  10.2 3.4 %collective-permute-start.2 = (f32[144,512]{1,0:T(8,128)S(1)}, f32[144,512]{1,0:T(8,128)S(1)}, u32[]{:S(2)}, u32[]{:S(2)}) collective-permute-start(f32[144,512]{1,0:T(8,128)S(1)} %get-tuple-element.37), channel_id=1, source_target_pairs={{0,1},{1,2},{2,3},{3,4},{4,5},{5,6},{6,7},{7,8},{8,9},{9,10},{10,1... | collective-permute-start | bytes 884744 | tf_op jit(solution)/shard_map/ppermute | solution.py:325
  13.7 2.3 %collective-permute-done.outer = f32[16,24,512]{2,1,0:T(8,128)S(1)} collective-permute-done((f32[16,24,512]{2,1,0:T(8,128)}, f32[16,24,512]{2,1,0:T(8,128)S(1)}, u32[]{:S(2)}, u32[]{:S(2)}) %collective-permute-start) | collective-permute-done | bytes 786464 | tf_op jit(solution)/shard_map/ppermute | solution.py:322
  15.9 0.0 collective-permute-done.1.inner
  15.9 0.8 %shard_map.31 = (f32[4,48,512]{2,1,0:T(8,128)S(1)}, f32[48,512]{1,0:T(8,128)S(1)}, f32[48,512]{1,0:T(8,128)S(1)}, f32[48,512]{1,0:T(8,128)S(1)}) custom-call(f32[16,192,512]{2,1,0:T(8,128)S(1)} %copy-done, f32[192,512]{1,0:T(8,128)S(1)} %get-tuple-element.24.inverse, f32[16,24,512]{2,1,0:T(8,128)S(1)} %collective-permute-done.outer, ...), custom_call_target="tpu_custom_call" | custom-call | flops 2000000000 | bytes 4000000 | tf_op jit(solution)/shard_map/pallas_call | solution.py:326
  16.8 3.4 %collective-permute-start.3 = (f32[48,512]{1,0:T(8,128)S(1)}, f32[48,512]{1,0:T(8,128)S(1)}, u32[]{:S(2)}, u32[]{:S(2)}) collective-permute-start(f32[48,512]{1,0:T(8,128)S(1)} %get-tuple-element.38), channel_id=1, source_target_pairs={{0,1},{1,2},{2,3},{3,4},{4,5},{5,6},{6,7},{7,8},{8,9},{9,10},{10,1... | collective-permute-start | bytes 294920 | tf_op jit(solution)/shard_map/ppermute | solution.py:329
  20.2 7.8 %shard_map.32 = (f32[12,144,512]{2,1,0:T(8,128)S(1)}, f32[144,512]{1,0:T(8,128)S(1)}, f32[144,512]{1,0:T(8,128)S(1)}, f32[12,48,512]{2,1,0:T(8,128)S(1)}, f32[48,512]{1,0:T(8,128)S(1)}, /*index=5*/f32[48,512]{1,0:T(8,128)S(1)}) custom-call(f32[16,192,512]{2,1,0:T(8,128)S(1)} %copy-done, f32[192,512]{1,0:T(8,128)S(1)} %get-tuple-element.24.inverse, ...), custom_call_target="tpu_custom_call" | custom-call | flops 8000000000 | bytes 10000000 | tf_op jit(solution)/shard_map/pallas_call | solution.py:331
  28.0 0.0 collective-permute-done.2.before_mid
  28.0 0.0 collective-permute-done.3.before_edge
  28.1 0.1 shard_map.33
  28.2 26.4 %all_to_all.10.pieces = f32[32,24,128]{2,1,0:T(8,128)S(1)} all-to-all(f32[32,24,128]{2,1,0:T(8,128)S(1)} %shard_map.33), channel_id=1, replica_groups=mesh['tile'=8,'depth'=32] {'depth'}, dimensions={0} | all-to-all | bytes 786432 | tf_op jit(solution)/shard_map/all_to_all | solution.py:338
  54.6 18.6 %all_to_all.11.pieces = f32[32,24,128]{2,1,0:T(8,128)S(1)} all-to-all(f32[32,24,128]{2,1,0:T(8,128)S(1)} %shard_map.34), channel_id=1, replica_groups=mesh['tile'=8,'depth'=32] {'depth'}, dimensions={0} | all-to-all | bytes 786432 | tf_op jit(solution)/shard_map/all_to_all | solution.py:340
  73.2 2.8 %shard_map.35 = f32[16,192,512]{2,1,0:T(8,128)} custom-call(f32[12,144,512]{2,1,0:T(8,128)S(1)} %get-tuple-element.33.shallow, f32[4,144,512]{2,1,0:T(8,128)S(1)} %get-tuple-element.34.deep, f32[12,48,512]{2,1,0:T(8,128)S(1)} %get-tuple-element.35.shallow_edge, f32[4,48,512]{2,1,0:T(8,128)S(1)} %get-tuple-element.36.deep_edge, ...), custom_call_target="tpu_custom_call" | custom-call | tf_op jit(solution)/shard_map/pallas_call | solution.py:299
  (1 shorter events, 0.0 us)
Async XLA Ops:
  2.1 6.1 %copy-start = (f32[16,192,512]{2,1,0:T(8,128)S(1)}, f32[16,192,512]{2,1,0:T(8,128)}, u32[]{:S(2)}) copy-start(f32[16,192,512]{2,1,0:T(8,128)} %volume.9) | copy-start | bytes 18874372
  2.1 6.1 %copy-start.1 = (f32[192,512]{1,0:T(8,128)S(1)}, f32[192,512]{1,0:T(8,128)}, u32[]{:S(2)}) copy-start(f32[192,512]{1,0:T(8,128)} %flat.5) | copy-start | bytes 1179652
  2.1 13.8 %collective-permute-start = (f32[16,24,512]{2,1,0:T(8,128)}, f32[16,24,512]{2,1,0:T(8,128)S(1)}, u32[]{:S(2)}, u32[]{:S(2)}) collective-permute-start(f32[16,24,512]{2,1,0:T(8,128)} %shard_map.29), channel_id=1, source_target_pairs={{32,64},{64,32},{96,128},{128,96},{160,192},{192,160},{33,65},{65,... | collective-permute-start | bytes 2359304 | tf_op jit(solution)/shard_map/ppermute | solution.py:322
  6.6 9.3 %collective-permute-start.1 = (f32[16,24,512]{2,1,0:T(8,128)}, f32[16,24,512]{2,1,0:T(8,128)S(1)}, u32[]{:S(2)}, u32[]{:S(2)}) collective-permute-start(f32[16,24,512]{2,1,0:T(8,128)} %shard_map.30), channel_id=1, source_target_pairs={{0,32},{32,0},{64,96},{96,64},{128,160},{160,128},{192,224},{224,1... | collective-permute-start | bytes 2359304 | tf_op jit(solution)/shard_map/ppermute | solution.py:323
  10.2 17.8 %collective-permute-start.2 = (f32[144,512]{1,0:T(8,128)S(1)}, f32[144,512]{1,0:T(8,128)S(1)}, u32[]{:S(2)}, u32[]{:S(2)}) collective-permute-start(f32[144,512]{1,0:T(8,128)S(1)} %get-tuple-element.37), channel_id=1, source_target_pairs={{0,1},{1,2},{2,3},{3,4},{4,5},{5,6},{6,7},{7,8},{8,9},{9,10},{10,1... | collective-permute-start | bytes 884744 | tf_op jit(solution)/shard_map/ppermute | solution.py:325
  16.8 11.3 %collective-permute-start.3 = (f32[48,512]{1,0:T(8,128)S(1)}, f32[48,512]{1,0:T(8,128)S(1)}, u32[]{:S(2)}, u32[]{:S(2)}) collective-permute-start(f32[48,512]{1,0:T(8,128)S(1)} %get-tuple-element.38), channel_id=1, source_target_pairs={{0,1},{1,2},{2,3},{3,4},{4,5},{5,6},{6,7},{7,8},{8,9},{9,10},{10,1... | collective-permute-start | bytes 294920 | tf_op jit(solution)/shard_map/ppermute | solution.py:329
